TPU v7x, 32 devices: a whole 2x2x4 slice. The times are simulated.
32 devices in a mesh: seq: 4 (over z), dp: 8 (over y, x, core).
Axes of the slice: x: 2, y: 2, z: 4, core: 2. Of those that a mesh axis runs over, the one named last changes fastest.
Arguments:
- tokens: bfloat16 [16384, 512], P(('seq', 'dp')), may hold values from -6 to 6
- cotangent: bfloat16 [16384, 512], P(('seq', 'dp')), may hold values from -6 to 6
- deal: int32 [32, 8], P(('seq', 'dp')), may hold values from 0 to 7, each once within a row
- lengths: int32 [8, 3], P('dp'), may hold values from 1 to 1024, 2048 in all within a row
- buckets: int32 [1024], replicated, may hold values from 0 to 31, as said below
- ln1_gain: bfloat16 [512], P('dp'), may hold values from 0.5 to 1.5
- ln1_bias: bfloat16 [512], P('dp'), may hold values from -2 to 2
- w_qkv: bfloat16 [512, 1536], P('dp'), may hold values from -0.25 to 0.25
- w_out: bfloat16 [512, 512], P('dp'), may hold values from -0.75 to 0.75
- rel_bias: bfloat16 [32, 8], P('dp'), may hold values from -4 to 4
- ln2_gain: bfloat16 [512], P('dp'), may hold values from 0.5 to 1.5
- ln2_bias: bfloat16 [512], P('dp'), may hold values from -2 to 2
- w_up: bfloat16 [512, 2048], P('dp'), may hold values from -0.25 to 0.25
- w_down: bfloat16 [2048, 512], P('dp'), may hold values from -0.125 to 0.125
Outputs:
- output: bfloat16 [16384, 512], P(('seq', 'dp'))
- grad_tokens: bfloat16 [16384, 512], P(('seq', 'dp'))
- grad_ln1_gain: float32 [512], P('dp')
- grad_ln1_bias: float32 [512], P('dp')
- grad_w_qkv: float32 [512, 1536], P('dp')
- grad_w_out: float32 [512, 512], P('dp')
- grad_rel_bias: float32 [32, 8], P('dp')
- grad_ln2_gain: float32 [512], P('dp')
- grad_ln2_bias: float32 [512], P('dp')
- grad_w_up: float32 [512, 2048], P('dp')
- grad_w_down: float32 [2048, 512], P('dp')
Inputs may be any that keep to these rules, and one draw needn't show every extreme that they name: `deal`: each row lists every group once. Each group's 3 lengths sum to 2048, and the longest of each group is exactly 1024. Never falling with the distance; buckets[0] = 0 and buckets[1023] = 31.
All inputs are finite; a program needn't handle non-finite values.
Results may differ from a plain program's by a relative error of at most 0.02.
Values may be sent and summed in bfloat16 or wider, within the bound.
A program may use at most 192 MiB of HBM per device.

v0:
```python
import jax
import jax.numpy as jnp
from jax import lax
from jax.sharding import PartitionSpec as P

H = 8
HD = 64
NBK = 32


def norm_rows(values, gain_vec, bias_vec):
    average = jnp.mean(values, axis=-1, keepdims=True)
    centred = values - average
    variance = jnp.mean(centred * centred, axis=-1, keepdims=True)
    return centred * lax.rsqrt(variance + 1e-05) * gain_vec + bias_vec


def gelu_exact(values):
    return jax.nn.gelu(values, approximate=False)


def segment_of(lengths_row, total_rows):
    ends_at = jnp.cumsum(lengths_row)
    places = jnp.arange(total_rows, dtype=jnp.int32)
    return jnp.sum((places[:, None] >= ends_at[None, :]).astype(jnp.int32), axis=1)


def inverse_of(deal_rows):
    slot_count = deal_rows.shape[-1]
    places = jnp.arange(slot_count, dtype=jnp.int32)
    matches = (deal_rows[..., :, None] == places).astype(jnp.int32)
    return jnp.sum(matches * places[:, None], axis=-2)


def shards(
    tokens,
    cotangent,
    deal,
    lengths,
    buckets,
    ln1_gain,
    ln1_bias,
    w_qkv,
    w_out,
    rel_bias,
    ln2_gain,
    ln2_bias,
    w_up,
    w_down,
):
    groups = lax.axis_size("dp")
    splits = lax.axis_size("seq")
    tok_dev, model_width = tokens.shape
    block_len = tok_dev // groups
    group_tok = tok_dev * splits
    local_heads = H // splits
    local_width = local_heads * HD
    head_first = lax.axis_index("seq") * local_heads
    col_first = head_first * HD
    rows_blk = min(512, group_tok)
    block_count = group_tok // rows_blk
    score_scale = HD ** (-0.5)
    deal_row = deal[0]
    inverse = inverse_of(deal_row)

    def to_slots(values):
        return jnp.take(values.reshape(groups, block_len, model_width), inverse, axis=0)

    dealt_in, dealt_grad = (
        lax.all_to_all(to_slots(tokens), "dp", split_axis=0, concat_axis=0, tiled=True),
        lax.all_to_all(to_slots(cotangent), "dp", split_axis=0, concat_axis=0, tiled=True),
    )
    x_rows = dealt_in.reshape(tok_dev, model_width).astype(jnp.float32)
    grad_out = dealt_grad.reshape(tok_dev, model_width)
    gain_one, bias_one, wqkv_full, wout_full, rel_full, gain_two, bias_two, wup_full, wdown_full = (
        lax.all_gather(ln1_gain, "dp", axis=0, tiled=True),
        lax.all_gather(ln1_bias, "dp", axis=0, tiled=True),
        lax.all_gather(w_qkv, "dp", axis=0, tiled=True),
        lax.all_gather(w_out, "dp", axis=0, tiled=True),
        lax.all_gather(rel_bias, "dp", axis=0, tiled=True),
        lax.all_gather(ln2_gain, "dp", axis=0, tiled=True),
        lax.all_gather(ln2_bias, "dp", axis=0, tiled=True),
        lax.all_gather(w_up, "dp", axis=0, tiled=True),
        lax.all_gather(w_down, "dp", axis=0, tiled=True),
    )
    normed, norm_one_back = jax.vjp(
        norm_rows, x_rows, gain_one.astype(jnp.float32), bias_one.astype(jnp.float32)
    )
    normed_low = normed.astype(jnp.bfloat16)
    own_cols = lax.dynamic_slice_in_dim(
        wqkv_full.reshape(model_width, 3, model_width), col_first, local_width, 2
    )
    all_rows = lax.all_gather(normed_low, "seq", axis=0, tiled=True)
    head_qkv = jnp.einsum(
        "td,dch->tch", all_rows, own_cols, preferred_element_type=jnp.float32
    ).astype(jnp.bfloat16)
    queries = head_qkv[:, 0].reshape(group_tok, local_heads, HD)
    keys_all = head_qkv[:, 1].reshape(group_tok, local_heads, HD)
    values_all = head_qkv[:, 2].reshape(group_tok, local_heads, HD)
    rel_local = lax.dynamic_slice_in_dim(rel_full.astype(jnp.float32), head_first, local_heads, 1)
    step_diff = rel_local[1:] - rel_local[:-1]
    bucket_ids = jnp.arange(1, NBK, dtype=jnp.int32)
    thresholds = jnp.sum((buckets[None, :] < bucket_ids[:, None]).astype(jnp.int32), axis=1)
    seg_ids = segment_of(lengths[0], group_tok)
    places = jnp.arange(group_tok, dtype=jnp.int32)
    starts = jnp.arange(block_count, dtype=jnp.int32) * rows_blk

    def scores_of(first_row):
        q_block = lax.dynamic_slice_in_dim(queries, first_row, rows_blk, 0)
        row_ids = first_row + jnp.arange(rows_blk, dtype=jnp.int32)
        distance = row_ids[:, None] - places[None, :]
        row_seg = lax.dynamic_slice_in_dim(seg_ids, first_row, rows_blk, 0)
        allowed = (row_seg[:, None] == seg_ids[None, :]) & (distance >= 0)
        raw_dot = (
            jnp.einsum("qhd,khd->hqk", q_block, keys_all, preferred_element_type=jnp.float32)
            * score_scale
        )
        shifted = raw_dot + rel_local[0][:, None, None]
        for level in range(NBK - 1):
            shifted = shifted + jnp.where(
                (distance >= thresholds[level])[None], step_diff[level][:, None, None], 0.0
            )
        return (q_block, shifted, allowed, distance)

    def forward_block(first_row):
        parts = scores_of(first_row)
        masked = jnp.where(parts[2][None], parts[1], -1e30)
        top_score = jnp.max(masked, axis=-1, keepdims=True)
        exponent = jnp.exp(masked - top_score)
        total_mass = jnp.sum(exponent, axis=-1, keepdims=True)
        attn_prob = (exponent / total_mass).astype(jnp.bfloat16)
        block_out = jnp.einsum(
            "hqk,khd->qhd", attn_prob, values_all, preferred_element_type=jnp.float32
        ).astype(jnp.bfloat16)
        return (block_out, (top_score + jnp.log(total_mass))[..., 0])

    head_out, lse_blocks = lax.map(forward_block, starts)
    head_out = head_out.reshape(group_tok, local_width)
    log_mass = jnp.transpose(lse_blocks, (1, 0, 2)).reshape(local_heads, group_tok)
    attended = lax.all_to_all(head_out, "seq", split_axis=0, concat_axis=1, tiled=True)
    branch = jnp.dot(attended, wout_full, preferred_element_type=jnp.float32)
    residual = x_rows + branch
    normed_two, norm_two_back = jax.vjp(
        norm_rows, residual, gain_two.astype(jnp.float32), bias_two.astype(jnp.float32)
    )
    normed_two_low = normed_two.astype(jnp.bfloat16)
    pre_act = jnp.dot(normed_two_low, wup_full, preferred_element_type=jnp.float32)
    active, gelu_back = jax.vjp(gelu_exact, pre_act)
    active_low = active.astype(jnp.bfloat16)
    output_rows = (
        residual + jnp.dot(active_low, wdown_full, preferred_element_type=jnp.float32)
    ).astype(jnp.bfloat16)
    grad_wdown = jnp.einsum("tf,td->fd", active_low, grad_out, preferred_element_type=jnp.float32)
    grad_active = jnp.einsum("td,fd->tf", grad_out, wdown_full, preferred_element_type=jnp.float32)
    grad_pre = gelu_back(grad_active)[0].astype(jnp.bfloat16)
    grad_wup = jnp.einsum("td,tf->df", normed_two_low, grad_pre, preferred_element_type=jnp.float32)
    grad_norm_two = jnp.einsum("tf,df->td", grad_pre, wup_full, preferred_element_type=jnp.float32)
    resid_part, grad_gain_two, grad_bias_two = norm_two_back(grad_norm_two)
    grad_resid = grad_out.astype(jnp.float32) + resid_part
    branch_grad = grad_resid.astype(jnp.bfloat16)
    grad_wout = jnp.einsum("td,te->de", attended, branch_grad, preferred_element_type=jnp.float32)
    grad_att = jnp.einsum(
        "te,de->td", branch_grad, wout_full, preferred_element_type=jnp.float32
    ).astype(jnp.bfloat16)
    head_grad = lax.all_to_all(grad_att, "seq", split_axis=1, concat_axis=0, tiled=True).reshape(
        group_tok, local_heads, HD
    )

    def backward_block(running, first_row):
        key_acc, value_acc, level_acc = running
        q_block, shifted, allowed, distance = scores_of(first_row)
        lse_rows = lax.dynamic_slice_in_dim(log_mass, first_row, rows_blk, 1)
        attn_prob = jnp.where(allowed[None], jnp.exp(shifted - lse_rows[..., None]), 0.0)
        prob_low = attn_prob.astype(jnp.bfloat16)
        out_grad = lax.dynamic_slice_in_dim(head_grad, first_row, rows_blk, 0)
        value_acc = value_acc + jnp.einsum(
            "hqk,qhd->khd", prob_low, out_grad, preferred_element_type=jnp.float32
        )
        prob_grad = jnp.einsum(
            "qhd,khd->hqk", out_grad, values_all, preferred_element_type=jnp.float32
        )
        row_inner = jnp.sum(attn_prob * prob_grad, axis=-1, keepdims=True)
        score_grad = (attn_prob * (prob_grad - row_inner)).astype(jnp.bfloat16)
        query_grad = (
            jnp.einsum("hqk,khd->qhd", score_grad, keys_all, preferred_element_type=jnp.float32)
            * score_scale
        )
        key_acc = (
            key_acc
            + jnp.einsum("hqk,qhd->khd", score_grad, q_block, preferred_element_type=jnp.float32)
            * score_scale
        )
        grad_wide = score_grad.astype(jnp.float32)
        level_sums = [jnp.sum(grad_wide, axis=(1, 2))]
        for level in range(NBK - 1):
            level_sums.append(
                jnp.sum(
                    jnp.where((distance >= thresholds[level])[None], grad_wide, 0.0), axis=(1, 2)
                )
            )
        level_acc = level_acc + jnp.stack(level_sums, axis=0)
        return ((key_acc, value_acc, level_acc), query_grad)

    zero_heads = jnp.zeros((group_tok, local_heads, HD), jnp.float32)
    zero_levels = jnp.zeros((NBK, local_heads), jnp.float32)
    (key_acc, value_acc, level_acc), query_blocks = lax.scan(
        backward_block, (zero_heads, zero_heads, zero_levels), starts
    )
    grad_heads = jnp.stack(
        [
            query_blocks.reshape(group_tok, local_width),
            key_acc.reshape(group_tok, local_width),
            value_acc.reshape(group_tok, local_width),
        ],
        axis=1,
    ).astype(jnp.bfloat16)
    own_rel = level_acc - jnp.concatenate(
        [level_acc[1:], jnp.zeros((1, local_heads), jnp.float32)], axis=0
    )
    qkv_term = jnp.einsum("td,tch->dch", all_rows, grad_heads, preferred_element_type=jnp.float32)
    partial_rows = jnp.einsum(
        "tch,dch->td", grad_heads, own_cols, preferred_element_type=jnp.float32
    )
    grad_normed = lax.psum_scatter(
        partial_rows.astype(jnp.bfloat16), "seq", scatter_dimension=0, tiled=True
    ).astype(jnp.float32)
    x_part, grad_gain_one, grad_bias_one = norm_one_back(grad_normed)
    grad_x = (grad_resid + x_part).astype(jnp.bfloat16)
    (
        shard_g1,
        shard_b1,
        shard_qkv,
        shard_out,
        shard_rel,
        shard_g2,
        shard_b2,
        shard_up,
        shard_down,
    ) = (
        lax.psum_scatter(
            grad_gain_one.astype(jnp.bfloat16), "dp", scatter_dimension=0, tiled=True
        ).astype(jnp.float32),
        lax.psum_scatter(
            grad_bias_one.astype(jnp.bfloat16), "dp", scatter_dimension=0, tiled=True
        ).astype(jnp.float32),
        lax.psum_scatter(
            qkv_term.astype(jnp.bfloat16), "dp", scatter_dimension=0, tiled=True
        ).astype(jnp.float32),
        lax.psum_scatter(
            grad_wout.astype(jnp.bfloat16), "dp", scatter_dimension=0, tiled=True
        ).astype(jnp.float32),
        lax.psum_scatter(
            own_rel.astype(jnp.bfloat16), "dp", scatter_dimension=0, tiled=True
        ).astype(jnp.float32),
        lax.psum_scatter(
            grad_gain_two.astype(jnp.bfloat16), "dp", scatter_dimension=0, tiled=True
        ).astype(jnp.float32),
        lax.psum_scatter(
            grad_bias_two.astype(jnp.bfloat16), "dp", scatter_dimension=0, tiled=True
        ).astype(jnp.float32),
        lax.psum_scatter(
            grad_wup.astype(jnp.bfloat16), "dp", scatter_dimension=0, tiled=True
        ).astype(jnp.float32),
        lax.psum_scatter(
            grad_wdown.astype(jnp.bfloat16), "dp", scatter_dimension=0, tiled=True
        ).astype(jnp.float32),
    )
    total_g1, total_b1, total_out, total_g2, total_b2, total_up, total_down = (
        lax.psum(shard_g1.astype(jnp.bfloat16), "seq").astype(jnp.float32),
        lax.psum(shard_b1.astype(jnp.bfloat16), "seq").astype(jnp.float32),
        lax.psum(shard_out.astype(jnp.bfloat16), "seq").astype(jnp.float32),
        lax.psum(shard_g2.astype(jnp.bfloat16), "seq").astype(jnp.float32),
        lax.psum(shard_b2.astype(jnp.bfloat16), "seq").astype(jnp.float32),
        lax.psum(shard_up.astype(jnp.bfloat16), "seq").astype(jnp.float32),
        lax.psum(shard_down.astype(jnp.bfloat16), "seq").astype(jnp.float32),
    )
    joined_qkv, total_rel = (
        lax.all_gather(shard_qkv, "seq", axis=2, tiled=True),
        lax.all_gather(shard_rel, "seq", axis=1, tiled=True),
    )
    total_qkv = joined_qkv.reshape(joined_qkv.shape[0], 3 * model_width)
    back_out, back_grad = (
        lax.all_to_all(
            output_rows.reshape(groups, block_len, model_width),
            "dp",
            split_axis=0,
            concat_axis=0,
            tiled=True,
        ),
        lax.all_to_all(
            grad_x.reshape(groups, block_len, model_width),
            "dp",
            split_axis=0,
            concat_axis=0,
            tiled=True,
        ),
    )
    output = jnp.take(back_out, deal_row, axis=0).reshape(tok_dev, model_width)
    grad_tokens = jnp.take(back_grad, deal_row, axis=0).reshape(tok_dev, model_width)
    return (
        output,
        grad_tokens,
        total_g1,
        total_b1,
        total_qkv,
        total_out,
        total_rel,
        total_g2,
        total_b2,
        total_up,
        total_down,
    )


def solution(mesh):
    placed = (
        P(("seq", "dp"), None),
        P(("seq", "dp"), None),
        P(("seq", "dp"), None),
        P("dp", None),
        P(),
        P("dp"),
        P("dp"),
        P("dp", None),
        P("dp", None),
        P("dp", None),
        P("dp"),
        P("dp"),
        P("dp", None),
        P("dp", None),
    )
    return jax.shard_map(
        shards,
        mesh=mesh,
        in_specs=placed,
        out_specs=(
            P(("seq", "dp"), None),
            P(("seq", "dp"), None),
            P("dp"),
            P("dp"),
            P("dp", None),
            P("dp", None),
            P("dp", None),
            P("dp"),
            P("dp"),
            P("dp", None),
            P("dp", None),
        ),
        check_vma=False,
    )
```

profile of v0, /device:TPU:0, one launch (start us, length us, event | category | flops | bytes accessed | tf_op | source)
XLA Modules:
  0.0 1490.9 jit_solution(9441929853740647218)
XLA Ops:
  19.6 16.6 %all-reduce.11 = (bf16[512]{0:T(512)(128)(2,1)S(1)}, bf16[512]{0:T(512)(128)(2,1)S(1)}, bf16[512]{0:T(512)(128)(2,1)}, bf16[512]{0:T(512)(128)(2,1)}) all-reduce(bf16[512]{0:T(512)(128)(2,1)S(1)} %dynamic-update-slice.1, bf16[512]{0:T(512)(128)(2,1)S(1)} %dynamic-update-slice, ...), channel_id=1, replica_groups=mesh['seq'=4,'dp'=8] {'dp'}, use_global_device_ids=true, to_apply=%add.2 | all-reduce | flops 2048 | bytes 8192
  40.2 9.2 all-gather
  51.5 38.4 %all-gather.7.cloned.1.call-done = bf16[2048,512]{1,0:T(8,128)(2,1)} async-done(((bf16[512,512]{1,0:T(8,128)(2,1)}), bf16[2048,512]{1,0:T(8,128)(2,1)}) %all-gather.7.cloned.1.call-update) | async-done | bytes 2097168 | tf_op jit(solution)/shard_map/all_gather | solution.py:93
  94.0 436.4 %while.30 = (s32[]{:T(128)}, bf16[4,512,2,64]{1,3,2,0:T(8,128)(2,1)}, f32[4,2,512]{2,1,0:T(2,128)S(1)}, s32[4]{0:T(128)S(1)}, s32[2048]{0:T(1024)S(1)}, /*index=...) while((s32[]{:T(128)}, ...), condition=%wide.region_9.11_spmd.clone, body=%wide.region_6.10_spmd.clone.sunk | while | flops 723582464 | bytes 127194456 | solution.py:137
  99.0 23.1 %fusion.221 = (pred[512,2048]{1,0:T(8,128)(4,1)S(1)}, pred[512,2048]{1,0:T(8,128)(4,1)S(1)}, pred[512,2048]{1,0:T(8,128)(4,1)}, pred[512,2048]{1,0:T(8,128)(4,1)...) fusion(s32[]{:T(128)} %bitcast.476, ...), kind=kLoop, calls=%fused_computation.41.clone.1 | loop fusion | flops 16777216 | bytes 15730748 | tf_op jit(solution)/shard_map/while/body/eval_jaxpr/ge | solution.py:121
  122.1 25.4 %fusion.219 = (pred[512,2048]{1,0:T(8,128)(4,1)}, pred[512,2048]{1,0:T(8,128)(4,1)}, pred[512,2048]{1,0:T(8,128)(4,1)}, pred[512,2048]{1,0:T(8,128)(4,1)}, pred[...) fusion(s32[512]{0:T(512)S(1)} %iota_add_fusion.5, ...), kind=kLoop, calls=%fused_computation.43.clone.1 | loop fusion | flops 20971520 | bytes 17838144 | tf_op jit(solution)/shard_map/while/body/eval_jaxpr/and | solution.py:113
  147.5 46.2 %fusion.222 = (f32[2,512]{1,0:T(2,128)S(1)}, f32[2,512,2048]{2,1,0:T(8,128)}) fusion(f32[2]{0:T(128)S(1)} %get-tuple-element.981, pred[512,2048]{1,0:T(8,128)(4,1)} %get-tuple-element.998, f32[2]{0:T(128)S(1)} %get-tuple-element.999, pred[512,2048]{1,0:T(8,128)(4,1)} %get-tuple-element.1000, f32[2]{0:T(128)S(1)} %get-tuple-element.1001, ...), kind=kOutput, calls=%fused_computation.324.clone.1 | convolution fusion | flops 406846464 | bytes 42602756 | tf_op jit(solution)/shard_map/while/body/eval_jaxpr/qhd,khd->hqk/dot_general | solution.py:115
  208.0 23.1 %fusion.221 = (pred[512,2048]{1,0:T(8,128)(4,1)S(1)}, pred[512,2048]{1,0:T(8,128)(4,1)S(1)}, pred[512,2048]{1,0:T(8,128)(4,1)}, pred[512,2048]{1,0:T(8,128)(4,1)...) fusion(s32[]{:T(128)} %bitcast.476, ...), kind=kLoop, calls=%fused_computation.41.clone.1 | loop fusion | flops 16777216 | bytes 15730748 | tf_op jit(solution)/shard_map/while/body/eval_jaxpr/ge | solution.py:121
  231.1 25.4 %fusion.219 = (pred[512,2048]{1,0:T(8,128)(4,1)}, pred[512,2048]{1,0:T(8,128)(4,1)}, pred[512,2048]{1,0:T(8,128)(4,1)}, pred[512,2048]{1,0:T(8,128)(4,1)}, pred[...) fusion(s32[512]{0:T(512)S(1)} %iota_add_fusion.5, ...), kind=kLoop, calls=%fused_computation.43.clone.1 | loop fusion | flops 20971520 | bytes 17838144 | tf_op jit(solution)/shard_map/while/body/eval_jaxpr/and | solution.py:113
  256.5 46.2 %fusion.222 = (f32[2,512]{1,0:T(2,128)S(1)}, f32[2,512,2048]{2,1,0:T(8,128)}) fusion(f32[2]{0:T(128)S(1)} %get-tuple-element.981, pred[512,2048]{1,0:T(8,128)(4,1)} %get-tuple-element.998, f32[2]{0:T(128)S(1)} %get-tuple-element.999, pred[512,2048]{1,0:T(8,128)(4,1)} %get-tuple-element.1000, f32[2]{0:T(128)S(1)} %get-tuple-element.1001, ...), kind=kOutput, calls=%fused_computation.324.clone.1 | convolution fusion | flops 406846464 | bytes 42602756 | tf_op jit(solution)/shard_map/while/body/eval_jaxpr/qhd,khd->hqk/dot_general | solution.py:115
  316.9 23.1 %fusion.221 = (pred[512,2048]{1,0:T(8,128)(4,1)S(1)}, pred[512,2048]{1,0:T(8,128)(4,1)S(1)}, pred[512,2048]{1,0:T(8,128)(4,1)}, pred[512,2048]{1,0:T(8,128)(4,1)...) fusion(s32[]{:T(128)} %bitcast.476, ...), kind=kLoop, calls=%fused_computation.41.clone.1 | loop fusion | flops 16777216 | bytes 15730748 | tf_op jit(solution)/shard_map/while/body/eval_jaxpr/ge | solution.py:121
  340.0 25.4 %fusion.219 = (pred[512,2048]{1,0:T(8,128)(4,1)}, pred[512,2048]{1,0:T(8,128)(4,1)}, pred[512,2048]{1,0:T(8,128)(4,1)}, pred[512,2048]{1,0:T(8,128)(4,1)}, pred[...) fusion(s32[512]{0:T(512)S(1)} %iota_add_fusion.5, ...), kind=kLoop, calls=%fused_computation.43.clone.1 | loop fusion | flops 20971520 | bytes 17838144 | tf_op jit(solution)/shard_map/while/body/eval_jaxpr/and | solution.py:113
  365.4 46.2 %fusion.222 = (f32[2,512]{1,0:T(2,128)S(1)}, f32[2,512,2048]{2,1,0:T(8,128)}) fusion(f32[2]{0:T(128)S(1)} %get-tuple-element.981, pred[512,2048]{1,0:T(8,128)(4,1)} %get-tuple-element.998, f32[2]{0:T(128)S(1)} %get-tuple-element.999, pred[512,2048]{1,0:T(8,128)(4,1)} %get-tuple-element.1000, f32[2]{0:T(128)S(1)} %get-tuple-element.1001, ...), kind=kOutput, calls=%fused_computation.324.clone.1 | convolution fusion | flops 406846464 | bytes 42602756 | tf_op jit(solution)/shard_map/while/body/eval_jaxpr/qhd,khd->hqk/dot_general | solution.py:115
  425.8 23.1 %fusion.221 = (pred[512,2048]{1,0:T(8,128)(4,1)S(1)}, pred[512,2048]{1,0:T(8,128)(4,1)S(1)}, pred[512,2048]{1,0:T(8,128)(4,1)}, pred[512,2048]{1,0:T(8,128)(4,1)...) fusion(s32[]{:T(128)} %bitcast.476, ...), kind=kLoop, calls=%fused_computation.41.clone.1 | loop fusion | flops 16777216 | bytes 15730748 | tf_op jit(solution)/shard_map/while/body/eval_jaxpr/ge | solution.py:121
  448.9 25.4 %fusion.219 = (pred[512,2048]{1,0:T(8,128)(4,1)}, pred[512,2048]{1,0:T(8,128)(4,1)}, pred[512,2048]{1,0:T(8,128)(4,1)}, pred[512,2048]{1,0:T(8,128)(4,1)}, pred[...) fusion(s32[512]{0:T(512)S(1)} %iota_add_fusion.5, ...), kind=kLoop, calls=%fused_computation.43.clone.1 | loop fusion | flops 20971520 | bytes 17838144 | tf_op jit(solution)/shard_map/while/body/eval_jaxpr/and | solution.py:113
  474.3 46.2 %fusion.222 = (f32[2,512]{1,0:T(2,128)S(1)}, f32[2,512,2048]{2,1,0:T(8,128)}) fusion(f32[2]{0:T(128)S(1)} %get-tuple-element.981, pred[512,2048]{1,0:T(8,128)(4,1)} %get-tuple-element.998, f32[2]{0:T(128)S(1)} %get-tuple-element.999, pred[512,2048]{1,0:T(8,128)(4,1)} %get-tuple-element.1000, f32[2]{0:T(128)S(1)} %get-tuple-element.1001, ...), kind=kOutput, calls=%fused_computation.324.clone.1 | convolution fusion | flops 406846464 | bytes 42602756 | tf_op jit(solution)/shard_map/while/body/eval_jaxpr/qhd,khd->hqk/dot_general | solution.py:115
  534.0 9.9 all_gather.41
  562.1 13.8 add_convert_fusion
  599.8 7.9 all-to-all-done.4
  609.5 689.0 %while.31 = (s32[]{:T(128)}, f32[2048,2,64]{0,2,1:T(8,128)S(1)}, f32[2048,2,64]{0,2,1:T(8,128)}, f32[32,2]{0,1:T(2,128)S(1)}, bf16[4,512,2,64]{1,3,2,0:T(8,128)(...) while((s32[]{:T(128)}, f32[2048,2,64]{0,2,1:T(8,128)S(1)}, ...), condition=%wide.region_48.50_spmd.clone, body=%wide.region_14.49_spmd.clone.sunk | while | flops 1668611712 | bytes 303345152 | solution.py:206
  619.5 21.0 %fusion.238 = (pred[512,2048]{1,0:T(8,128)(4,1)S(1)}, pred[512,2048]{1,0:T(8,128)(4,1)}, pred[512,2048]{1,0:T(8,128)(4,1)}, pred[512,2048]{1,0:T(8,128)(4,1)}, p...) fusion(s32[]{:T(128)} %bitcast.518, ...), kind=kLoop, calls=%fused_computation.181.clone.1 | loop fusion | flops 16777216 | bytes 15730748 | tf_op jit(solution)/shard_map/while/body/eval_jaxpr/ge | solution.py:121
  640.5 25.6 %fusion.235 = (pred[512,2048]{1,0:T(8,128)(4,1)}, pred[512,2048]{1,0:T(8,128)(4,1)}, pred[512,2048]{1,0:T(8,128)(4,1)}, pred[512,2048]{1,0:T(8,128)(4,1)}, pred[...) fusion(s32[512]{0:T(512)S(1)} %iota_add_fusion.6, ...), kind=kLoop, calls=%fused_computation.185.clone.1 | loop fusion | flops 20971520 | bytes 17838144 | tf_op jit(solution)/shard_map/while/body/eval_jaxpr/and | solution.py:113
  666.1 48.5 %multiply_reduce_fusion.6 = (f32[2,512]{1,0:T(2,128)S(1)}, f32[2,512,2048]{2,1,0:T(8,128)}) fusion(f32[2,512,2048]{2,1,0:T(8,128)} %fusion.236, f32[2,512]{1,0:T(2,128)S(1)} %constant_dynamic-slice_fusion.3, f32[2]{0:T(128)S(1)} %get-tuple-element.1122, pred[512,2048]{1,0:T(8,128)(4,1)} %get-tuple-element.1123, f32[2]{0:T(128)S(1)} %get-tuple-element.1124, ...), kind=kOutput, calls=%fused_computation.148.clone.1 | convolution fusion | flops 411040768 | bytes 50995460 | tf_op jit(solution)/shard_map/while/body/eval_jaxpr/qhd,khd->hqk/dot_general | solution.py:115
  714.6 26.0 %fusion.239 = (f32[2]{0:T(128)S(1)}, f32[2]{0:T(128)S(1)}, f32[2]{0:T(128)S(1)}, f32[2]{0:T(128)S(1)}, f32[2]{0:T(128)S(1)}, /*index=5*/f32[2]{0:T(128)S(1)}, f3...) fusion(pred[512,2048]{1,0:T(8,128)(4,1)} %get-tuple-element.110, ...), kind=kLoop, calls=%fused_computation.145.clone.1 | loop fusion | flops 62914544 | bytes 34607208 | tf_op jit(solution)/shard_map/while/body/eval_jaxpr/reduce_sum | solution.py:197
  746.7 26.2 %fusion.242 = (f32[2]{0:T(128)S(1)}, f32[2]{0:T(128)S(1)}, f32[2]{0:T(128)S(1)}, f32[2]{0:T(128)S(1)}, f32[2]{0:T(128)S(1)}, /*index=5*/f32[2]{0:T(128)S(1)}, f3...) fusion(bf16[2,512,2048]{2,1,0:T(8,128)(2,1)S(1)} %get-tuple-ele, ...), kind=kLoop, calls=%fused_computation.146.clone.1 | loop fusion | flops 79691760 | bytes 23068824 | tf_op jit(solution)/shard_map/while/body/eval_jaxpr/reduce_sum | solution.py:197
  792.0 21.0 %fusion.238 = (pred[512,2048]{1,0:T(8,128)(4,1)S(1)}, pred[512,2048]{1,0:T(8,128)(4,1)}, pred[512,2048]{1,0:T(8,128)(4,1)}, pred[512,2048]{1,0:T(8,128)(4,1)}, p...) fusion(s32[]{:T(128)} %bitcast.518, ...), kind=kLoop, calls=%fused_computation.181.clone.1 | loop fusion | flops 16777216 | bytes 15730748 | tf_op jit(solution)/shard_map/while/body/eval_jaxpr/ge | solution.py:121
  813.0 25.6 %fusion.235 = (pred[512,2048]{1,0:T(8,128)(4,1)}, pred[512,2048]{1,0:T(8,128)(4,1)}, pred[512,2048]{1,0:T(8,128)(4,1)}, pred[512,2048]{1,0:T(8,128)(4,1)}, pred[...) fusion(s32[512]{0:T(512)S(1)} %iota_add_fusion.6, ...), kind=kLoop, calls=%fused_computation.185.clone.1 | loop fusion | flops 20971520 | bytes 17838144 | tf_op jit(solution)/shard_map/while/body/eval_jaxpr/and | solution.py:113
  838.6 48.0 %multiply_reduce_fusion.6 = (f32[2,512]{1,0:T(2,128)S(1)}, f32[2,512,2048]{2,1,0:T(8,128)}) fusion(f32[2,512,2048]{2,1,0:T(8,128)} %fusion.236, f32[2,512]{1,0:T(2,128)S(1)} %constant_dynamic-slice_fusion.3, f32[2]{0:T(128)S(1)} %get-tuple-element.1122, pred[512,2048]{1,0:T(8,128)(4,1)} %get-tuple-element.1123, f32[2]{0:T(128)S(1)} %get-tuple-element.1124, ...), kind=kOutput, calls=%fused_computation.148.clone.1 | convolution fusion | flops 411040768 | bytes 50995460 | tf_op jit(solution)/shard_map/while/body/eval_jaxpr/qhd,khd->hqk/dot_general | solution.py:115
  886.6 26.0 %fusion.239 = (f32[2]{0:T(128)S(1)}, f32[2]{0:T(128)S(1)}, f32[2]{0:T(128)S(1)}, f32[2]{0:T(128)S(1)}, f32[2]{0:T(128)S(1)}, /*index=5*/f32[2]{0:T(128)S(1)}, f3...) fusion(pred[512,2048]{1,0:T(8,128)(4,1)} %get-tuple-element.110, ...), kind=kLoop, calls=%fused_computation.145.clone.1 | loop fusion | flops 62914544 | bytes 34607208 | tf_op jit(solution)/shard_map/while/body/eval_jaxpr/reduce_sum | solution.py:197
  918.6 26.2 %fusion.242 = (f32[2]{0:T(128)S(1)}, f32[2]{0:T(128)S(1)}, f32[2]{0:T(128)S(1)}, f32[2]{0:T(128)S(1)}, f32[2]{0:T(128)S(1)}, /*index=5*/f32[2]{0:T(128)S(1)}, f3...) fusion(bf16[2,512,2048]{2,1,0:T(8,128)(2,1)S(1)} %get-tuple-ele, ...), kind=kLoop, calls=%fused_computation.146.clone.1 | loop fusion | flops 79691760 | bytes 23068824 | tf_op jit(solution)/shard_map/while/body/eval_jaxpr/reduce_sum | solution.py:197
  964.0 21.0 %fusion.238 = (pred[512,2048]{1,0:T(8,128)(4,1)S(1)}, pred[512,2048]{1,0:T(8,128)(4,1)}, pred[512,2048]{1,0:T(8,128)(4,1)}, pred[512,2048]{1,0:T(8,128)(4,1)}, p...) fusion(s32[]{:T(128)} %bitcast.518, ...), kind=kLoop, calls=%fused_computation.181.clone.1 | loop fusion | flops 16777216 | bytes 15730748 | tf_op jit(solution)/shard_map/while/body/eval_jaxpr/ge | solution.py:121
  985.0 25.6 %fusion.235 = (pred[512,2048]{1,0:T(8,128)(4,1)}, pred[512,2048]{1,0:T(8,128)(4,1)}, pred[512,2048]{1,0:T(8,128)(4,1)}, pred[512,2048]{1,0:T(8,128)(4,1)}, pred[...) fusion(s32[512]{0:T(512)S(1)} %iota_add_fusion.6, ...), kind=kLoop, calls=%fused_computation.185.clone.1 | loop fusion | flops 20971520 | bytes 17838144 | tf_op jit(solution)/shard_map/while/body/eval_jaxpr/and | solution.py:113
  1010.6 48.0 %multiply_reduce_fusion.6 = (f32[2,512]{1,0:T(2,128)S(1)}, f32[2,512,2048]{2,1,0:T(8,128)}) fusion(f32[2,512,2048]{2,1,0:T(8,128)} %fusion.236, f32[2,512]{1,0:T(2,128)S(1)} %constant_dynamic-slice_fusion.3, f32[2]{0:T(128)S(1)} %get-tuple-element.1122, pred[512,2048]{1,0:T(8,128)(4,1)} %get-tuple-element.1123, f32[2]{0:T(128)S(1)} %get-tuple-element.1124, ...), kind=kOutput, calls=%fused_computation.148.clone.1 | convolution fusion | flops 411040768 | bytes 50995460 | tf_op jit(solution)/shard_map/while/body/eval_jaxpr/qhd,khd->hqk/dot_general | solution.py:115
  1058.6 26.0 %fusion.239 = (f32[2]{0:T(128)S(1)}, f32[2]{0:T(128)S(1)}, f32[2]{0:T(128)S(1)}, f32[2]{0:T(128)S(1)}, f32[2]{0:T(128)S(1)}, /*index=5*/f32[2]{0:T(128)S(1)}, f3...) fusion(pred[512,2048]{1,0:T(8,128)(4,1)} %get-tuple-element.110, ...), kind=kLoop, calls=%fused_computation.145.clone.1 | loop fusion | flops 62914544 | bytes 34607208 | tf_op jit(solution)/shard_map/while/body/eval_jaxpr/reduce_sum | solution.py:197
  1090.6 26.2 %fusion.242 = (f32[2]{0:T(128)S(1)}, f32[2]{0:T(128)S(1)}, f32[2]{0:T(128)S(1)}, f32[2]{0:T(128)S(1)}, f32[2]{0:T(128)S(1)}, /*index=5*/f32[2]{0:T(128)S(1)}, f3...) fusion(bf16[2,512,2048]{2,1,0:T(8,128)(2,1)S(1)} %get-tuple-ele, ...), kind=kLoop, calls=%fused_computation.146.clone.1 | loop fusion | flops 79691760 | bytes 23068824 | tf_op jit(solution)/shard_map/while/body/eval_jaxpr/reduce_sum | solution.py:197
  1136.0 21.0 %fusion.238 = (pred[512,2048]{1,0:T(8,128)(4,1)S(1)}, pred[512,2048]{1,0:T(8,128)(4,1)}, pred[512,2048]{1,0:T(8,128)(4,1)}, pred[512,2048]{1,0:T(8,128)(4,1)}, p...) fusion(s32[]{:T(128)} %bitcast.518, ...), kind=kLoop, calls=%fused_computation.181.clone.1 | loop fusion | flops 16777216 | bytes 15730748 | tf_op jit(solution)/shard_map/while/body/eval_jaxpr/ge | solution.py:121
  1157.0 25.6 %fusion.235 = (pred[512,2048]{1,0:T(8,128)(4,1)}, pred[512,2048]{1,0:T(8,128)(4,1)}, pred[512,2048]{1,0:T(8,128)(4,1)}, pred[512,2048]{1,0:T(8,128)(4,1)}, pred[...) fusion(s32[512]{0:T(512)S(1)} %iota_add_fusion.6, ...), kind=kLoop, calls=%fused_computation.185.clone.1 | loop fusion | flops 20971520 | bytes 17838144 | tf_op jit(solution)/shard_map/while/body/eval_jaxpr/and | solution.py:113
  1182.6 48.0 %multiply_reduce_fusion.6 = (f32[2,512]{1,0:T(2,128)S(1)}, f32[2,512,2048]{2,1,0:T(8,128)}) fusion(f32[2,512,2048]{2,1,0:T(8,128)} %fusion.236, f32[2,512]{1,0:T(2,128)S(1)} %constant_dynamic-slice_fusion.3, f32[2]{0:T(128)S(1)} %get-tuple-element.1122, pred[512,2048]{1,0:T(8,128)(4,1)} %get-tuple-element.1123, f32[2]{0:T(128)S(1)} %get-tuple-element.1124, ...), kind=kOutput, calls=%fused_computation.148.clone.1 | convolution fusion | flops 411040768 | bytes 50995460 | tf_op jit(solution)/shard_map/while/body/eval_jaxpr/qhd,khd->hqk/dot_general | solution.py:115
  1230.6 26.0 %fusion.239 = (f32[2]{0:T(128)S(1)}, f32[2]{0:T(128)S(1)}, f32[2]{0:T(128)S(1)}, f32[2]{0:T(128)S(1)}, f32[2]{0:T(128)S(1)}, /*index=5*/f32[2]{0:T(128)S(1)}, f3...) fusion(pred[512,2048]{1,0:T(8,128)(4,1)} %get-tuple-element.110, ...), kind=kLoop, calls=%fused_computation.145.clone.1 | loop fusion | flops 62914544 | bytes 34607208 | tf_op jit(solution)/shard_map/while/body/eval_jaxpr/reduce_sum | solution.py:197
  1262.6 26.2 %fusion.242 = (f32[2]{0:T(128)S(1)}, f32[2]{0:T(128)S(1)}, f32[2]{0:T(128)S(1)}, f32[2]{0:T(128)S(1)}, f32[2]{0:T(128)S(1)}, /*index=5*/f32[2]{0:T(128)S(1)}, f3...) fusion(bf16[2,512,2048]{2,1,0:T(8,128)(2,1)S(1)} %get-tuple-ele, ...), kind=kLoop, calls=%fused_computation.146.clone.1 | loop fusion | flops 79691760 | bytes 23068824 | tf_op jit(solution)/shard_map/while/body/eval_jaxpr/reduce_sum | solution.py:197
  1322.1 9.7 all-to-all-done.2
  1333.2 18.5 %reduce-scatter.6.cloned.1.call-done = bf16[512,512]{1,0:T(8,128)(2,1)} async-done(((bf16[2048,512]{1,0:T(8,128)(2,1)}), bf16[512,512]{1,0:T(8,128)(2,1)}) %reduce-scatter.6.cloned.1.call-update) | async-done | bytes 524304 | tf_op jit(solution)/shard_map/reduce_scatter | solution.py:224
  1361.3 27.3 %reduce-scatter.8.cloned.1.call-done = bf16[64,3,128]{2,0,1:T(8,128)(2,1)} async-done(((bf16[512,3,128]{2,0,1:T(8,128)(2,1)}), bf16[64,3,128]{2,0,1:T(8,128)(2,1)}) %reduce-scatter.8.cloned.1.call-update) | async-done | bytes 49168 | tf_op jit(solution)/shard_map/reduce_scatter | solution.py:246
  1389.4 17.6 %all_gather.46 = f32[64,3,512]{2,0,1:T(8,128)S(1)} all-gather(f32[64,3,128]{2,0,1:T(8,128)S(1)} %convert_element_type.179), channel_id=1, replica_groups=mesh['seq'=4,'dp'=8] {'seq'}, dimensions={2}, use_global_device_ids=true | all-gather | bytes 491520 | tf_op jit(solution)/shard_map/all_gather | solution.py:278
  1407.7 24.7 %all-reduce.16.cloned.1.call-done = (bf16[64,512]{1,0:T(8,128)(2,1)}, bf16[64,2048]{1,0:T(8,128)(2,1)}, bf16[256,512]{1,0:T(8,128)(2,1)}) async-done(((bf16[64,512]{1,0:T(8,128)(2,1)}, bf16[64,2048]{1,0:T(8,128)(2,1)}, bf16[256,512]{1,0:T(8,128)(2,1)}), (bf16[64,512]{1,0:T(8,128)(2,1)}, bf16[64,2048]{1,0:T(8,128)(2,1)}, bf16[256,512]{1,0:T(8,128)(2,1)})) %all-reduce.16.cloned.1.call-update) | async-done | bytes 589840 | tf_op jit(solution)/shard_map/psum | solution.py:271
  1437.6 23.5 %all-reduce.10 = (bf16[512]{0:T(512)(128)(2,1)S(1)}, bf16[512]{0:T(512)(128)(2,1)S(1)}, bf16[32,2]{1,0:T(8,128)(2,1)S(1)}, bf16[512]{0:T(512)(128)(2,1)S(1)}, bf16[512]{0:T(512)(128)(2,1)S(1)}) all-reduce(bf16[512]{0:T(512)(128)(2,1)S(1)} %get-tuple-element.329, ...), channel_id=3, replica_groups=mesh['seq'=4,'dp'=8] {'dp'}, use_global_device_ids=true, to_apply=%region_53.55.clone | all-reduce | flops 2112 | bytes 8448
  1461.3 8.8 all-gather.1
  1470.4 9.1 all-reduce.12
  (615 shorter events, 254.3 us)
Async XLA Ops:
  7.2 42.5 %all-gather.9.cloned.1.call-start = ((), (), s32[]{:S(2)}) async-start(), calls=%async_computation.12 | async-start | bytes 1769472 | tf_op jit(solution)/shard_map/all_gather | solution.py:78
  8.7 31.2 %copy-start.63 = (s32[1,3]{1,0:T(1,128)S(1)}, s32[1,3]{1,0:T(1,128)}, u32[]{:S(2)}) copy-start(s32[1,3]{1,0:T(1,128)} %param.23) | copy-start | bytes 40
  8.8 31.5 %copy-start.54 = (bf16[4,8]{1,0:T(4,128)(2,1)S(1)}, bf16[4,8]{1,0:T(4,128)(2,1)}, u32[]{:S(2)}) copy-start(bf16[4,8]{1,0:T(4,128)(2,1)} %param.29) | copy-start | bytes 196
  8.8 40.7 %copy-start.52 = (s32[1024]{0:T(1024)S(1)}, s32[1024]{0:T(1024)}, u32[]{:S(2)}) copy-start(s32[1024]{0:T(1024)} %param.24) | copy-start | bytes 12292
  12.1 24.1 %all-to-all-start = ((bf16[8,64,512]{2,1,0:T(8,128)(2,1)}), bf16[8,64,512]{2,1,0:T(8,128)(2,1)S(1)}, u32[]{:S(2)}, u32[]{:S(2)}) async-start(bf16[8,64,512]{2,1,0:T(8,128)(2,1)} %get-tuple-element.607), calls=%async_computation | async-start | bytes 1048576 | tf_op jit(solution)/shard_map/all_to_all | solution.py:70
  17.3 72.7 %all-gather.7.cloned.1.call-start = ((), (), s32[]{:S(2)}) async-start(), calls=%async_computation.11 | async-start | bytes 2621440 | tf_op jit(solution)/shard_map/all_gather | solution.py:93
  38.6 515.8 %all-gather.11.cloned.1.call-start = ((), (), s32[]{:S(2)}) async-start(), calls=%async_computation.13 | async-start | bytes 2359296 | tf_op jit(solution)/shard_map/all_gather | solution.py:83
  39.3 522.8 %all-gather.13.cloned.1.call-start = ((), (), s32[]{:S(2)}) async-start(), calls=%async_computation.14 | async-start | bytes 2359296 | tf_op jit(solution)/shard_map/all_gather | solution.py:84
  51.5 41.3 %copy-start.39 = (bf16[512,3,128]{0,2,1:T(8,128)(2,1)}, bf16[512,3,128]{0,2,1:T(8,128)(2,1)S(1)}, u32[]{:S(2)}) copy-start(bf16[512,3,128]{0,2,1:T(8,128)(2,1)S(1)} %constant_dynamic-slice_fusion.1) | copy-start | bytes 1179652
  94.0 439.9 %copy-start.58 = (bf16[512]{0:T(512)(128)(2,1)S(1)}, bf16[512]{0:T(512)(128)(2,1)}, u32[]{:S(2)}) copy-start(bf16[512]{0:T(512)(128)(2,1)} %get-tuple-element.392) | copy-start | bytes 3076
  94.0 439.9 %copy-start.57 = (bf16[512]{0:T(512)(128)(2,1)S(1)}, bf16[512]{0:T(512)(128)(2,1)}, u32[]{:S(2)}) copy-start(bf16[512]{0:T(512)(128)(2,1)} %get-tuple-element.391) | copy-start | bytes 3076
  94.0 439.9 %copy-start.41 = (bf16[64,512]{1,0:T(8,128)(2,1)S(1)}, bf16[64,512]{1,0:T(8,128)(2,1)}, u32[]{:S(2)}) copy-start(bf16[64,512]{1,0:T(8,128)(2,1)} %param.28) | copy-start | bytes 196612
  94.0 458.4 %copy-start.22 = (bf16[8,64,512]{2,1,0:T(8,128)(2,1)S(1)}, bf16[8,64,512]{2,1,0:T(8,128)(2,1)}, u32[]{:S(2)}) copy-start(bf16[8,64,512]{2,1,0:T(8,128)(2,1)} %copy-done.21) | copy-start | bytes 1572868
  530.4 18.4 %all-to-all-start.1 = ((bf16[4,512,128]{1,2,0:T(8,128)(2,1)}), bf16[4,512,128]{1,2,0:T(8,128)(2,1)S(1)}, u32[]{:S(2)}, u32[]{:S(2)}) async-start(bf16[4,512,128]{1,2,0:T(8,128)(2,1)} %bitcast.583), calls=%async_computation.1 | async-start | bytes 1048576 | tf_op jit(solution)/shard_map/all_to_all | solution.py:140
  548.8 13.3 all-to-all-start.3
  552.4 780.8 %reduce-scatter.10.cloned.1.call-start = ((), (), s32[]{:S(2)}) async-start(), calls=%async_computation.17 | async-start | bytes 589824 | tf_op jit(solution)/shard_map/reduce_scatter | solution.py:249
  554.0 41.2 %copy-start.25 = (f32[512,512]{1,0:T(8,128)}, f32[512,512]{1,0:T(8,128)S(1)}, u32[]{:S(2)}) copy-start(f32[512,512]{1,0:T(8,128)S(1)} %get-tuple-element.609) | copy-start | bytes 3145732
  580.9 752.3 %reduce-scatter.14.cloned.1.call-start = ((), (), s32[]{:S(2)}) async-start(), calls=%async_computation.19 | async-start | bytes 2359296 | tf_op jit(solution)/shard_map/reduce_scatter | solution.py:264
  591.0 16.7 %all-to-all-start.4 = ((bf16[512,4,128]{0,2,1:T(8,128)(2,1)}), bf16[512,4,128]{0,2,1:T(8,128)(2,1)}, u32[]{:S(2)}, u32[]{:S(2)}) async-start(bf16[512,4,128]{0,2,1:T(8,128)(2,1)} %bitcast.23), calls=%async_computation.4 | async-start | bytes 1048576 | tf_op jit(solution)/shard_map/all_to_all | solution.py:165
  595.1 738.1 %reduce-scatter.12.cloned.1.call-start = ((), (), s32[]{:S(2)}) async-start(), calls=%async_computation.18 | async-start | bytes 2359296 | tf_op jit(solution)/shard_map/reduce_scatter | solution.py:261
  599.7 752.0 %reduce-scatter.6.cloned.1.call-start = ((), (), s32[]{:S(2)}) async-start(), calls=%async_computation.15 | async-start | bytes 2621440 | tf_op jit(solution)/shard_map/reduce_scatter | solution.py:224
  714.6 26.1 %copy-start.4 = (f32[2,512,2048]{2,1,0:T(8,128)S(1)}, f32[2,512,2048]{2,1,0:T(8,128)}, u32[]{:S(2)}) copy-start(f32[2,512,2048]{2,1,0:T(8,128)} %get-tuple-element.1188) | copy-start | bytes 25165828 | tf_op jit(solution)/shard_map/while
  714.6 26.1 %copy-start.18 = (f32[2048,2,64]{0,2,1:T(8,128)S(1)}, f32[2048,2,64]{0,2,1:T(8,128)}, u32[]{:S(2)}) copy-start(f32[2048,2,64]{0,2,1:T(8,128)} %get-tuple-element.1285) | copy-start | bytes 3145732 | tf_op jit(solution)/shard_map/while
  714.6 29.8 %copy-start.16 = (pred[512,2048]{1,0:T(8,128)(4,1)S(1)}, pred[512,2048]{1,0:T(8,128)(4,1)}, u32[]{:S(2)}) copy-start(pred[512,2048]{1,0:T(8,128)(4,1)} %get-tuple-element.1177) | copy-start | bytes 3145732 | tf_op jit(solution)/shard_map/while
  714.6 29.8 %copy-start.17 = (pred[512,2048]{1,0:T(8,128)(4,1)S(1)}, pred[512,2048]{1,0:T(8,128)(4,1)}, u32[]{:S(2)}) copy-start(pred[512,2048]{1,0:T(8,128)(4,1)} %get-tuple-element.1179) | copy-start | bytes 3145732 | tf_op jit(solution)/shard_map/while
  886.6 29.8 %copy-start.16 = (pred[512,2048]{1,0:T(8,128)(4,1)S(1)}, pred[512,2048]{1,0:T(8,128)(4,1)}, u32[]{:S(2)}) copy-start(pred[512,2048]{1,0:T(8,128)(4,1)} %get-tuple-element.1177) | copy-start | bytes 3145732 | tf_op jit(solution)/shard_map/while
  886.6 29.8 %copy-start.17 = (pred[512,2048]{1,0:T(8,128)(4,1)S(1)}, pred[512,2048]{1,0:T(8,128)(4,1)}, u32[]{:S(2)}) copy-start(pred[512,2048]{1,0:T(8,128)(4,1)} %get-tuple-element.1179) | copy-start | bytes 3145732 | tf_op jit(solution)/shard_map/while
  1058.6 29.8 %copy-start.16 = (pred[512,2048]{1,0:T(8,128)(4,1)S(1)}, pred[512,2048]{1,0:T(8,128)(4,1)}, u32[]{:S(2)}) copy-start(pred[512,2048]{1,0:T(8,128)(4,1)} %get-tuple-element.1177) | copy-start | bytes 3145732 | tf_op jit(solution)/shard_map/while
  1058.6 29.8 %copy-start.17 = (pred[512,2048]{1,0:T(8,128)(4,1)S(1)}, pred[512,2048]{1,0:T(8,128)(4,1)}, u32[]{:S(2)}) copy-start(pred[512,2048]{1,0:T(8,128)(4,1)} %get-tuple-element.1179) | copy-start | bytes 3145732 | tf_op jit(solution)/shard_map/while
  1230.6 29.7 %copy-start.16 = (pred[512,2048]{1,0:T(8,128)(4,1)S(1)}, pred[512,2048]{1,0:T(8,128)(4,1)}, u32[]{:S(2)}) copy-start(pred[512,2048]{1,0:T(8,128)(4,1)} %get-tuple-element.1177) | copy-start | bytes 3145732 | tf_op jit(solution)/shard_map/while
  1230.6 29.7 %copy-start.17 = (pred[512,2048]{1,0:T(8,128)(4,1)S(1)}, pred[512,2048]{1,0:T(8,128)(4,1)}, u32[]{:S(2)}) copy-start(pred[512,2048]{1,0:T(8,128)(4,1)} %get-tuple-element.1179) | copy-start | bytes 3145732 | tf_op jit(solution)/shard_map/while
  1308.1 80.5 %reduce-scatter.8.cloned.1.call-start = ((), (), s32[]{:S(2)}) async-start(), calls=%async_computation.16 | async-start | bytes 442368 | tf_op jit(solution)/shard_map/reduce_scatter | solution.py:246
  1313.1 38.6 %copy-start.23 = (bf16[8,64,512]{2,1,0:T(8,128)(2,1)S(1)}, bf16[8,64,512]{2,1,0:T(8,128)(2,1)}, u32[]{:S(2)}) copy-start(bf16[8,64,512]{2,1,0:T(8,128)(2,1)} %copy-done.21) | copy-start | bytes 1572868
  1313.2 38.5 %copy-start.43 = (f32[512]{0:T(512)S(1)}, f32[512]{0:T(512)}, u32[]{:S(2)}) copy-start(f32[512]{0:T(512)} %copy-done.42) | copy-start | bytes 6148
  1313.2 38.5 %copy-start.45 = (f32[512]{0:T(512)S(1)}, f32[512]{0:T(512)}, u32[]{:S(2)}) copy-start(f32[512]{0:T(512)} %copy-done.44) | copy-start | bytes 6148
  1313.2 39.9 %copy-start.51 = (f32[512]{0:T(512)S(1)}, f32[512]{0:T(512)}, u32[]{:S(2)}) copy-start(f32[512]{0:T(512)} %copy-done.50) | copy-start | bytes 6148
  1313.2 39.9 %copy-start.47 = (f32[512]{0:T(512)S(1)}, f32[512]{0:T(512)}, u32[]{:S(2)}) copy-start(f32[512]{0:T(512)} %copy-done.46) | copy-start | bytes 6148
  1317.8 37.1 %copy-start.28 = (f32[512,512]{1,0:T(8,128)S(1)}, f32[512,512]{1,0:T(8,128)}, u32[]{:S(2)}) copy-start(f32[512,512]{1,0:T(8,128)} %copy-done.27) | copy-start | bytes 3145732
  1317.8 37.1 %copy-start.33 = (bf16[8,64,512]{2,1,0:T(8,128)(2,1)S(1)}, bf16[8,64,512]{2,1,0:T(8,128)(2,1)}, u32[]{:S(2)}) copy-start(bf16[8,64,512]{2,1,0:T(8,128)(2,1)} %copy-done.32) | copy-start | bytes 1572868
  1317.8 37.1 %copy-start.49 = (f32[512]{0:T(512)S(1)}, f32[512]{0:T(512)}, u32[]{:S(2)}) copy-start(f32[512]{0:T(512)} %copy-done.48) | copy-start | bytes 6148
  1317.8 14.0 all-to-all-start.2
  1322.0 110.4 %all-reduce.16.cloned.1.call-start = ((), (), s32[]{:S(2)}) async-start(), calls=%async_computation.20 | async-start | bytes 1179648 | tf_op jit(solution)/shard_map/psum | solution.py:271
  1353.1 84.4 %copy-start.29 = (bf16[512,512]{1,0:T(8,128)(2,1)S(1)}, bf16[512,512]{1,0:T(8,128)(2,1)}, u32[]{:S(2)}) copy-start(bf16[512,512]{1,0:T(8,128)(2,1)} %reduce-scatter.6.cloned.1.call-done) | copy-start | bytes 1572868
  1354.9 82.7 %copy-start.55 = (bf16[512]{0:T(512)(128)(2,1)S(1)}, bf16[512]{0:T(512)(128)(2,1)}, u32[]{:S(2)}) copy-start(bf16[512]{0:T(512)(128)(2,1)} %get-tuple-element.327) | copy-start | bytes 3076
  1354.9 82.7 %copy-start.56 = (bf16[512]{0:T(512)(128)(2,1)S(1)}, bf16[512]{0:T(512)(128)(2,1)}, u32[]{:S(2)}) copy-start(bf16[512]{0:T(512)(128)(2,1)} %get-tuple-element.331) | copy-start | bytes 3076
  1354.9 129.0 %copy-start.1 = (bf16[512,512]{1,0:T(8,128)(2,1)S(1)}, bf16[512,512]{1,0:T(8,128)(2,1)}, u32[]{:S(2)}) copy-start(bf16[512,512]{1,0:T(8,128)(2,1)} %param.21) | copy-start | bytes 1572868
  1357.4 125.4 %copy-start.37 = (bf16[8,64,512]{2,1,0:T(8,128)(2,1)S(1)}, bf16[8,64,512]{2,1,0:T(8,128)(2,1)}, u32[]{:S(2)}) copy-start(bf16[8,64,512]{2,1,0:T(8,128)(2,1)} %gather_fusion.1) | copy-start | bytes 1572868
  1357.4 124.8 %all-to-all-start.5 = ((bf16[8,64,512]{2,1,0:T(8,128)(2,1)}), bf16[8,64,512]{2,1,0:T(8,128)(2,1)S(1)}, u32[]{:S(2)}, u32[]{:S(2)}) async-start(bf16[8,64,512]{2,1,0:T(8,128)(2,1)} %bitcast.578), calls=%async_computation.6 | async-start | bytes 1048576 | tf_op jit(solution)/shard_map/all_to_all | solution.py:290
  (94 other events, 626.4 us)
Sparse Core Ops, SparseCore 0:
  10.0 31.8 all-gather.8
  44.0 45.8 all-gather.6
  91.9 26.6 all-gather.10
  120.3 27.8 all-gather.12
  581.1 31.3 reduce-scatter.9
  616.0 41.2 reduce-scatter.13
  660.5 41.1 reduce-scatter.11
  1308.2 43.4 reduce-scatter.5
  1355.3 33.1 reduce-scatter.7
  1391.0 41.3 all-reduce.15
where the time goes:
time: 1500 us; the launch traced here: 1490 us
  other arithmetic  638 us (43%)
  matrix products  492 us (33%)
  waiting for transfers between devices  136 us (9%)
  blocking collectives  94.6 us (6%)
  local copies, waits for them, and re-layouts  69.3 us (5%)
  starting transfers between devices  24.9 us (2%)
  loops' own time  18.1 us (1%)
  between operations  17.2 us (1%)
    dot_general x8, matrix products, scores_of(): jnp.einsum('qhd,khd->hqk', q_block, keys_all, preferred_element_type=jnp....  377 us
    reduce_sum x8, other arithmetic, backward_block(): jnp.sum(jnp.where((distance >= thresholds[level])[None], grad_wide, 0.0),...  209 us
    and x8, other arithmetic, scores_of(): allowed = (row_seg[:, None] == seg_ids[None, :]) & (distance >= 0)  204 us
    ge x8, other arithmetic, scores_of(): distance >= thresholds[level]  176 us
    unnamed x2, blocking collectives  40.1 us
    all_gather x1, waiting for transfers between devices, shards(): all_rows = lax.all_gather(normed_low, 'seq', axis=0, tiled=True)  38.4 us
  transfers between devices with their start and end apart: 16, of which 8 were waited for; matrix products, arithmetic and copies ran while one was open for 78% of the time, Pallas kernels for 0%

commit v1 on v0

v1 whole, which is shorter than its diff:
```python
import functools

import jax
import jax.numpy as jnp
from jax import lax
from jax.experimental import pallas as pl
from jax.experimental.pallas import tpu as pltpu
from jax.sharding import PartitionSpec as P

H = 8
HD = 64
NBK = 32
QB = 256
PAIR = 2 * HD
BIG = -1e30
F32 = jnp.float32
BF16 = jnp.bfloat16
VMEM_LIMIT = 60 * 1024 * 1024

NT = (((1,), (1,)), ((), ()))
NN = (((1,), (0,)), ((), ()))


def dot_nt(a, b):
    return lax.dot_general(a, b, NT, preferred_element_type=F32)


def dot_nn(a, b):
    return lax.dot_general(a, b, NN, preferred_element_type=F32)


def norm_rows(values, gain_vec, bias_vec):
    average = jnp.mean(values, axis=-1, keepdims=True)
    centred = values - average
    variance = jnp.mean(centred * centred, axis=-1, keepdims=True)
    return centred * lax.rsqrt(variance + 1e-05) * gain_vec + bias_vec


def gelu_exact(values):
    return jax.nn.gelu(values, approximate=False)


def toeplitz(row, width):
    return pltpu.roll(jnp.broadcast_to(row, (QB, width)), 0, 1, stride=1, stride_axis=0)


def attention_fwd_kernel(base_ref, q_ref, qx_ref, k_ref, kx_ref, v_ref, att_ref, lse_ref, bias, kaug, vaug, scores):
    rows = q_ref.shape[0]
    width = base_ref.shape[-1]
    tiles = width // QB
    lane_q = lax.broadcasted_iota(jnp.int32, (QB, PAIR), 1) < HD
    lane_k = lax.broadcasted_iota(jnp.int32, k_ref.shape, 1) < HD
    for h in range(2):
        mine_k = lane_k if h == 0 else jnp.logical_not(lane_k)
        mine_q = lane_q if h == 0 else jnp.logical_not(lane_q)
        bias[...] = toeplitz(base_ref[0, h : h + 1, :], width)
        kaug[...] = jnp.where(mine_k, k_ref[...], kx_ref[...])
        vaug[...] = jnp.where(mine_k, v_ref[...], jnp.ones_like(v_ref))
        for b in range(rows // QB):
            here = pl.ds(b * QB, QB)
            q_aug = jnp.where(mine_q, q_ref[here, :], qx_ref[here, :])
            top = None
            for j in range(tiles):
                cols = pl.ds(j * QB, QB)
                s = dot_nt(q_aug, kaug[pl.ds((b + j) * QB, QB), :]) + bias[:, cols]
                scores[:, cols] = s
                most = jnp.maximum(s[:, :128], s[:, 128:])
                top = most if top is None else jnp.maximum(top, most)
            top = jnp.max(top, axis=1, keepdims=True)
            acc = jnp.zeros((QB, PAIR), F32)
            for j in range(tiles):
                p = jnp.exp(scores[:, pl.ds(j * QB, QB)] - top).astype(BF16)
                acc = acc + dot_nn(p, vaug[pl.ds((b + j) * QB, QB), :])
            att = acc / pltpu.roll(acc, HD, 1)
            lse = top + jnp.log(acc)
            if h == 0:
                att_ref[here, :] = att.astype(BF16)
                lse_ref[here, :] = lse
            else:
                att_ref[here, :] = jnp.where(mine_q, att.astype(BF16), att_ref[here, :])
                lse_ref[here, :] = jnp.where(mine_q, lse_ref[here, :], lse)


def attention_bwd_kernel(
    base_ref, q_ref, qx_ref, k_ref, kx_ref, v_ref, att_ref, lse_ref, do_ref,
    dq_ref, dk_ref, dv_ref, dd_ref,
    bias, kaug, vaug, qaug, doaug, dsum, dkt, dvt,
):
    rows = q_ref.shape[0]
    width = base_ref.shape[-1]
    tiles = width // QB
    lane_q = lax.broadcasted_iota(jnp.int32, (rows, PAIR), 1)
    extra = lax.rem(lane_q, HD)
    lane_k = lax.broadcasted_iota(jnp.int32, k_ref.shape, 1) < HD
    swap = (
        (lax.broadcasted_iota(jnp.int32, (PAIR, PAIR), 0) < HD)
        != (lax.broadcasted_iota(jnp.int32, (PAIR, PAIR), 1) < HD)
    ).astype(BF16)
    prod = do_ref[...].astype(F32) * att_ref[...].astype(F32)
    prod_hi = prod.astype(BF16)
    prod_lo = (prod - prod_hi.astype(F32)).astype(BF16)
    delta = -(dot_nn(prod_hi, swap) + dot_nn(prod_lo, swap))
    delta_hi = delta.astype(BF16).astype(F32)
    lse = -lse_ref[...]
    lse_hi = lse.astype(BF16).astype(F32)
    lse_mid = (lse - lse_hi).astype(BF16).astype(F32)
    lse_lo = lse - lse_hi - lse_mid
    q_extra = jnp.where(
        extra == HD - 3, lse_hi, jnp.where(extra == HD - 2, lse_mid, jnp.where(extra == HD - 1, lse_lo, qx_ref[...].astype(F32)))
    ).astype(BF16)
    do_extra = jnp.where(extra == 0, delta_hi, jnp.where(extra == 1, delta - delta_hi, 0.0)).astype(BF16)
    dkt[...] = jnp.zeros_like(dkt)
    dvt[...] = jnp.zeros_like(dvt)
    for h in range(2):
        mine_k = lane_k if h == 0 else jnp.logical_not(lane_k)
        mine_q = (lane_q < HD) if h == 0 else (lane_q >= HD)
        bias[...] = toeplitz(base_ref[0, h : h + 1, :], width)
        kaug[...] = jnp.where(mine_k, k_ref[...], kx_ref[...])
        vaug[...] = jnp.where(mine_k, v_ref[...], jnp.ones_like(v_ref))
        qaug[...] = jnp.where(mine_q, q_ref[...], q_extra)
        doaug[...] = jnp.where(mine_q, do_ref[...], do_extra)
        feat = pl.ds(h * HD, HD)
        for b in range(rows // QB):
            here = pl.ds(b * QB, QB)
            q_t = q_ref[here, :].astype(F32).T[h * HD : (h + 1) * HD].astype(BF16)
            do_t = do_ref[here, :].astype(F32).T[h * HD : (h + 1) * HD].astype(BF16)
            dq = jnp.zeros((QB, PAIR), F32)
            for j in range(tiles):
                cols = pl.ds(j * QB, QB)
                keys = pl.ds((b + j) * QB, QB)
                p = jnp.exp(dot_nt(qaug[here, :], kaug[keys, :]) + bias[:, cols])
                ds = p * dot_nt(doaug[here, :], vaug[keys, :])
                ds_low = ds.astype(BF16)
                dvt[feat, keys] += dot_nn(do_t, p.astype(BF16))
                dkt[feat, keys] += dot_nn(q_t, ds_low)
                dq = dq + dot_nn(ds_low, k_ref[keys, :])
                if b == 0:
                    dsum[:, cols] = ds
                else:
                    dsum[:, cols] += ds
            dq = (dq * (HD**-0.5)).astype(BF16)
            if h == 0:
                dq_ref[here, :] = dq
            else:
                dq_ref[here, :] = jnp.where(mine_q[:QB], dq, dq_ref[here, :])
        left, half = dsum[...], QB // 2
        while half:
            left = left[:half] + pltpu.roll(left[half:], width - half, 1)
            half //= 2
        dd_ref[0, h : h + 1, :] = left
    dk_ref[...] = dkt[...].T.astype(BF16)
    dv_ref[...] = dvt[...].T.astype(BF16)


def column_block(rows):
    return pl.BlockSpec((rows, PAIR), lambda i: (0, i))


def whole_block(rows):
    return pl.BlockSpec((rows, PAIR), lambda i: (0, 0))


def attention_fwd(base, q, qx, k, kx, v):
    rows, width, window = q.shape[0], base.shape[-1], k.shape[0]
    return pl.pallas_call(
        attention_fwd_kernel,
        grid=(H // 2,),
        in_specs=[
            pl.BlockSpec((1, 2, width), lambda i: (i, 0, 0)),
            column_block(rows),
            whole_block(rows),
            column_block(window),
            whole_block(window),
            column_block(window),
        ],
        out_specs=[column_block(rows), column_block(rows)],
        out_shape=[jax.ShapeDtypeStruct(q.shape, BF16), jax.ShapeDtypeStruct(q.shape, F32)],
        scratch_shapes=[
            pltpu.VMEM((QB, width), F32),
            pltpu.VMEM((window, PAIR), BF16),
            pltpu.VMEM((window, PAIR), BF16),
            pltpu.VMEM((QB, width), F32),
        ],
        compiler_params=pltpu.CompilerParams(vmem_limit_bytes=VMEM_LIMIT),
        name="attention_fwd",
    )(base, q, qx, k, kx, v)


def attention_bwd(base, q, qx, k, kx, v, att, lse, do):
    rows, width, window = q.shape[0], base.shape[-1], k.shape[0]
    return pl.pallas_call(
        attention_bwd_kernel,
        grid=(H // 2,),
        in_specs=[
            pl.BlockSpec((1, 2, width), lambda i: (i, 0, 0)),
            column_block(rows),
            whole_block(rows),
            column_block(window),
            whole_block(window),
            column_block(window),
            column_block(rows),
            column_block(rows),
            column_block(rows),
        ],
        out_specs=[
            column_block(rows),
            column_block(window),
            column_block(window),
            pl.BlockSpec((1, 2, width), lambda i: (i, 0, 0)),
        ],
        out_shape=[
            jax.ShapeDtypeStruct(q.shape, BF16),
            jax.ShapeDtypeStruct(k.shape, BF16),
            jax.ShapeDtypeStruct(k.shape, BF16),
            jax.ShapeDtypeStruct(base.shape, F32),
        ],
        scratch_shapes=[
            pltpu.VMEM((QB, width), F32),
            pltpu.VMEM((window, PAIR), BF16),
            pltpu.VMEM((window, PAIR), BF16),
            pltpu.VMEM((rows, PAIR), BF16),
            pltpu.VMEM((rows, PAIR), BF16),
            pltpu.VMEM((QB, width), F32),
            pltpu.VMEM((PAIR, window), F32),
            pltpu.VMEM((PAIR, window), F32),
        ],
        compiler_params=pltpu.CompilerParams(vmem_limit_bytes=VMEM_LIMIT),
        name="attention_bwd",
    )(base, q, qx, k, kx, v, att, lse, do)


def copy_kernel(deal_ref, *refs):
    count = len(refs) // 2
    for i in range(count):
        refs[count + i][...] = refs[i][...]


def to_slots(deal_row, arrays):
    groups, length, width = arrays[0].shape
    spec_in = pl.BlockSpec((1, length, width), lambda g, deal: (g, 0, 0))
    spec_out = pl.BlockSpec((1, length, width), lambda g, deal: (deal[g], 0, 0))
    return pl.pallas_call(
        copy_kernel,
        grid_spec=pltpu.PrefetchScalarGridSpec(
            num_scalar_prefetch=1, grid=(groups,), in_specs=[spec_in] * len(arrays), out_specs=[spec_out] * len(arrays)
        ),
        out_shape=[jax.ShapeDtypeStruct(a.shape, a.dtype) for a in arrays],
        name="to_slots",
    )(deal_row, *arrays)


def from_slots(deal_row, arrays):
    groups, length, width = arrays[0].shape
    spec_out = pl.BlockSpec((1, length, width), lambda g, deal: (g, 0, 0))
    spec_in = pl.BlockSpec((1, length, width), lambda g, deal: (deal[g], 0, 0))
    return pl.pallas_call(
        copy_kernel,
        grid_spec=pltpu.PrefetchScalarGridSpec(
            num_scalar_prefetch=1, grid=(groups,), in_specs=[spec_in] * len(arrays), out_specs=[spec_out] * len(arrays)
        ),
        out_shape=[jax.ShapeDtypeStruct(a.shape, a.dtype) for a in arrays],
        name="from_slots",
    )(deal_row, *arrays)


def swap_slots(values):
    return lax.all_to_all(values, "dp", split_axis=0, concat_axis=0, tiled=True)


def shards(
    tokens,
    cotangent,
    deal,
    lengths,
    buckets,
    ln1_gain,
    ln1_bias,
    w_qkv,
    w_out,
    rel_bias,
    ln2_gain,
    ln2_bias,
    w_up,
    w_down,
):
    groups = lax.axis_size("dp")
    splits = lax.axis_size("seq")
    tok_dev, width = tokens.shape
    block_len = tok_dev // groups
    maxlen = buckets.shape[0]
    back = -(-maxlen // tok_dev)
    window = (back + 1) * tok_dev
    span = back * tok_dev + QB
    chunk = lax.axis_index("seq")
    deal_row = deal[0]
    shard_rows = ln1_gain.shape[0]

    small = jnp.concatenate([ln1_gain, ln1_bias, ln2_gain, ln2_bias, rel_bias.reshape(-1)])
    wqkv_full = lax.all_gather(w_qkv, "dp", axis=0, tiled=True)
    small_full = lax.all_gather(small, "dp", axis=0, tiled=False)
    wout_full = lax.all_gather(w_out, "dp", axis=0, tiled=True)
    wup_full = lax.all_gather(w_up, "dp", axis=0, tiled=True)
    wdown_full = lax.all_gather(w_down, "dp", axis=0, tiled=True)
    gains = small_full[:, : 4 * shard_rows].reshape(groups, 4, shard_rows).transpose(1, 0, 2).reshape(4, width)
    gain_one, bias_one, gain_two, bias_two = (gains[i].astype(F32) for i in range(4))
    rel_full = small_full[:, 4 * shard_rows :].reshape(NBK, H)

    pieces = (groups, block_len, width)
    slot_in, slot_grad = to_slots(deal_row, [tokens.reshape(pieces), cotangent.reshape(pieces)])
    dealt = swap_slots(jnp.stack([slot_in, slot_grad], axis=1))
    x_rows = dealt[:, 0].reshape(tok_dev, width).astype(F32)
    grad_out = dealt[:, 1].reshape(tok_dev, width)

    ends, so_far = [], 0
    for c in range(lengths.shape[1]):
        so_far = so_far + lengths[0, c]
        ends.append(so_far)
    lane = lax.rem(jnp.arange(PAIR, dtype=jnp.int32), HD)[None, :]
    key_pos = (chunk - back) * tok_dev + jnp.arange(window, dtype=jnp.int32)
    key_seg = sum((key_pos >= e).astype(jnp.int32) for e in ends)
    key_seg = jnp.where(key_pos < 0, len(ends), key_seg)[:, None]
    query_seg = key_seg[back * tok_dev :]
    kx = jnp.where((lane == key_seg) | (lane >= HD - 3), 1.0, 0.0).astype(BF16)
    qx = jnp.where((lane <= len(ends)) & (lane != query_seg), BIG, 0.0).astype(BF16)
    offset = jnp.arange(span, dtype=jnp.int32)
    distance = back * tok_dev - offset
    in_reach = (distance >= 0) & (distance < maxlen)
    table_bucket = jnp.concatenate(
        [jnp.zeros((back * tok_dev + 1 - maxlen,), jnp.int32), buckets[::-1], jnp.zeros((QB - 1,), jnp.int32)]
    )
    one_hot = ((table_bucket[:, None] == jnp.arange(NBK, dtype=jnp.int32)[None, :]) & in_reach[:, None]).astype(F32)
    base = jnp.einsum("cb,bh->hc", one_hot, rel_full.astype(F32), precision=lax.Precision.HIGHEST)
    base = jnp.where(in_reach[None], base, BIG).reshape(H // 2, 2, span)

    normed, norm_one_back = jax.vjp(norm_rows, x_rows, gain_one, bias_one)
    normed_low = normed.astype(BF16)
    earlier = [
        lax.ppermute(normed_low, "seq", [(i, i + step) for i in range(splits - step)]) for step in range(back, 0, -1)
    ]
    scale = HD**-0.5
    own_qkv = jnp.dot(normed_low, wqkv_full, preferred_element_type=F32).astype(BF16)
    rows_before = jnp.concatenate(earlier, axis=0)
    kv_before = jnp.dot(rows_before, wqkv_full[:, width:], preferred_element_type=F32).astype(BF16)
    queries = own_qkv[:, :width] * jnp.asarray(scale, BF16)
    keys_all = jnp.concatenate([kv_before[:, :width], own_qkv[:, width : 2 * width]], axis=0)
    values_all = jnp.concatenate([kv_before[:, width:], own_qkv[:, 2 * width :]], axis=0)
    attended, lse = attention_fwd(base, queries, qx, keys_all, kx, values_all)
    residual = x_rows + jnp.dot(attended, wout_full, preferred_element_type=F32)
    normed_two, norm_two_back = jax.vjp(norm_rows, residual, gain_two, bias_two)
    normed_two_low = normed_two.astype(BF16)
    pre_act = jnp.dot(normed_two_low, wup_full, preferred_element_type=F32)
    active, gelu_back = jax.vjp(gelu_exact, pre_act)
    active_low = active.astype(BF16)
    output_rows = (residual + jnp.dot(active_low, wdown_full, preferred_element_type=F32)).astype(BF16)

    grad_wdown = jnp.einsum("tf,td->fd", active_low, grad_out, preferred_element_type=F32)
    grad_active = jnp.einsum("td,fd->tf", grad_out, wdown_full, preferred_element_type=F32)
    grad_pre = gelu_back(grad_active)[0].astype(BF16)
    grad_wup = jnp.einsum("td,tf->df", normed_two_low, grad_pre, preferred_element_type=F32)
    grad_norm_two = jnp.einsum("tf,df->td", grad_pre, wup_full, preferred_element_type=F32)
    resid_part, grad_gain_two, grad_bias_two = norm_two_back(grad_norm_two)
    grad_resid = grad_out.astype(F32) + resid_part
    branch_grad = grad_resid.astype(BF16)
    grad_wout = jnp.einsum("td,te->de", attended, branch_grad, preferred_element_type=F32)
    grad_att = jnp.einsum("te,de->td", branch_grad, wout_full, preferred_element_type=F32).astype(BF16)
    dq, dk, dv, dd = attention_bwd(base, queries, qx, keys_all, kx, values_all, attended, lse, grad_att)
    grad_kv = jnp.concatenate([dk, dv], axis=1)
    part_before = jnp.einsum(
        "tc,dc->td", grad_kv[: back * tok_dev], wqkv_full[:, width:], preferred_element_type=F32
    ).astype(BF16)
    returned = [
        lax.ppermute(
            part_before[(back - step) * tok_dev : (back - step + 1) * tok_dev],
            "seq",
            [(i + step, i) for i in range(splits - step)],
        )
        for step in range(back, 0, -1)
    ]
    grad_own = jnp.concatenate([dq, grad_kv[back * tok_dev :]], axis=1)
    grad_normed = jnp.einsum("tc,dc->td", grad_own, wqkv_full, preferred_element_type=F32)
    all_rows = jnp.concatenate([rows_before, normed_low], axis=0)
    grad_wq = jnp.einsum("td,tc->dc", normed_low, dq, preferred_element_type=F32)
    grad_wkv = jnp.einsum("td,tc->dc", all_rows, grad_kv, preferred_element_type=F32)
    grad_wqkv = jnp.concatenate([grad_wq, grad_wkv], axis=1)
    for part in returned:
        grad_normed = grad_normed + part.astype(F32)
    x_part, grad_gain_one, grad_bias_one = norm_one_back(grad_normed)
    grad_x = (grad_resid + x_part).astype(BF16)
    grad_rel = jnp.einsum(
        "cb,hc->bh", one_hot, dd.reshape(H, span), precision=lax.Precision.HIGHEST
    )

    def total(values):
        part = lax.psum_scatter(values.astype(BF16), "dp", scatter_dimension=0, tiled=True)
        return lax.psum(part, "seq").astype(F32)

    total_down = total(grad_wdown)
    total_up = total(grad_wup)
    total_out = total(grad_wout)
    total_qkv = total(grad_wqkv)
    small_grads = jnp.concatenate(
        [
            g.reshape(groups, -1)
            for g in (grad_gain_one, grad_bias_one, grad_gain_two, grad_bias_two, grad_rel)
        ],
        axis=1,
    )
    small_total = lax.psum(lax.psum_scatter(small_grads, "dp", scatter_dimension=0, tiled=True), "seq")[0]
    cut = [small_total[i * shard_rows : (i + 1) * shard_rows] for i in range(4)]
    total_rel = small_total[4 * shard_rows :].reshape(rel_bias.shape)

    returned_both = swap_slots(jnp.stack([output_rows.reshape(pieces), grad_x.reshape(pieces)], axis=1))
    output, grad_tokens = from_slots(deal_row, [returned_both[:, 0], returned_both[:, 1]])
    return (
        output.reshape(tok_dev, width),
        grad_tokens.reshape(tok_dev, width),
        cut[0],
        cut[1],
        total_qkv,
        total_out,
        total_rel,
        cut[2],
        cut[3],
        total_up,
        total_down,
    )


def solution(mesh):
    by_all, by_dp = P(("seq", "dp"), None), P("dp", None)
    return jax.shard_map(
        shards,
        mesh=mesh,
        in_specs=(
            by_all, by_all, by_all, by_dp, P(), P("dp"), P("dp"), by_dp, by_dp, by_dp, P("dp"), P("dp"), by_dp, by_dp,
        ),
        out_specs=(by_all, by_all, P("dp"), P("dp"), by_dp, by_dp, by_dp, P("dp"), P("dp"), by_dp, by_dp),
        check_vma=False,
    )
```

time: 1500 us -> 383 us (0.26)
  other arithmetic: 638 us -> 19.7 us
  matrix products: 492 us -> 52.2 us
  local copies, waits for them, and re-layouts: 69.3 us -> 15.9 us
  Pallas kernels: 0 us -> 53.3 us
  blocking collectives: 94.6 us -> 69.9 us
  loops' own time: 18.1 us -> 0 us
    dot_general x38 -> x16, matrix products: 485 us -> 47.9 us  [the longest x1 13.4 us: shards(): pre_act = jnp.dot(normed_two_low, wup_full, preferred_element_type=F32)]
    reduce_sum x15 -> x0, other arithmetic: 229 us -> none  [the longest x8 209 us: backward_block(): jnp.sum(jnp.where((distance >= thresholds[level])[None], grad_wide, 0.0),...]
    and x10 -> x1, other arithmetic: 204 us -> 0.01 us  [shards(): in_reach = (distance >= 0) & (distance < maxlen)]
    ge x8 -> x1, other arithmetic: 176 us -> 0.01 us  [shards(): kx = jnp.where((lane == key_seg) | (lane >= HD - 3), 1.0, 0.0).astype(BF16)]
    pallas_call x0 -> x4, Pallas kernels: none -> 53.3 us  [the longest x1 28.4 us: attention_bwd(): pl.pallas_call(attention_bwd_kernel, grid=(H // 2,), in_specs=[pl.BlockSp...]
    reduce_scatter x5 -> x4, waiting for transfers between devices: 45.8 us -> 92.9 us  [total(): lax.psum_scatter(values.astype(BF16), 'dp', scatter_dimension=0, tiled=True)]
    all_gather x4 -> x3, waiting for transfers between devices: 38.5 us -> 0.02 us  [the longest x1 0.02 us: shards(): wup_full = lax.all_gather(w_up, 'dp', axis=0, tiled=True)]
    all_gather x4 -> x1, blocking collectives: 45.4 us -> 10 us  [shards(): wout_full = lax.all_gather(w_out, 'dp', axis=0, tiled=True)]
  transfers between devices with their start and end apart: 16 -> 14, of which waited for: 8 -> 8; matrix products, arithmetic and copies ran while one was open for 78% -> 18% of each run, Pallas kernels for 0% -> 14%
where the time goes in v1:
time: 383 us; the launch traced here: 381 us
  waiting for transfers between devices  132 us (34%)
  blocking collectives  69.9 us (18%)
  Pallas kernels  53.3 us (14%)
  matrix products  52.2 us (14%)
  starting transfers between devices  21 us (5%)
  other arithmetic  19.7 us (5%)
  between operations  17.4 us (5%)
  local copies, waits for them, and re-layouts  15.9 us (4%)
    reduce_scatter x4, waiting for transfers between devices, total(): lax.psum_scatter(values.astype(BF16), 'dp', scatter_dimension=0, tiled=True)  92.9 us
    unnamed x2, blocking collectives  47.8 us
    pallas_call x1, Pallas kernels, attention_bwd(): pl.pallas_call(attention_bwd_kernel, grid=(H // 2,), in_specs=[pl.BlockSp...  28.4 us
    ppermute x2, waiting for transfers between devices, shards(): lax.ppermute(part_before[(back - step) * tok_dev:(back - step + 1) * tok_...  22.2 us
    dot_general x1, matrix products, shards(): pre_act = jnp.dot(normed_two_low, wup_full, preferred_element_type=F32)  13.4 us
    pallas_call x1, Pallas kernels, attention_fwd(): pl.pallas_call(attention_fwd_kernel, grid=(H // 2,), in_specs=[pl.BlockSp...  13.3 us
    ppermute x2, waiting for transfers between devices, shards(): lax.ppermute(normed_low, 'seq', [(i, i + step) for i in range(splits - st...  12.9 us
    psum x1, blocking collectives, shards(): lax.psum(lax.psum_scatter(small_grads, 'dp', scatter_dimension=0, tiled=T...  12.1 us
  transfers between devices with their start and end apart: 14, of which 8 were waited for; matrix products, arithmetic and copies ran while one was open for 18% of the time, Pallas kernels for 14%

profile of v1, /device:TPU:0, one launch (start us, length us, event | category | flops | bytes accessed | tf_op | source)
XLA Modules:
  0.0 381.1 jit_solution(7013752987559384127)
XLA Ops:
  8.8 5.9 %to_slots.1 = (bf16[8,64,512]{2,1,0:T(8,128)(2,1)}, bf16[8,64,512]{2,1,0:T(8,128)(2,1)}) custom-call(s32[8]{0:T(128)} %bitcast.86, bf16[8,64,512]{2,1,0:T(8,128)(2,1)} %bitcast.80, bf16[8,64,512]{2,1,0:T(8,128)(2,1)} %bitcast.81), custom_call_target="tpu_custom_call" | custom-call | tf_op jit(solution)/shard_map/to_slots/pallas_call | solution.py:242
  14.6 1.3 pad_maximum_fusion.3
  17.0 5.2 %all-to-all-start = ((bf16[8,2,64,512]{3,2,1,0:T(8,128)(2,1)}), bf16[8,2,64,512]{3,2,1,0:T(8,128)(2,1)S(1)}, u32[]{:S(2)}, u32[]{:S(2)}) async-start(bf16[8,2,64,512]{3,2,1,0:T(8,128)(2,1)} %copy.28), calls=%async_computation | async-start | bytes 2097152 | tf_op jit(solution)/shard_map/all_to_all | solution.py:267
  24.7 23.9 %all-reduce = bf16[2304]{0:T(1024)(128)(2,1)S(1)} all-reduce(bf16[2304]{0:T(1024)(128)(2,1)S(1)} %dynamic-update-slice), channel_id=2, replica_groups=mesh['seq'=4,'dp'=8] {'dp'}, use_global_device_ids=true, to_apply=%add | all-reduce | flops 2304 | bytes 9216
  53.8 10.0 %all_gather.21 = bf16[512,512]{1,0:T(8,128)(2,1)S(1)} all-gather(bf16[64,512]{1,0:T(8,128)(2,1)S(1)} %copy-done.12), channel_id=1, replica_groups=mesh['seq'=4,'dp'=8] {'dp'}, dimensions={0}, use_global_device_ids=true | all-gather | bytes 589824 | tf_op jit(solution)/shard_map/all_gather | solution.py:301
  66.6 4.3 %collective-permute-start.1 = (bf16[512,512]{1,0:T(8,128)(2,1)S(1)}, bf16[512,512]{1,0:T(8,128)(2,1)}, u32[]{:S(2)}, u32[]{:S(2)}) collective-permute-start(bf16[512,512]{1,0:T(8,128)(2,1)S(1)} %add_convert_fusion.3), channel_id=1, source_target_pairs={{0,8},{8,16},{16,24},{1,9},{9,17},{17,25},{2,10},{10,18},{18,26},{... | collective-permute-start | bytes 1572872 | tf_op jit(solution)/shard_map/ppermute | solution.py:338
  70.9 4.5 %collective-permute-start = (bf16[512,512]{1,0:T(8,128)(2,1)S(1)}, bf16[512,512]{1,0:T(8,128)(2,1)}, u32[]{:S(2)}, u32[]{:S(2)}) collective-permute-start(bf16[512,512]{1,0:T(8,128)(2,1)S(1)} %add_convert_fusion.3), channel_id=1, source_target_pairs={{0,16},{8,24},{1,17},{9,25},{2,18},{10,26},{3,19},{11,27},{4,20},{... | collective-permute-start | bytes 1572872 | tf_op jit(solution)/shard_map/ppermute | solution.py:338
  76.6 2.6 convolution_convert_fusion
  80.1 2.2 collective-permute-done.1
  82.3 10.7 %collective-permute-done = bf16[512,512]{1,0:T(8,128)(2,1)} collective-permute-done((bf16[512,512]{1,0:T(8,128)(2,1)S(1)}, bf16[512,512]{1,0:T(8,128)(2,1)}, u32[]{:S(2)}, u32[]{:S(2)}) %collective-permute-start) | collective-permute-done | bytes 524320 | tf_op jit(solution)/shard_map/ppermute | solution.py:338
  93.1 2.5 convolution_convert_fusion.3
  95.7 1.9 pad_maximum_fusion
  97.6 13.3 %attention_fwd.1 = (bf16[512,512]{1,0:T(8,128)(2,1)}, f32[512,512]{1,0:T(8,128)}) custom-call(f32[4,2,1280]{2,1,0:T(2,128)} %reshape.248.base_ref, bf16[512,512]{1,0:T(8,128)(2,1)} %get-tuple-element.54.q_ref, bf16[512,128]{1,0:T(8,128)(2,1)} %select_convert_fusion.1.qx_ref, bf16[1536,512]{1,0:T(8,128)(2,1)} %get-tuple-element.75.k_ref, ...), custom_call_target="tpu_custom_call" | custom-call | tf_op jit(solution)/shard_map/attention_fwd/pallas_call | solution.py:165
  110.9 1.9 fusion.67
  113.1 13.4 %multiply_convert_fusion = (bf16[512,2048]{1,0:T(8,128)(2,1)}, f32[512,2048]{1,0:T(8,128)}, f32[512,2048]{1,0:T(8,128)}) fusion(bf16[512,2048]{1,0:T(8,128)(2,1)} %all-gather.7.cloned.1.call-done, f32[512,512]{1,0:T(8,128)S(1)} %get-tuple-element.71, f32[512]{0:T(512)S(1)} %reshape.263, f32[512]{0:T(512)S(1)} %reshape.262, f32[512]{0:T(512)S(1)} %fusion.51, ...), kind=kOutput, calls=%fused_computation.3 | convolution fusion | flops 1143209984 | bytes 13639680 | tf_op jit(solution)/shard_map/dot_general | solution.py:351
  126.5 6.4 %add_convert_fusion = bf16[512,2048]{1,0:T(8,128)(2,1)S(1)} fusion(f32[512,2048]{1,0:T(8,128)} %get-tuple-element.47, f32[512,2048]{1,0:T(8,128)} %get-tuple-element.72, bf16[512,512]{1,0:T(8,128)(2,1)S(1)} %bitcast.76, bf16[2048,512]{1,0:T(8,128)(2,1)} %all-gather.9.cloned.1.call-done), kind=kOutput, calls=%fused_computation.2 | convolution fusion | flops 1088421888 | bytes 13107200 | tf_op jit(solution)/shard_map/td,fd->tf/dot_general | solution.py:357
  133.0 1.6 multiply_reduce_fusion
  135.6 1.3 convolution_convert_fusion.6.do_ref
  136.9 1.3 convolution_convert_fusion.4
  138.2 28.4 %attention_bwd.1 = (bf16[512,512]{1,0:T(8,128)(2,1)}, bf16[1536,512]{1,0:T(8,128)(2,1)}, bf16[1536,512]{1,0:T(8,128)(2,1)}, f32[4,2,1280]{2,1,0:T(2,128)}) custom-call(f32[4,2,1280]{2,1,0:T(2,128)} %reshape.248.base_ref, bf16[512,512]{1,0:T(8,128)(2,1)} %get-tuple-element.54.q_ref, bf16[512,128]{1,0:T(8,128)(2,1)} %select_convert_fusion.1.qx_ref, ...), custom_call_target="tpu_custom_call" | custom-call | tf_op jit(solution)/shard_map/attention_bwd/pallas_call | solution.py:191
  166.6 2.9 constant_dynamic-update-slice_fusion.1
  169.5 1.4 constant_dynamic-update-slice_fusion
  170.9 1.3 convolution_convert_fusion.5
  172.2 2.0 copy.34
  174.2 4.3 %fusion.18 = bf16[512,1024]{1,0:T(8,128)(2,1)S(1)} fusion(bf16[1536,1024]{1,0:T(8,128)(2,1)} %constant_dynamic-update-slice_fusion, bf16[512,512]{1,0:T(8,128)(2,1)} %copy-done.5, bf16[512,512]{1,0:T(8,128)(2,1)} %collective-permute-done.1, bf16[512,512]{1,0:T(8,128)(2,1)} %collective-permute-done), kind=kOutput, calls=%fused_computation.39 | convolution fusion | flops 1615855616 | bytes 5767168 | tf_op jit(solution)/shard_map/td,tc->dc/dot_general | solution.py:383
  178.5 1.2 pad_maximum_fusion.2
  179.8 4.3 %convolution_convert_fusion.1 = bf16[2048,512]{1,0:T(8,128)(2,1)} fusion(bf16[512,2048]{1,0:T(8,128)(2,1)} %get-tuple-element.46, bf16[512,512]{1,0:T(8,128)(2,1)} %bitcast.77), kind=kOutput, calls=%fused_computation.18 | convolution fusion | flops 1074790400 | bytes 4718592 | tf_op jit(solution)/shard_map/tf,td->fd/dot_general | solution.py:356
  184.2 4.3 %convolution_convert_fusion.2 = bf16[512,2048]{1,0:T(8,128)(2,1)} fusion(bf16[512,2048]{1,0:T(8,128)(2,1)} %copy-done.26, f32[512,512]{1,0:T(8,128)S(1)} %get-tuple-element.71, f32[512]{0:T(512)S(1)} %reshape.263, f32[512]{0:T(512)S(1)} %reshape.262, f32[512]{0:T(512)S(1)} %fusion.51, f32[512]{0:T(512)S(1)} %broadcast_multiply_fusion.1), kind=kOutput, calls=%fused_computation.19 | convolution fusion | flops 1076101120 | bytes 5251072 | tf_op jit(solution)/shard_map/td,tf->df/dot_general | solution.py:359
  188.6 3.1 fusion.21
  191.8 1.6 collective-permute-start.2
  193.4 1.6 collective-permute-start.3
  195.0 1.3 slice.154
  196.3 1.3 fusion.24
  197.6 10.9 %collective-permute-done.2 = bf16[512,512]{1,0:T(8,128)(2,1)S(1)} collective-permute-done((bf16[512,512]{1,0:T(8,128)(2,1)S(1)}, bf16[512,512]{1,0:T(8,128)(2,1)S(1)}, u32[]{:S(2)}, u32[]{:S(2)}) %collective-permute-start.2) | collective-permute-done | bytes 524320 | tf_op jit(solution)/shard_map/ppermute | solution.py:372
  208.5 11.3 %collective-permute-done.3 = bf16[512,512]{1,0:T(8,128)(2,1)S(1)} collective-permute-done((bf16[512,512]{1,0:T(8,128)(2,1)S(1)}, bf16[512,512]{1,0:T(8,128)(2,1)S(1)}, u32[]{:S(2)}, u32[]{:S(2)}) %collective-permute-start.3) | collective-permute-done | bytes 524320 | tf_op jit(solution)/shard_map/ppermute | solution.py:372
  219.8 1.3 fusion.59
  223.3 3.6 all-to-all-start.1
  227.0 3.7 reduce-scatter.5.cloned.1.call-done
  230.7 44.7 %reduce-scatter.11.cloned.1.call-done = bf16[256,512]{1,0:T(8,128)(2,1)} async-done(((bf16[2048,512]{1,0:T(8,128)(2,1)}), bf16[256,512]{1,0:T(8,128)(2,1)}) %reduce-scatter.11.cloned.1.call-update) | async-done | bytes 262160 | tf_op jit(solution)/shard_map/reduce_scatter | solution.py:394
  275.4 44.5 %reduce-scatter.9.cloned.1.call-done = bf16[64,2048]{1,0:T(8,128)(2,1)} async-done(((bf16[512,2048]{1,0:T(8,128)(2,1)}), bf16[64,2048]{1,0:T(8,128)(2,1)}) %reduce-scatter.9.cloned.1.call-update) | async-done | bytes 262160 | tf_op jit(solution)/shard_map/reduce_scatter | solution.py:394
  321.3 23.9 %all-reduce.1 = f32[8,288]{1,0:T(8,128)S(1)} all-reduce(f32[8,288]{1,0:T(8,128)S(1)} %concatenate.39), channel_id=3, replica_groups=mesh['seq'=4,'dp'=8] {'dp'}, use_global_device_ids=true, to_apply=%region_12.13.clone | all-reduce | flops 2304 | bytes 18432
  345.8 12.1 %psum.35 = f32[1,288]{1,0:T(1,128)S(1)} all-reduce(f32[1,288]{1,0:T(1,128)S(1)} %constant_dynamic-slice_fusion), channel_id=1, replica_groups=mesh['seq'=4,'dp'=8] {'seq'}, use_global_device_ids=true, to_apply=%region_13.14 | all-reduce | flops 288 | bytes 2304 | tf_op jit(solution)/shard_map/psum | solution.py:408
  360.3 5.7 %from_slots.1 = (bf16[8,64,512]{2,1,0:T(8,128)(2,1)}, bf16[8,64,512]{2,1,0:T(8,128)(2,1)}) custom-call(s32[8]{0:T(128)} %bitcast.87, bf16[8,64,512]{2,1,0:T(8,128)(2,1)} %get-tuple-element.56.refs_0_, bf16[8,64,512]{2,1,0:T(8,128)(2,1)} %get-tuple-element.55.refs_1_), custom_call_target="tpu_custom_call" | custom-call | tf_op jit(solution)/shard_map/from_slots/pallas_call | solution.py:256
  366.0 1.5 all-reduce.5.cloned.1.call-done
  367.4 1.5 convert_element_type.175
  369.0 1.7 convert_element_type.173
  370.7 1.8 convert_element_type.177
  372.4 1.8 convert_element_type.179
  (145 shorter events, 20.8 us)
Async XLA Ops:
  7.2 15.9 %copy-start.16 = (u32[32]{0:T(128)S(1)}, u32[32]{0:T(128)}, u32[]{:S(2)}) copy-start(u32[32]{0:T(128)} %constant.117) | copy-start | bytes 388
  7.2 15.8 %copy-start.25 = (bf16[4,8]{1,0:T(4,128)(2,1)S(1)}, bf16[4,8]{1,0:T(4,128)(2,1)}, u32[]{:S(2)}) copy-start(bf16[4,8]{1,0:T(4,128)(2,1)} %param.23) | copy-start | bytes 196
  7.2 17.1 %copy-start.20 = (bf16[64]{0:T(256)(128)(2,1)S(1)}, bf16[64]{0:T(256)(128)(2,1)}, u32[]{:S(2)}) copy-start(bf16[64]{0:T(256)(128)(2,1)} %param.25) | copy-start | bytes 388
  7.2 17.1 %copy-start.19 = (bf16[64]{0:T(256)(128)(2,1)S(1)}, bf16[64]{0:T(256)(128)(2,1)}, u32[]{:S(2)}) copy-start(bf16[64]{0:T(256)(128)(2,1)} %param.24) | copy-start | bytes 388
  7.2 17.1 %copy-start.18 = (bf16[64]{0:T(256)(128)(2,1)S(1)}, bf16[64]{0:T(256)(128)(2,1)}, u32[]{:S(2)}) copy-start(bf16[64]{0:T(256)(128)(2,1)} %param.20) | copy-start | bytes 388
  7.2 17.1 %copy-start.17 = (bf16[64]{0:T(256)(128)(2,1)S(1)}, bf16[64]{0:T(256)(128)(2,1)}, u32[]{:S(2)}) copy-start(bf16[64]{0:T(256)(128)(2,1)} %param.19) | copy-start | bytes 388
  7.2 41.5 %copy-start.14 = (s32[1,3]{1,0:T(1,128)S(1)}, s32[1,3]{1,0:T(1,128)}, u32[]{:S(2)}) copy-start(s32[1,3]{1,0:T(1,128)} %param.17) | copy-start | bytes 40
  7.3 42.0 %copy-start.15 = (s32[1024]{0:T(1024)S(1)}, s32[1024]{0:T(1024)}, u32[]{:S(2)}) copy-start(s32[1024]{0:T(1024)} %param.18) | copy-start | bytes 12292
  7.3 69.3 %all-gather.5.cloned.1.call-start = ((), (), s32[]{:S(2)}) async-start(), calls=%async_computation.6 | async-start | bytes 1769472 | tf_op jit(solution)/shard_map/all_gather | solution.py:299
  8.0 105.1 %all-gather.7.cloned.1.call-start = ((), (), s32[]{:S(2)}) async-start(), calls=%async_computation.7 | async-start | bytes 2359296 | tf_op jit(solution)/shard_map/all_gather | solution.py:302
  8.7 45.1 %copy-start.12 = (bf16[64,512]{1,0:T(8,128)(2,1)S(1)}, bf16[64,512]{1,0:T(8,128)(2,1)}, u32[]{:S(2)}) copy-start(bf16[64,512]{1,0:T(8,128)(2,1)} %param.22) | copy-start | bytes 196612
  17.0 48.7 %all-to-all-start = ((bf16[8,2,64,512]{3,2,1,0:T(8,128)(2,1)}), bf16[8,2,64,512]{3,2,1,0:T(8,128)(2,1)S(1)}, u32[]{:S(2)}, u32[]{:S(2)}) async-start(bf16[8,2,64,512]{3,2,1,0:T(8,128)(2,1)} %copy.28), calls=%async_computation | async-start | bytes 2097152 | tf_op jit(solution)/shard_map/all_to_all | solution.py:267
  22.2 104.4 %all-gather.9.cloned.1.call-start = ((), (), s32[]{:S(2)}) async-start(), calls=%async_computation.8 | async-start | bytes 2359296 | tf_op jit(solution)/shard_map/all_gather | solution.py:303
  22.9 204.1 %reduce-scatter.7.cloned.1.call-start = ((), (), s32[]{:S(2)}) async-start(), calls=%async_computation.10 | async-start | bytes 589824 | tf_op jit(solution)/shard_map/reduce_scatter | solution.py:394
  63.8 47.0 %copy-start.3 = (bf16[512,512]{1,0:T(8,128)(2,1)}, bf16[512,512]{1,0:T(8,128)(2,1)S(1)}, u32[]{:S(2)}) copy-start(bf16[512,512]{1,0:T(8,128)(2,1)S(1)} %all_gather.21) | copy-start | bytes 1572868
  66.6 12.6 %copy-start.5 = (bf16[512,512]{1,0:T(8,128)(2,1)}, bf16[512,512]{1,0:T(8,128)(2,1)S(1)}, u32[]{:S(2)}) copy-start(bf16[512,512]{1,0:T(8,128)(2,1)S(1)} %add_convert_fusion.3) | copy-start | bytes 1572868
  66.6 15.7 %collective-permute-start.1 = (bf16[512,512]{1,0:T(8,128)(2,1)S(1)}, bf16[512,512]{1,0:T(8,128)(2,1)}, u32[]{:S(2)}, u32[]{:S(2)}) collective-permute-start(bf16[512,512]{1,0:T(8,128)(2,1)S(1)} %add_convert_fusion.3), channel_id=1, source_target_pairs={{0,8},{8,16},{16,24},{1,9},{9,17},{17,25},{2,10},{10,18},{18,26},{... | collective-permute-start | bytes 1572872 | tf_op jit(solution)/shard_map/ppermute | solution.py:338
  70.9 22.2 %collective-permute-start = (bf16[512,512]{1,0:T(8,128)(2,1)S(1)}, bf16[512,512]{1,0:T(8,128)(2,1)}, u32[]{:S(2)}, u32[]{:S(2)}) collective-permute-start(bf16[512,512]{1,0:T(8,128)(2,1)S(1)} %add_convert_fusion.3), channel_id=1, source_target_pairs={{0,16},{8,24},{1,17},{9,25},{2,18},{10,26},{3,19},{11,27},{4,20},{... | collective-permute-start | bytes 1572872 | tf_op jit(solution)/shard_map/ppermute | solution.py:338
  76.6 50.0 %copy-start = (bf16[8,1,64,512]{3,2,1,0:T(8,128)(2,1)}, bf16[8,1,64,512]{3,2,1,0:T(8,128)(2,1)S(1)}, u32[]{:S(2)}) copy-start(bf16[8,1,64,512]{3,2,1,0:T(8,128)(2,1)S(1)} %get-tuple-element.60) | copy-start | bytes 1572868
  76.6 16.5 %copy-start.23 = (bf16[512,1536]{1,0:T(8,128)(2,1)S(1)}, bf16[512,1536]{1,0:T(8,128)(2,1)}, u32[]{:S(2)}) copy-start(bf16[512,1536]{1,0:T(8,128)(2,1)} %all-gather.5.cloned.1.call-done) | copy-start | bytes 4718596
  126.5 6.4 %copy-start.22 = (bf16[512,2048]{1,0:T(8,128)(2,1)S(1)}, bf16[512,2048]{1,0:T(8,128)(2,1)}, u32[]{:S(2)}) copy-start(bf16[512,2048]{1,0:T(8,128)(2,1)} %all-gather.7.cloned.1.call-done) | copy-start | bytes 6291460
  133.0 1.6 copy-start.26
  133.0 2.1 copy-start.1
  134.6 1.0 copy-start.4
  134.6 2.3 copy-start.7
  138.2 92.5 %reduce-scatter.5.cloned.1.call-start = ((), (), s32[]{:S(2)}) async-start(), calls=%async_computation.9 | async-start | bytes 1769472 | tf_op jit(solution)/shard_map/reduce_scatter | solution.py:394
  166.6 2.9 copy-start.9
  166.6 4.3 %copy-start.6 = (bf16[512,512]{1,0:T(8,128)(2,1)S(1)}, bf16[512,512]{1,0:T(8,128)(2,1)}, u32[]{:S(2)}) copy-start(bf16[512,512]{1,0:T(8,128)(2,1)} %copy-done.5) | copy-start | bytes 1572868
  166.6 4.3 %copy-start.10 = (bf16[512,512]{1,0:T(8,128)(2,1)S(1)}, bf16[512,512]{1,0:T(8,128)(2,1)}, u32[]{:S(2)}) copy-start(bf16[512,512]{1,0:T(8,128)(2,1)} %get-tuple-element.25) | copy-start | bytes 1572868
  174.2 4.3 %copy-start.8 = (bf16[512,512]{1,0:T(8,128)(2,1)S(1)}, bf16[512,512]{1,0:T(8,128)(2,1)}, u32[]{:S(2)}) copy-start(bf16[512,512]{1,0:T(8,128)(2,1)} %copy.34) | copy-start | bytes 1572868
  179.8 95.6 %reduce-scatter.11.cloned.1.call-start = ((), (), s32[]{:S(2)}) async-start(), calls=%async_computation.12 | async-start | bytes 2359296 | tf_op jit(solution)/shard_map/reduce_scatter | solution.py:394
  184.2 135.7 %reduce-scatter.9.cloned.1.call-start = ((), (), s32[]{:S(2)}) async-start(), calls=%async_computation.11 | async-start | bytes 2359296 | tf_op jit(solution)/shard_map/reduce_scatter | solution.py:394
  191.7 4.5 %copy-start.21 = (bf16[2048,512]{1,0:T(8,128)(2,1)S(1)}, bf16[2048,512]{1,0:T(8,128)(2,1)}, u32[]{:S(2)}) copy-start(bf16[2048,512]{1,0:T(8,128)(2,1)} %all-gather.9.cloned.1.call-done) | copy-start | bytes 6291460
  191.7 4.5 %copy-start.27 = (bf16[512,2048]{1,0:T(8,128)(2,1)S(1)}, bf16[512,2048]{1,0:T(8,128)(2,1)}, u32[]{:S(2)}) copy-start(bf16[512,2048]{1,0:T(8,128)(2,1)} %get-tuple-element.46) | copy-start | bytes 6291460
  191.8 16.7 %collective-permute-start.2 = (bf16[512,512]{1,0:T(8,128)(2,1)S(1)}, bf16[512,512]{1,0:T(8,128)(2,1)S(1)}, u32[]{:S(2)}, u32[]{:S(2)}) collective-permute-start(bf16[512,512]{1,0:T(8,128)(2,1)S(1)} %get-tuple-element.57), channel_id=1, source_target_pairs={{16,0},{24,8},{17,1},{25,9},{18,2},{26,10},{19,3},{27,11},{20,4},{... | collective-permute-start | bytes 1572872 | tf_op jit(solution)/shard_map/ppermute | solution.py:372
  193.4 26.4 %collective-permute-start.3 = (bf16[512,512]{1,0:T(8,128)(2,1)S(1)}, bf16[512,512]{1,0:T(8,128)(2,1)S(1)}, u32[]{:S(2)}, u32[]{:S(2)}) collective-permute-start(bf16[512,512]{1,0:T(8,128)(2,1)S(1)} %get-tuple-element.58), channel_id=1, source_target_pairs={{8,0},{16,8},{24,16},{9,1},{17,9},{25,17},{10,2},{18,10},{26,18},{... | collective-permute-start | bytes 1572872 | tf_op jit(solution)/shard_map/ppermute | solution.py:372
  196.3 23.5 %copy-start.11 = (bf16[512,512]{1,0:T(8,128)(2,1)S(1)}, bf16[512,512]{1,0:T(8,128)(2,1)}, u32[]{:S(2)}) copy-start(bf16[512,512]{1,0:T(8,128)(2,1)} %get-tuple-element.25) | copy-start | bytes 1572868
  196.3 23.5 %copy-start.24 = (bf16[512,1536]{1,0:T(8,128)(2,1)S(1)}, bf16[512,1536]{1,0:T(8,128)(2,1)}, u32[]{:S(2)}) copy-start(bf16[512,1536]{1,0:T(8,128)(2,1)} %all-gather.5.cloned.1.call-done) | copy-start | bytes 4718596
  197.6 24.1 %copy-start.2 = (bf16[8,1,64,512]{3,2,1,0:T(8,128)(2,1)S(1)}, bf16[8,1,64,512]{3,2,1,0:T(8,128)(2,1)}, u32[]{:S(2)}) copy-start(bf16[8,1,64,512]{3,2,1,0:T(8,128)(2,1)} %copy-done) | copy-start | bytes 1572868
  221.7 5.3 %copy-start.13 = (f32[4,2,1280]{2,1,0:T(2,128)S(1)}, f32[4,2,1280]{2,1,0:T(2,128)}, u32[]{:S(2)}) copy-start(f32[4,2,1280]{2,1,0:T(2,128)} %get-tuple-element.30) | copy-start | bytes 122884
  223.3 135.9 %all-to-all-start.1 = ((bf16[8,2,64,512]{3,2,1,0:T(8,128)(2,1)}), bf16[8,2,64,512]{3,2,1,0:T(8,128)(2,1)S(1)}, u32[]{:S(2)}, u32[]{:S(2)}) async-start(bf16[8,2,64,512]{3,2,1,0:T(8,128)(2,1)} %pad_maximum_fusion.4), calls=%async_computation.1 | async-start | bytes 2097152 | tf_op jit(solution)/shard_map/all_to_all | solution.py:267
  226.9 140.5 %all-reduce.5.cloned.1.call-start = ((), (), s32[]{:S(2)}) async-start(), calls=%async_computation.13 | async-start | bytes 1572864 | tf_op jit(solution)/shard_map/psum | solution.py:395
Sparse Core Ops, SparseCore 0:
  10.0 32.4 all-gather.4
  44.3 28.6 all-gather.6
  74.9 27.8 all-gather.8
  138.3 46.4 reduce-scatter.6
  188.3 42.3 reduce-scatter.4
  234.2 41.1 reduce-scatter.10
  278.7 41.1 reduce-scatter.8
  322.7 44.6 all-reduce.4

commit v2 on v1

--- a/solution.py
+++ b/solution.py
@@ -249,18 +249,204 @@
     )(deal_row, *arrays)
 
 
-def from_slots(deal_row, arrays):
-    groups, length, width = arrays[0].shape
-    spec_out = pl.BlockSpec((1, length, width), lambda g, deal: (g, 0, 0))
-    spec_in = pl.BlockSpec((1, length, width), lambda g, deal: (deal[g], 0, 0))
+def add_low(first, *others):
+    total = first.astype(F32)
+    for other in others:
+        total = total + other.astype(F32)
+    return total
+
+
+class Summer:
+    def __init__(self, source, recv1, pair, recv2, mine, recv3, out, sems):
+        self.source, self.recv1, self.pair, self.recv2 = source, recv1, pair, recv2
+        self.mine, self.recv3, self.out, self.sems = mine, recv3, out, sems
+        self.dp, self.seq = lax.axis_index("dp"), lax.axis_index("seq")
+        self.pairs, self.splits = source.shape[0] // 2, lax.axis_size("seq")
+        self.core, self.chip = lax.rem(self.dp, 2), self.dp // 2
+        self.scatter = out.shape[1] < mine.shape[0]
+        self.sent = []
+        self.count = 0
+
+    def send(self, src, dst, device):
+        slot = self.count
+        self.count += 1
+        copy = pltpu.make_async_remote_copy(
+            src_ref=src, dst_ref=dst, send_sem=self.sems.at[0, slot], recv_sem=self.sems.at[1, slot],
+            device_id=device, device_id_type=pl.DeviceIdType.MESH,
+        )
+        copy.start()
+        self.sent.append(copy)
+        return copy
+
+    def stage1(self):
+        other = 1 - self.core
+        self.first = [
+            self.send(self.source.at[2 * k + other], self.recv1.at[k], {"dp": self.dp + 1 - 2 * self.core})
+            for k in range(self.pairs)
+        ]
+
+    def stage2(self):
+        self.second = []
+        for step in range(self.pairs):
+            k = lax.rem(self.chip + 1 + step, self.pairs)
+            if step == 0:
+                for copy in self.first:
+                    copy.wait_recv()
+            self.pair[k] = add_low(self.source[2 * k + self.core], self.recv1[k]).astype(self.pair.dtype)
+            if step < self.pairs - 1:
+                self.second.append(self.send(self.pair.at[k], self.recv2.at[step], {"dp": 2 * k + self.core}))
+
+    def stage3(self):
+        for copy in self.second:
+            copy.wait_recv()
+        total = add_low(self.pair[self.chip], *[self.recv2[step] for step in range(self.pairs - 1)])
+        self.mine[...] = total.astype(self.mine.dtype)
+        self.third = []
+        rows = self.out.shape[1]
+        for step in range(self.splits - 1):
+            t = lax.rem(self.seq + 1 + step, self.splits)
+            src = self.mine.at[pl.ds(pl.multiple_of(t * rows, rows), rows)] if self.scatter else self.mine
+            dst = self.recv3.at[step] if self.scatter else self.out.at[self.seq]
+            self.third.append(self.send(src, dst, {"seq": t}))
+        if not self.scatter:
+            self.out[self.seq] = self.mine[...]
+
+    def stage4(self):
+        for copy in self.third:
+            copy.wait_recv()
+        if not self.scatter:
+            return
+        rows = self.out.shape[1]
+        own = self.mine[pl.ds(pl.multiple_of(self.seq * rows, rows), rows)]
+        total = add_low(own, *[self.recv3[step] for step in range(self.splits - 1)])
+        self.out[self.seq] = total.astype(self.out.dtype)
+        self.fourth = [
+            self.send(self.out.at[self.seq], self.out.at[self.seq], {"seq": lax.rem(self.seq + 1 + step, self.splits)})
+            for step in range(self.splits - 1)
+        ]
+
+    def finish(self):
+        if self.scatter:
+            for copy in self.fourth:
+                copy.wait_recv()
+        for copy in self.sent:
+            copy.wait_send()
+
+
+def summer_shapes(shape, dtype, splits):
+    groups, rows, cols = shape
+    pairs = groups // 2
+    scatter = rows % (16 * splits) == 0
+    out = jax.ShapeDtypeStruct((splits, rows // splits if scatter else rows, cols), dtype)
+    copies = pairs + (pairs - 1) + (splits - 1) * (2 if scatter else 1)
+    scratch = [
+        pltpu.VMEM((pairs, rows, cols), dtype),
+        pltpu.VMEM((pairs, rows, cols), dtype),
+        pltpu.VMEM((pairs - 1, rows, cols), dtype),
+        pltpu.VMEM((rows, cols), dtype),
+        pltpu.VMEM((splits - 1, out.shape[1] if scatter else 16, cols), dtype),
+        pltpu.SemaphoreType.DMA((2, copies)),
+    ]
+    return out, scratch
+
+
+def greet(peers):
+    barrier = pltpu.get_barrier_semaphore()
+    for device in peers:
+        pl.semaphore_signal(barrier, inc=1, device_id=device, device_id_type=pl.DeviceIdType.MESH)
+    pl.semaphore_wait(barrier, len(peers))
+
+
+def others(axis):
+    size, me = lax.axis_size(axis), lax.axis_index(axis)
+    return [{axis: lax.rem(me + step, size)} for step in range(1, size)]
+
+
+def tail_kernel(units, *refs):
+    sources, slots = refs[:units], refs[units : units + 2]
+    outs, landed = refs[units + 2 : 2 * units + 2], refs[2 * units + 2 : 2 * units + 4]
+    scratch, ret_sems = refs[2 * units + 4 : -1], refs[-1]
+    greet(others("dp") + others("seq"))
+    summers = [
+        Summer(sources[i], *scratch[6 * i : 6 * i + 5], outs[i], scratch[6 * i + 5]) for i in range(units)
+    ]
+    dp, groups = lax.axis_index("dp"), lax.axis_size("dp")
+    for summer in summers:
+        summer.stage1()
+    back = []
+    for a in range(2):
+        landed[a][dp] = slots[a][dp]
+        for step in range(1, groups):
+            peer = lax.rem(dp + step, groups)
+            copy = pltpu.make_async_remote_copy(
+                src_ref=slots[a].at[peer], dst_ref=landed[a].at[dp],
+                send_sem=ret_sems.at[0, a, step - 1], recv_sem=ret_sems.at[1, a, step - 1],
+                device_id={"dp": peer}, device_id_type=pl.DeviceIdType.MESH,
+            )
+            copy.start()
+            back.append(copy)
+    for summer in summers:
+        summer.stage2()
+    for summer in summers:
+        summer.stage3()
+    for summer in summers:
+        summer.stage4()
+    for summer in summers:
+        summer.finish()
+    for copy in back:
+        copy.wait()
+
+
+def tail(partials, slots):
+    splits, groups = lax.axis_size("seq"), lax.axis_size("dp")
+    out_shapes, scratch = [], []
+    for p in partials:
+        out, more = summer_shapes(p.shape, p.dtype, splits)
+        out_shapes.append(out)
+        scratch += more
+    vmem = pl.BlockSpec(memory_space=pltpu.VMEM)
     return pl.pallas_call(
-        copy_kernel,
-        grid_spec=pltpu.PrefetchScalarGridSpec(
-            num_scalar_prefetch=1, grid=(groups,), in_specs=[spec_in] * len(arrays), out_specs=[spec_out] * len(arrays)
+        functools.partial(tail_kernel, len(partials)),
+        in_specs=[vmem] * (len(partials) + 2),
+        out_specs=[vmem] * (len(partials) + 2),
+        out_shape=out_shapes + [jax.ShapeDtypeStruct(a.shape, a.dtype) for a in slots],
+        scratch_shapes=scratch + [pltpu.SemaphoreType.DMA((2, 2, groups - 1))],
+        compiler_params=pltpu.CompilerParams(
+            collective_id=1, has_side_effects=True, vmem_limit_bytes=VMEM_LIMIT
         ),
-        out_shape=[jax.ShapeDtypeStruct(a.shape, a.dtype) for a in arrays],
-        name="from_slots",
-    )(deal_row, *arrays)
+        name="tail",
+    )(*partials, *slots)
+
+
+def finish_kernel(deal_ref, down, up, out, qkv, small, ret_out, ret_grad, *outs):
+    o_out, o_grad, o_qkv, o_wout, o_up, o_down, o_small = outs
+    length = ret_out.shape[1]
+    for g in range(ret_out.shape[0]):
+        piece = deal_ref[0, g]
+        o_out[pl.ds(g * length, length), :] = ret_out[piece]
+        o_grad[pl.ds(g * length, length), :] = ret_grad[piece]
+    for source, target in ((down, o_down), (up, o_up), (out, o_wout), (qkv, o_qkv)):
+        direct = source.shape[0] * source.shape[1] * source.shape[2] != target.shape[0] * target.shape[1]
+        cols = source.shape[2]
+        if direct:
+            value = add_low(*[source[t] for t in range(source.shape[0])])
+        else:
+            value = source[...].reshape(-1, cols).astype(F32)
+        height = target.shape[0]
+        for c in range(target.shape[1] // cols):
+            target[:, c * cols : (c + 1) * cols] = value[c * height : (c + 1) * height]
+    o_small[...] = add_low(*[small[t] for t in range(small.shape[0])])
+
+
+def finish(deal, sums, returned, shapes):
+    return pl.pallas_call(
+        finish_kernel,
+        in_specs=[pl.BlockSpec(memory_space=pltpu.SMEM)] + [pl.BlockSpec(memory_space=pltpu.VMEM)] * 7,
+        out_specs=[pl.BlockSpec(memory_space=pltpu.VMEM)] * len(shapes),
+        out_shape=shapes,
+        compiler_params=pltpu.CompilerParams(vmem_limit_bytes=VMEM_LIMIT),
+        name="finish",
+    )(deal, *sums, *returned)
 
 
 def swap_slots(values):
@@ -390,30 +576,40 @@
         "cb,hc->bh", one_hot, dd.reshape(H, span), precision=lax.Precision.HIGHEST
     )
 
-    def total(values):
-        part = lax.psum_scatter(values.astype(BF16), "dp", scatter_dimension=0, tiled=True)
-        return lax.psum(part, "seq").astype(F32)
-
-    total_down = total(grad_wdown)
-    total_up = total(grad_wup)
-    total_out = total(grad_wout)
-    total_qkv = total(grad_wqkv)
+    def by_owner(values):
+        rows, cols = values.shape
+        parts = values.astype(BF16).reshape(groups, rows // groups, cols // width, width)
+        return parts.transpose(0, 2, 1, 3).reshape(groups, -1, width)
+
     small_grads = jnp.concatenate(
+        [g.reshape(groups, -1) for g in (grad_gain_one, grad_bias_one, grad_gain_two, grad_bias_two, grad_rel)], axis=1
+    )
+    small_cols = small_grads.shape[1]
+    small_grads = jnp.pad(small_grads, ((0, 0), (0, 8 * PAIR - small_cols))).reshape(groups, 8, PAIR)
+    *sums, back_out, back_grad = tail(
+        [by_owner(grad_wdown), by_owner(grad_wup), by_owner(grad_wout), by_owner(grad_wqkv), small_grads],
+        [output_rows.reshape(pieces), grad_x.reshape(pieces)],
+    )
+    output, grad_tokens, total_qkv, total_out, total_up, total_down, small_total = finish(
+        deal,
+        sums,
+        [back_out, back_grad],
         [
-            g.reshape(groups, -1)
-            for g in (grad_gain_one, grad_bias_one, grad_gain_two, grad_bias_two, grad_rel)
+            jax.ShapeDtypeStruct((tok_dev, width), BF16),
+            jax.ShapeDtypeStruct((tok_dev, width), BF16),
+            jax.ShapeDtypeStruct(w_qkv.shape, F32),
+            jax.ShapeDtypeStruct(w_out.shape, F32),
+            jax.ShapeDtypeStruct(w_up.shape, F32),
+            jax.ShapeDtypeStruct(w_down.shape, F32),
+            jax.ShapeDtypeStruct((8, PAIR), F32),
         ],
-        axis=1,
     )
-    small_total = lax.psum(lax.psum_scatter(small_grads, "dp", scatter_dimension=0, tiled=True), "seq")[0]
+    small_total = small_total.reshape(-1)[:small_cols]
     cut = [small_total[i * shard_rows : (i + 1) * shard_rows] for i in range(4)]
     total_rel = small_total[4 * shard_rows :].reshape(rel_bias.shape)
-
-    returned_both = swap_slots(jnp.stack([output_rows.reshape(pieces), grad_x.reshape(pieces)], axis=1))
-    output, grad_tokens = from_slots(deal_row, [returned_both[:, 0], returned_both[:, 1]])
     return (
-        output.reshape(tok_dev, width),
-        grad_tokens.reshape(tok_dev, width),
+        output,
+        grad_tokens,
         cut[0],
         cut[1],
         total_qkv,

time: 383 us -> 322 us (0.84)
  waiting for transfers between devices: 132 us -> 15 us
  Pallas kernels: 53.3 us -> 140 us
  blocking collectives: 69.9 us -> 33.9 us
  local copies, waits for them, and re-layouts: 15.9 us -> 34.1 us
  other arithmetic: 19.7 us -> 15.1 us
  starting transfers between devices: 21 us -> 16.8 us
  matrix products: 52.2 us -> 48.2 us
    reduce_scatter x4 -> x0, waiting for transfers between devices: 92.9 us -> none  [total(): lax.psum_scatter(values.astype(BF16), 'dp', scatter_dimension=0, tiled=True)]
    pallas_call x1 -> x2, Pallas kernels: 5.72 us -> 92.9 us  [the longest x1 89.9 us: tail(): pl.pallas_call(functools.partial(tail_kernel, len(partials)), in_specs=[v...]
    unnamed x2 -> x1, blocking collectives: 47.8 us -> 24 us
    ppermute x2, waiting for transfers between devices: 22.2 us -> 0.01 us  [shards(): lax.ppermute(part_before[(back - step) * tok_dev:(back - step + 1) * tok_...]
    psum x1 -> x0, blocking collectives: 12.1 us -> none  [shards(): lax.psum(lax.psum_scatter(small_grads, 'dp', scatter_dimension=0, tiled=T...]
    dot_general x1, matrix products: 13.4 us -> 4.87 us  [shards(): pre_act = jnp.dot(normed_two_low, wup_full, preferred_element_type=F32)]
    reshape x1 -> x2, local copies, waits for them, and re-layouts: 0.66 us -> 7.97 us  [by_owner(): values.astype(BF16).reshape(groups, rows // groups, cols // width, width)]
    dot_general x1, matrix products: 6.43 us -> 12.4 us  [shards(): jnp.einsum('td,fd->tf', grad_out, wdown_full, preferred_element_type=F32)]
  transfers between devices with their start and end apart: 14 -> 8, of which waited for: 8 -> 2; matrix products, arithmetic and copies ran while one was open for 18% -> 17% of each run, Pallas kernels for 14% -> 6%
where the time goes in v2:
time: 322 us; the launch traced here: 320 us
  Pallas kernels  140 us (43%)
  matrix products  48.2 us (15%)
  local copies, waits for them, and re-layouts  34.1 us (11%)
  blocking collectives  33.9 us (11%)
  between operations  16.9 us (5%)
  starting transfers between devices  16.8 us (5%)
  other arithmetic  15.1 us (5%)
  waiting for transfers between devices  15 us (5%)
    pallas_call x1, Pallas kernels, tail(): pl.pallas_call(functools.partial(tail_kernel, len(partials)), in_specs=[v...  89.9 us
    pallas_call x1, Pallas kernels, attention_bwd(): pl.pallas_call(attention_bwd_kernel, grid=(H // 2,), in_specs=[pl.BlockSp...  28.2 us
    unnamed x1, blocking collectives  24 us
    pallas_call x1, Pallas kernels, attention_fwd(): pl.pallas_call(attention_fwd_kernel, grid=(H // 2,), in_specs=[pl.BlockSp...  13.3 us
    ppermute x2, waiting for transfers between devices, shards(): lax.ppermute(normed_low, 'seq', [(i, i + step) for i in range(splits - st...  12.9 us
    dot_general x1, matrix products, shards(): jnp.einsum('td,fd->tf', grad_out, wdown_full, preferred_element_type=F32)  12.4 us
    all_gather x1, blocking collectives, shards(): wout_full = lax.all_gather(w_out, 'dp', axis=0, tiled=True)  9.94 us
    ppermute x2, starting transfers between devices, shards(): lax.ppermute(normed_low, 'seq', [(i, i + step) for i in range(splits - st...  8.8 us
  transfers between devices with their start and end apart: 8, of which 2 were waited for; matrix products, arithmetic and copies ran while one was open for 17% of the time, Pallas kernels for 6%

profile of v2, /device:TPU:0, one launch (start us, length us, event | category | flops | bytes accessed | tf_op | source)
XLA Modules:
  0.0 320.1 jit_solution(4103397156145149459)
XLA Ops:
  8.7 5.7 %to_slots.1 = (bf16[8,64,512]{2,1,0:T(8,128)(2,1)}, bf16[8,64,512]{2,1,0:T(8,128)(2,1)}) custom-call(s32[8]{0:T(128)} %bitcast.83, bf16[8,64,512]{2,1,0:T(8,128)(2,1)} %bitcast.76, bf16[8,64,512]{2,1,0:T(8,128)(2,1)} %bitcast.77), custom_call_target="tpu_custom_call" | custom-call | tf_op jit(solution)/shard_map/to_slots/pallas_call | solution.py:242
  14.5 1.4 pad_maximum_fusion.3
  15.8 1.1 copy.32
  16.9 5.2 %all-to-all-start = ((bf16[8,2,64,512]{3,2,1,0:T(8,128)(2,1)}), bf16[8,2,64,512]{3,2,1,0:T(8,128)(2,1)S(1)}, u32[]{:S(2)}, u32[]{:S(2)}) async-start(bf16[8,2,64,512]{3,2,1,0:T(8,128)(2,1)} %copy.32), calls=%async_computation | async-start | bytes 2097152 | tf_op jit(solution)/shard_map/all_to_all | solution.py:453
  24.6 24.0 %all-reduce.1 = bf16[2304]{0:T(1024)(128)(2,1)S(1)} all-reduce(bf16[2304]{0:T(1024)(128)(2,1)S(1)} %dynamic-update-slice), channel_id=2, replica_groups=mesh['seq'=4,'dp'=8] {'dp'}, use_global_device_ids=true, to_apply=%add.1 | all-reduce | flops 2304 | bytes 9216
  53.8 9.9 %all_gather.21 = bf16[512,512]{1,0:T(8,128)(2,1)S(1)} all-gather(bf16[64,512]{1,0:T(8,128)(2,1)S(1)} %copy-done.17), channel_id=1, replica_groups=mesh['seq'=4,'dp'=8] {'dp'}, dimensions={0}, use_global_device_ids=true | all-gather | bytes 589824 | tf_op jit(solution)/shard_map/all_gather | solution.py:487
  64.6 1.0 select_convert_fusion.kx_ref
  66.5 4.3 %collective-permute-start.1 = (bf16[512,512]{1,0:T(8,128)(2,1)S(1)}, bf16[512,512]{1,0:T(8,128)(2,1)}, u32[]{:S(2)}, u32[]{:S(2)}) collective-permute-start(bf16[512,512]{1,0:T(8,128)(2,1)S(1)} %add_convert_fusion.3), channel_id=1, source_target_pairs={{0,8},{8,16},{16,24},{1,9},{9,17},{17,25},{2,10},{10,18},{18,26},{... | collective-permute-start | bytes 1572872 | tf_op jit(solution)/shard_map/ppermute | solution.py:524
  70.8 4.5 %collective-permute-start = (bf16[512,512]{1,0:T(8,128)(2,1)S(1)}, bf16[512,512]{1,0:T(8,128)(2,1)}, u32[]{:S(2)}, u32[]{:S(2)}) collective-permute-start(bf16[512,512]{1,0:T(8,128)(2,1)S(1)} %add_convert_fusion.3), channel_id=1, source_target_pairs={{0,16},{8,24},{1,17},{9,25},{2,18},{10,26},{3,19},{11,27},{4,20},{... | collective-permute-start | bytes 1572872 | tf_op jit(solution)/shard_map/ppermute | solution.py:524
  75.3 1.2 slice_convert_fusion
  76.5 2.6 convolution_convert_fusion
  79.1 0.9 fusion.62
  80.0 2.2 collective-permute-done.1
  82.2 10.7 %collective-permute-done = bf16[512,512]{1,0:T(8,128)(2,1)} collective-permute-done((bf16[512,512]{1,0:T(8,128)(2,1)S(1)}, bf16[512,512]{1,0:T(8,128)(2,1)}, u32[]{:S(2)}, u32[]{:S(2)}) %collective-permute-start) | collective-permute-done | bytes 524320 | tf_op jit(solution)/shard_map/ppermute | solution.py:524
  93.0 2.5 convolution_convert_fusion.3
  95.6 1.9 pad_maximum_fusion
  97.5 13.3 %attention_fwd.1 = (bf16[512,512]{1,0:T(8,128)(2,1)}, f32[512,512]{1,0:T(8,128)}) custom-call(f32[4,2,1280]{2,1,0:T(2,128)} %reshape.260.base_ref, bf16[512,512]{1,0:T(8,128)(2,1)} %get-tuple-element.73.q_ref, bf16[512,128]{1,0:T(8,128)(2,1)} %select_convert_fusion.1.qx_ref, bf16[1536,512]{1,0:T(8,128)(2,1)} %get-tuple-element.90.k_ref, ...), custom_call_target="tpu_custom_call" | custom-call | tf_op jit(solution)/shard_map/attention_fwd/pallas_call | solution.py:165
  110.8 1.9 fusion.66
  113.0 4.9 %fusion.58 = f32[512,2048]{1,0:T(8,128)} fusion(bf16[512,2048]{1,0:T(8,128)(2,1)} %all-gather.7.cloned.1.call-done, f32[512,512]{1,0:T(8,128)S(1)} %get-tuple-element.86, f32[512]{0:T(512)S(1)} %reshape.279, f32[512]{0:T(512)S(1)} %reshape.278, f32[512]{0:T(512)S(1)} %fusion.51, f32[512]{0:T(512)S(1)} %broadcast_multiply_fusion.1), kind=kOutput, calls=%fused_computation.117 | convolution fusion | flops 1075052544 | bytes 7348224 | tf_op jit(solution)/shard_map/dot_general | solution.py:537
  117.9 12.4 %add_convert_fusion = (bf16[512,2048]{1,0:T(8,128)(2,1)S(1)}, f32[512,2048]{1,0:T(8,128)S(1)}) fusion(f32[512,2048]{1,0:T(8,128)} %fusion.58, bf16[512,512]{1,0:T(8,128)(2,1)S(1)} %bitcast.69, bf16[2048,512]{1,0:T(8,128)(2,1)} %all-gather.9.cloned.1.call-done), kind=kOutput, calls=%fused_computation.2 | convolution fusion | flops 1149239296 | bytes 13107200 | tf_op jit(solution)/shard_map/td,fd->tf/dot_general | solution.py:543
  130.3 2.8 convolution_convert_fusion.1
  133.1 1.6 multiply_reduce_fusion.1
  135.9 1.3 convolution_convert_fusion.5.do_ref
  137.2 1.3 convolution_convert_fusion.6
  138.4 1.0 multiply_convert_fusion
  139.4 2.6 convolution_convert_fusion.2
  142.1 28.2 %attention_bwd.1 = (bf16[512,512]{1,0:T(8,128)(2,1)}, bf16[1536,512]{1,0:T(8,128)(2,1)}, bf16[1536,512]{1,0:T(8,128)(2,1)}, f32[4,2,1280]{2,1,0:T(2,128)}) custom-call(f32[4,2,1280]{2,1,0:T(2,128)} %reshape.260.base_ref, bf16[512,512]{1,0:T(8,128)(2,1)} %get-tuple-element.73.q_ref, bf16[512,128]{1,0:T(8,128)(2,1)} %select_convert_fusion.1.qx_ref, ...), custom_call_target="tpu_custom_call" | custom-call | tf_op jit(solution)/shard_map/attention_bwd/pallas_call | solution.py:191
  171.1 2.5 convolution_convert_fusion.4
  173.5 2.0 copy.34
  175.6 1.8 constant_dynamic-update-slice_fusion.1
  177.9 1.3 fusion.21
  179.2 1.1 fusion.63
  180.3 1.3 collective-permute-start.2
  181.6 1.4 collective-permute-start.3
  183.0 3.0 fusion.18
  186.1 1.3 pad_maximum_fusion.2
  188.3 1.0 slice.139
  189.3 4.5 %reshape.262 = bf16[8,64,4,512]{3,2,1,0:T(4,128)(2,1)} reshape(bf16[512,2048]{1,0:T(8,128)(2,1)} %convolution_convert_fusion.1) | data formatting | bytes 4194304 | tf_op jit(solution)/shard_map/reshape | solution.py:581
  193.8 3.4 %copy.33 = bf16[8,64,4,512]{3,1,2,0:T(8,128)(2,1)} copy(bf16[8,64,4,512]{3,2,1,0:T(4,128)(2,1)} %reshape.262) | data formatting | bytes 4194304 | tf_op jit(solution)/shard_map/reshape | solution.py:581
  197.5 5.6 %convert_element_type.165 = bf16[8,64,3,512]{3,2,1,0:T(4,128)(2,1)} reshape(bf16[512,1536]{1,0:T(8,128)(2,1)} %pad_maximum_fusion.2) | data formatting | bytes 3145728 | tf_op jit(solution)/shard_map/convert_element_type | solution.py:581
  203.1 3.4 %copy.35 = bf16[8,3,64,512]{3,2,1,0:T(8,128)(2,1)} copy(bf16[8,3,64,512]{3,1,2,0:T(4,128)(2,1)} %bitcast.67) | data formatting | bytes 3145728 | tf_op jit(solution)/shard_map/transpose | solution.py:582
  206.5 3.8 %fusion.24 = bf16[512,512]{1,0:T(8,128)(2,1)} fusion(f32[512,512]{1,0:T(8,128)S(1)} %get-tuple-element.86, bf16[512,2048]{1,0:T(8,128)(2,1)S(1)} %copy-done.8, bf16[2048,512]{1,0:T(8,128)(2,1)} %all-gather.9.cloned.1.call-done), kind=kOutput, calls=%fused_computation.46 | convolution fusion | flops 1074266112 | bytes 5767168 | tf_op jit(solution)/shard_map/dot_general | solution.py:540
  210.4 2.5 multiply_reduce_fusion
  212.9 1.0 copy-done.6
  215.4 2.5 add_convert_fusion.1
  218.0 89.9 %tail.1 = (bf16[4,64,512]{2,1,0:T(8,128)(2,1)}, bf16[4,64,512]{2,1,0:T(8,128)(2,1)}, bf16[4,16,512]{2,1,0:T(8,128)(2,1)}, bf16[4,48,512]{2,1,0:T(8,128)(2,1)}, f...) custom-call(bf16[8,256,512]{2,1,0:T(8,128)(2,1)} %bitcast.73, ...), custom_call_target="tpu_custom_call" | custom-call | tf_op jit(solution)/shard_map/tail/pallas_call | solution.py:408
  307.8 3.0 finish.1
  311.6 1.4 fusion.64
  (129 shorter events, 15.1 us)
Async XLA Ops:
  7.2 69.3 %all-gather.5.cloned.1.call-start = ((), (), s32[]{:S(2)}) async-start(), calls=%async_computation.1 | async-start | bytes 1769472 | tf_op jit(solution)/shard_map/all_gather | solution.py:485
  7.9 105.1 %all-gather.7.cloned.1.call-start = ((), (), s32[]{:S(2)}) async-start(), calls=%async_computation.2 | async-start | bytes 2359296 | tf_op jit(solution)/shard_map/all_gather | solution.py:488
  14.4 8.5 %copy-start.27 = (bf16[4,8]{1,0:T(4,128)(2,1)S(1)}, bf16[4,8]{1,0:T(4,128)(2,1)}, u32[]{:S(2)}) copy-start(bf16[4,8]{1,0:T(4,128)(2,1)} %param.23) | copy-start | bytes 196
  14.4 8.6 %copy-start.28 = (u32[32]{0:T(128)S(1)}, u32[32]{0:T(128)}, u32[]{:S(2)}) copy-start(u32[32]{0:T(128)} %constant.121) | copy-start | bytes 388
  14.4 9.8 %copy-start.20 = (bf16[64]{0:T(256)(128)(2,1)S(1)}, bf16[64]{0:T(256)(128)(2,1)}, u32[]{:S(2)}) copy-start(bf16[64]{0:T(256)(128)(2,1)} %param.19) | copy-start | bytes 388
  14.4 9.8 %copy-start.21 = (bf16[64]{0:T(256)(128)(2,1)S(1)}, bf16[64]{0:T(256)(128)(2,1)}, u32[]{:S(2)}) copy-start(bf16[64]{0:T(256)(128)(2,1)} %param.20) | copy-start | bytes 388
  14.4 9.8 %copy-start.22 = (bf16[64]{0:T(256)(128)(2,1)S(1)}, bf16[64]{0:T(256)(128)(2,1)}, u32[]{:S(2)}) copy-start(bf16[64]{0:T(256)(128)(2,1)} %param.24) | copy-start | bytes 388
  14.4 9.8 %copy-start.23 = (bf16[64]{0:T(256)(128)(2,1)S(1)}, bf16[64]{0:T(256)(128)(2,1)}, u32[]{:S(2)}) copy-start(bf16[64]{0:T(256)(128)(2,1)} %param.25) | copy-start | bytes 388
  14.4 34.2 %copy-start.18 = (s32[1,3]{1,0:T(1,128)S(1)}, s32[1,3]{1,0:T(1,128)}, u32[]{:S(2)}) copy-start(s32[1,3]{1,0:T(1,128)} %param.17) | copy-start | bytes 40
  14.4 34.8 %copy-start.19 = (s32[1024]{0:T(1024)S(1)}, s32[1024]{0:T(1024)}, u32[]{:S(2)}) copy-start(s32[1024]{0:T(1024)} %param.18) | copy-start | bytes 12292
  14.5 39.4 %copy-start.17 = (bf16[64,512]{1,0:T(8,128)(2,1)S(1)}, bf16[64,512]{1,0:T(8,128)(2,1)}, u32[]{:S(2)}) copy-start(bf16[64,512]{1,0:T(8,128)(2,1)} %param.22) | copy-start | bytes 196612
  16.9 48.7 %all-to-all-start = ((bf16[8,2,64,512]{3,2,1,0:T(8,128)(2,1)}), bf16[8,2,64,512]{3,2,1,0:T(8,128)(2,1)S(1)}, u32[]{:S(2)}, u32[]{:S(2)}) async-start(bf16[8,2,64,512]{3,2,1,0:T(8,128)(2,1)} %copy.32), calls=%async_computation | async-start | bytes 2097152 | tf_op jit(solution)/shard_map/all_to_all | solution.py:453
  22.1 95.8 %all-gather.9.cloned.1.call-start = ((), (), s32[]{:S(2)}) async-start(), calls=%async_computation.3 | async-start | bytes 2359296 | tf_op jit(solution)/shard_map/all_gather | solution.py:489
  63.8 47.0 %copy-start.4 = (bf16[512,512]{1,0:T(8,128)(2,1)}, bf16[512,512]{1,0:T(8,128)(2,1)S(1)}, u32[]{:S(2)}) copy-start(bf16[512,512]{1,0:T(8,128)(2,1)S(1)} %all_gather.21) | copy-start | bytes 1572868
  66.5 12.6 %copy-start.9 = (bf16[512,512]{1,0:T(8,128)(2,1)}, bf16[512,512]{1,0:T(8,128)(2,1)S(1)}, u32[]{:S(2)}) copy-start(bf16[512,512]{1,0:T(8,128)(2,1)S(1)} %add_convert_fusion.3) | copy-start | bytes 1572868
  66.5 15.7 %collective-permute-start.1 = (bf16[512,512]{1,0:T(8,128)(2,1)S(1)}, bf16[512,512]{1,0:T(8,128)(2,1)}, u32[]{:S(2)}, u32[]{:S(2)}) collective-permute-start(bf16[512,512]{1,0:T(8,128)(2,1)S(1)} %add_convert_fusion.3), channel_id=1, source_target_pairs={{0,8},{8,16},{16,24},{1,9},{9,17},{17,25},{2,10},{10,18},{18,26},{... | collective-permute-start | bytes 1572872 | tf_op jit(solution)/shard_map/ppermute | solution.py:524
  70.8 22.2 %collective-permute-start = (bf16[512,512]{1,0:T(8,128)(2,1)S(1)}, bf16[512,512]{1,0:T(8,128)(2,1)}, u32[]{:S(2)}, u32[]{:S(2)}) collective-permute-start(bf16[512,512]{1,0:T(8,128)(2,1)S(1)} %add_convert_fusion.3), channel_id=1, source_target_pairs={{0,16},{8,24},{1,17},{9,25},{2,18},{10,26},{3,19},{11,27},{4,20},{... | collective-permute-start | bytes 1572872 | tf_op jit(solution)/shard_map/ppermute | solution.py:524
  76.5 41.4 %copy-start.1 = (bf16[8,1,64,512]{3,2,1,0:T(8,128)(2,1)}, bf16[8,1,64,512]{3,2,1,0:T(8,128)(2,1)S(1)}, u32[]{:S(2)}) copy-start(bf16[8,1,64,512]{3,2,1,0:T(8,128)(2,1)S(1)} %get-tuple-element.77) | copy-start | bytes 1572868
  79.1 13.9 %copy-start.24 = (bf16[512,1536]{1,0:T(8,128)(2,1)S(1)}, bf16[512,1536]{1,0:T(8,128)(2,1)}, u32[]{:S(2)}) copy-start(bf16[512,1536]{1,0:T(8,128)(2,1)} %all-gather.5.cloned.1.call-done) | copy-start | bytes 4718596
  130.3 2.8 copy-start.13
  134.6 1.0 copy-start.2
  134.6 1.2 copy-start.5
  134.7 2.5 copy-start.11
  135.1 3.3 %copy-start = (f32[512,2048]{1,0:T(8,128)S(1)}, f32[512,2048]{1,0:T(8,128)}, u32[]{:S(2)}) copy-start(f32[512,2048]{1,0:T(8,128)} %fusion.58) | copy-start | bytes 12582916
  139.4 2.6 copy-start.7
  175.6 1.9 copy-start.14
  175.6 2.4 copy-start.25
  177.9 5.1 %copy-start.10 = (bf16[512,512]{1,0:T(8,128)(2,1)S(1)}, bf16[512,512]{1,0:T(8,128)(2,1)}, u32[]{:S(2)}) copy-start(bf16[512,512]{1,0:T(8,128)(2,1)} %copy-done.9) | copy-start | bytes 1572868
  180.3 30.0 %collective-permute-start.2 = (bf16[512,512]{1,0:T(8,128)(2,1)}, bf16[512,512]{1,0:T(8,128)(2,1)}, u32[]{:S(2)}, u32[]{:S(2)}) collective-permute-start(bf16[512,512]{1,0:T(8,128)(2,1)} %get-tuple-element.74), channel_id=1, source_target_pairs={{16,0},{24,8},{17,1},{25,9},{18,2},{26,10},{19,3},{27,11},{20,4},{... | collective-permute-start | bytes 1572872 | tf_op jit(solution)/shard_map/ppermute | solution.py:558
  181.6 4.5 %copy-start.12 = (bf16[512,512]{1,0:T(8,128)(2,1)S(1)}, bf16[512,512]{1,0:T(8,128)(2,1)}, u32[]{:S(2)}) copy-start(bf16[512,512]{1,0:T(8,128)(2,1)} %copy.34) | copy-start | bytes 1572868
  181.6 28.7 %collective-permute-start.3 = (bf16[512,512]{1,0:T(8,128)(2,1)}, bf16[512,512]{1,0:T(8,128)(2,1)}, u32[]{:S(2)}, u32[]{:S(2)}) collective-permute-start(bf16[512,512]{1,0:T(8,128)(2,1)} %get-tuple-element.75), channel_id=1, source_target_pairs={{8,0},{16,8},{24,16},{9,1},{17,9},{25,17},{10,2},{18,10},{26,18},{... | collective-permute-start | bytes 1572872 | tf_op jit(solution)/shard_map/ppermute | solution.py:558
  203.1 3.4 %copy-start.8 = (bf16[512,2048]{1,0:T(8,128)(2,1)S(1)}, bf16[512,2048]{1,0:T(8,128)(2,1)}, u32[]{:S(2)}) copy-start(bf16[512,2048]{1,0:T(8,128)(2,1)} %copy-done.7) | copy-start | bytes 6291460
  206.5 3.8 %copy-start.15 = (bf16[512,1024]{1,0:T(8,128)(2,1)S(1)}, bf16[512,1024]{1,0:T(8,128)(2,1)}, u32[]{:S(2)}) copy-start(bf16[512,1024]{1,0:T(8,128)(2,1)} %slice.139) | copy-start | bytes 3145732
  206.5 3.8 %copy-start.16 = (bf16[512,512]{1,0:T(8,128)(2,1)S(1)}, bf16[512,512]{1,0:T(8,128)(2,1)}, u32[]{:S(2)}) copy-start(bf16[512,512]{1,0:T(8,128)(2,1)} %get-tuple-element.37) | copy-start | bytes 1572868
  206.5 3.8 %copy-start.26 = (bf16[512,1536]{1,0:T(8,128)(2,1)S(1)}, bf16[512,1536]{1,0:T(8,128)(2,1)}, u32[]{:S(2)}) copy-start(bf16[512,1536]{1,0:T(8,128)(2,1)} %all-gather.5.cloned.1.call-done) | copy-start | bytes 4718596
  210.3 5.1 %copy-start.3 = (bf16[8,1,64,512]{3,2,1,0:T(8,128)(2,1)S(1)}, bf16[8,1,64,512]{3,2,1,0:T(8,128)(2,1)}, u32[]{:S(2)}) copy-start(bf16[8,1,64,512]{3,2,1,0:T(8,128)(2,1)} %copy-done.1) | copy-start | bytes 1572868
  212.8 1.1 copy-start.6
Sparse Core Ops, SparseCore 0:
  9.9 32.3 all-gather.4
  44.2 28.6 all-gather.6
  74.8 27.8 all-gather.8

commit v3 on v2

v3 whole, which is shorter than its diff:
```python
import functools

import jax
import jax.numpy as jnp
from jax import lax
from jax.experimental import pallas as pl
from jax.experimental.pallas import tpu as pltpu
from jax.sharding import PartitionSpec as P

H = 8
HD = 64
NBK = 32
QB = 256
PAIR = 2 * HD
BIG = -1e30
F32 = jnp.float32
BF16 = jnp.bfloat16
VMEM_LIMIT = 60 * 1024 * 1024

NT = (((1,), (1,)), ((), ()))
NN = (((1,), (0,)), ((), ()))


def dot_nt(a, b):
    return lax.dot_general(a, b, NT, preferred_element_type=F32)


def dot_nn(a, b):
    return lax.dot_general(a, b, NN, preferred_element_type=F32)


def norm_rows(values, gain_vec, bias_vec):
    average = jnp.mean(values, axis=-1, keepdims=True)
    centred = values - average
    variance = jnp.mean(centred * centred, axis=-1, keepdims=True)
    return centred * lax.rsqrt(variance + 1e-05) * gain_vec + bias_vec


def toeplitz(row):
    width = row.shape[1]
    return pltpu.roll(jnp.broadcast_to(row, (QB, width)), 0, 1, stride=1, stride_axis=0)[:, QB:]


def attention_fwd_kernel(base_ref, q_ref, qx_ref, k_ref, kx_ref, v_ref, att_ref, lse_ref, bias, kaug, vaug, scores):
    rows = q_ref.shape[0]
    tiles = base_ref.shape[-1] // QB - 1
    lane_q = lax.broadcasted_iota(jnp.int32, (QB, PAIR), 1) < HD
    lane_k = lax.broadcasted_iota(jnp.int32, k_ref.shape, 1) < HD
    for h in range(2):
        mine_k = lane_k if h == 0 else jnp.logical_not(lane_k)
        mine_q = lane_q if h == 0 else jnp.logical_not(lane_q)
        bias[...] = toeplitz(base_ref[0, h : h + 1, :])
        kaug[...] = jnp.where(mine_k, k_ref[...], kx_ref[...])
        vaug[...] = jnp.where(mine_k, v_ref[...], jnp.ones_like(v_ref))
        for b in range(rows // QB):
            here = pl.ds(b * QB, QB)
            q_aug = jnp.where(mine_q, q_ref[here, :], qx_ref[here, :])
            top = None
            for j in range(tiles):
                cols = pl.ds(j * QB, QB)
                s = dot_nt(q_aug, kaug[pl.ds((b + j) * QB, QB), :]) + bias[:, cols]
                scores[:, cols] = s
                most = jnp.maximum(s[:, :128], s[:, 128:])
                top = most if top is None else jnp.maximum(top, most)
            top = jnp.max(top, axis=1, keepdims=True)
            acc = jnp.zeros((QB, PAIR), F32)
            for j in range(tiles):
                p = jnp.exp(scores[:, pl.ds(j * QB, QB)] - top).astype(BF16)
                acc = acc + dot_nn(p, vaug[pl.ds((b + j) * QB, QB), :])
            att = acc / pltpu.roll(acc, HD, 1)
            lse = top + jnp.log(acc)
            if h == 0:
                att_ref[here, :] = att.astype(BF16)
                lse_ref[here, :] = lse
            else:
                att_ref[here, :] = jnp.where(mine_q, att.astype(BF16), att_ref[here, :])
                lse_ref[here, :] = jnp.where(mine_q, lse_ref[here, :], lse)


def column_block(rows):
    return pl.BlockSpec((rows, PAIR), lambda i: (0, i))


def whole_block(rows):
    return pl.BlockSpec((rows, PAIR), lambda i: (0, 0))


def attention_fwd(base, q, qx, k, kx, v):
    rows, width, window = q.shape[0], base.shape[-1], k.shape[0]
    return pl.pallas_call(
        attention_fwd_kernel,
        grid=(H // 2,),
        in_specs=[
            pl.BlockSpec((1, 2, width), lambda i: (i, 0, 0)),
            column_block(rows),
            whole_block(rows),
            column_block(window),
            whole_block(window),
            column_block(window),
        ],
        out_specs=[column_block(rows), column_block(rows)],
        out_shape=[jax.ShapeDtypeStruct(q.shape, BF16), jax.ShapeDtypeStruct(q.shape, F32)],
        scratch_shapes=[
            pltpu.VMEM((QB, width - QB), F32),
            pltpu.VMEM((window, PAIR), BF16),
            pltpu.VMEM((window, PAIR), BF16),
            pltpu.VMEM((QB, width - QB), F32),
        ],
        compiler_params=pltpu.CompilerParams(vmem_limit_bytes=VMEM_LIMIT),
        name="attention_fwd",
    )(base, q, qx, k, kx, v)


def copy_kernel(deal_ref, *refs):
    count = len(refs) // 2
    for i in range(count):
        refs[count + i][...] = refs[i][...]


def to_slots(deal_row, arrays):
    groups, length, width = arrays[0].shape
    spec_in = pl.BlockSpec((1, length, width), lambda g, deal: (g, 0, 0))
    spec_out = pl.BlockSpec((1, length, width), lambda g, deal: (deal[g], 0, 0))
    return pl.pallas_call(
        copy_kernel,
        grid_spec=pltpu.PrefetchScalarGridSpec(
            num_scalar_prefetch=1, grid=(groups,), in_specs=[spec_in] * len(arrays), out_specs=[spec_out] * len(arrays)
        ),
        out_shape=[jax.ShapeDtypeStruct(a.shape, a.dtype) for a in arrays],
        name="to_slots",
    )(deal_row, *arrays)


def add_low(first, *others):
    total = first.astype(F32)
    for other in others:
        total = total + other.astype(F32)
    return total


class Summer:
    def __init__(self, source, pair, recv2, mine, recv3, out, sems):
        self.source, self.pair, self.recv2 = source, pair, recv2
        self.mine, self.recv3, self.out, self.sems = mine, recv3, out, sems
        self.dp, self.seq = lax.axis_index("dp"), lax.axis_index("seq")
        self.pairs, self.splits = source.shape[0] // 2, lax.axis_size("seq")
        self.core, self.chip = lax.rem(self.dp, 2), self.dp // 2
        self.scatter = out.shape[1] < mine.shape[0]
        self.sent = []
        self.count = 0

    def send(self, src, dst, device):
        slot = self.count
        self.count += 1
        copy = pltpu.make_async_remote_copy(
            src_ref=src, dst_ref=dst, send_sem=self.sems.at[0, slot], recv_sem=self.sems.at[1, slot],
            device_id=device, device_id_type=pl.DeviceIdType.MESH,
        )
        copy.start()
        self.sent.append(copy)
        return copy

    def stage1(self):
        other = 1 - self.core
        self.first = [
            self.send(self.source.at[2 * k + other], self.pair.at[k], {"dp": self.dp + 1 - 2 * self.core})
            for k in range(self.pairs)
        ]

    def stage2(self):
        self.second = []
        for step in range(self.pairs):
            k = lax.rem(self.chip + 1 + step, self.pairs)
            if step == 0:
                for copy in self.first:
                    copy.wait_recv()
            self.pair[k] = add_low(self.source[2 * k + self.core], self.pair[k]).astype(self.pair.dtype)
            if step < self.pairs - 1:
                self.second.append(self.send(self.pair.at[k], self.recv2.at[step], {"dp": 2 * k + self.core}))

    def stage3(self):
        for copy in self.second:
            copy.wait_recv()
        total = add_low(self.pair[self.chip], *[self.recv2[step] for step in range(self.pairs - 1)])
        self.mine[...] = total.astype(self.mine.dtype)
        self.third = []
        rows = self.out.shape[1]
        for step in range(self.splits - 1):
            t = lax.rem(self.seq + 1 + step, self.splits)
            src = self.mine.at[pl.ds(pl.multiple_of(t * rows, rows), rows)] if self.scatter else self.mine
            dst = self.recv3.at[step] if self.scatter else self.out.at[self.seq]
            self.third.append(self.send(src, dst, {"seq": t}))
        if not self.scatter:
            self.out[self.seq] = self.mine[...]

    def stage4(self):
        for copy in self.third:
            copy.wait_recv()
        if not self.scatter:
            return
        rows = self.out.shape[1]
        own = self.mine[pl.ds(pl.multiple_of(self.seq * rows, rows), rows)]
        total = add_low(own, *[self.recv3[step] for step in range(self.splits - 1)])
        self.out[self.seq] = total.astype(self.out.dtype)
        self.fourth = [
            self.send(self.out.at[self.seq], self.out.at[self.seq], {"seq": lax.rem(self.seq + 1 + step, self.splits)})
            for step in range(self.splits - 1)
        ]

    def finish(self):
        if self.scatter:
            for copy in self.fourth:
                copy.wait_recv()
        for copy in self.sent:
            copy.wait_send()


def summer_shapes(shape, dtype, splits):
    groups, rows, cols = shape
    pairs = groups // 2
    scatter = rows % (16 * splits) == 0
    out = jax.ShapeDtypeStruct((splits, rows // splits if scatter else rows, cols), dtype)
    copies = pairs + (pairs - 1) + (splits - 1) * (2 if scatter else 1)
    scratch = [
        pltpu.VMEM((pairs, rows, cols), dtype),
        pltpu.VMEM((pairs - 1, rows, cols), dtype),
        pltpu.VMEM((rows, cols), dtype),
        pltpu.VMEM((splits - 1, out.shape[1] if scatter else 16, cols), dtype),
        pltpu.SemaphoreType.DMA((2, copies)),
    ]
    return out, scratch


def greet(peers):
    barrier = pltpu.get_barrier_semaphore()
    for device in peers:
        pl.semaphore_signal(barrier, inc=1, device_id=device, device_id_type=pl.DeviceIdType.MESH)
    pl.semaphore_wait(barrier, len(peers))


def others(axis):
    size, me = lax.axis_size(axis), lax.axis_index(axis)
    return [{axis: lax.rem(me + step, size)} for step in range(1, size)]


class SmallSummer:
    def __init__(self, ref, land, sems):
        self.ref, self.land, self.sems = ref, land, sems
        self.dp, self.seq = lax.axis_index("dp"), lax.axis_index("seq")
        self.pairs, self.splits = lax.axis_size("dp") // 2, lax.axis_size("seq")
        self.slot, self.copies, self.sent = 0, [], []

    def send(self, devices):
        self.copies = []
        for device in devices:
            copy = pltpu.make_async_remote_copy(
                src_ref=self.ref.at[len(self.sent)], dst_ref=self.land.at[self.slot],
                send_sem=self.sems.at[0, self.slot], recv_sem=self.sems.at[1, self.slot],
                device_id=device, device_id_type=pl.DeviceIdType.MESH,
            )
            copy.start()
            self.copies.append((self.slot, copy))
            self.slot += 1
        self.sent.append(self.copies)

    def take(self):
        stage = len(self.sent) - 1
        total = self.ref[stage]
        for slot, copy in self.copies:
            copy.wait_recv()
            total = total + self.land[slot]
        self.ref[stage + 1] = total

    def pair(self):
        self.send([{"dp": self.dp + 1 - 2 * lax.rem(self.dp, 2)}])

    def plane(self):
        core, chip = lax.rem(self.dp, 2), self.dp // 2
        self.send([{"dp": 2 * lax.rem(chip + step, self.pairs) + core} for step in range(1, self.pairs)])

    def along(self):
        self.send([{"seq": lax.rem(self.seq + step, self.splits)} for step in range(1, self.splits)])

    def finish(self):
        for copies in self.sent:
            for _, copy in copies:
                copy.wait_send()


def norm_stats(values):
    average = jnp.mean(values, axis=-1, keepdims=True)
    centred = values - average
    scale = lax.rsqrt(jnp.mean(centred * centred, axis=-1, keepdims=True) + 1e-05)
    return centred * scale, scale


def norm_back(grad, normal, scale):
    return scale * (
        grad - jnp.mean(grad, axis=-1, keepdims=True) - normal * jnp.mean(grad * normal, axis=-1, keepdims=True)
    )


def flip(values):
    return values.astype(F32).T.astype(BF16)


def phase_spans(back, per_chunk, tiles):
    spans = []
    for chunk in range(back + 1):
        jobs = [
            (kt, b, chunk * per_chunk + kt - b)
            for kt in range(per_chunk)
            for b in range(per_chunk)
            if 0 <= chunk * per_chunk + kt - b < tiles
        ]
        first, last = min(j[2] for j in jobs), max(j[2] for j in jobs)
        spans.append((chunk, first, last - first + 1, jobs))
    return spans


def rest_kernel(back, *refs):
    (
        x_ref, g_ref, gains_ref, wqkv_ref, wout_ref, wup_ref, wdown_ref, rows_ref,
        base_ref, hot_hi_ref, q_ref, qx_ref, k_ref, kx_ref, v_ref, att_ref, lse_ref,
    ) = refs[:17]
    sum_down, sum_up, sum_out, sum_qkv, small_out, ret_out, ret_grad = refs[17:24]
    it = iter(refs[24:])
    sources = [next(it) for _ in range(4)]
    summers = [
        Summer(source, *[next(it) for _ in range(4)], out, next(it))
        for source, out in zip(sources, (sum_down, sum_up, sum_out, sum_qkv))
    ]
    down, up, out_sum, qkv_sum = summers
    small_ref, small_land, small_sems = next(it), next(it), next(it)
    slots, ret_sems, halo_send, halo_land, halo_sems = (next(it) for _ in range(5))
    dres_ref, do_ref, qaug, doaug, q_t, do_t = (next(it) for _ in range(6))
    bias, dsum, dd, dq_acc, dkt, dvt, dkv, gkv = (next(it) for _ in range(8))
    dp, groups = lax.axis_index("dp"), lax.axis_size("dp")
    seq, splits = lax.axis_index("seq"), lax.axis_size("seq")
    tokens, width = x_ref.shape
    length = tokens // groups
    per_chunk = tokens // QB
    tiles = base_ref.shape[-1] // QB - 1
    greet(others("dp") + others("seq"))

    returns = []

    def send_back(which, landed):
        landed[dp] = slots[which, dp]
        for step in range(1, groups):
            peer = lax.rem(dp + step, groups)
            copy = pltpu.make_async_remote_copy(
                src_ref=slots.at[which, peer], dst_ref=landed.at[dp],
                send_sem=ret_sems.at[0, which, step - 1], recv_sem=ret_sems.at[1, which, step - 1],
                device_id={"dp": peer}, device_id_type=pl.DeviceIdType.MESH,
            )
            copy.start()
            returns.append(copy)

    resid = x_ref[...].astype(F32) + dot_nn(att_ref[...], wout_ref[...])
    normal, scale = norm_stats(resid)
    gain_two = gains_ref[2:3, :]
    a2 = (normal * gain_two + gains_ref[3:4, :]).astype(BF16)
    a2_t = flip(a2)
    g = g_ref[...]
    y = resid
    da2 = jnp.zeros((tokens, width), F32)
    rows_up, rows_down = width // groups, wdown_ref.shape[0] // groups
    for c in range(wdown_ref.shape[0] // width):
        cols = pl.ds(c * width, width)
        upper = dot_nn(a2, wup_ref[:, cols])
        phi = 0.5 + 0.5 * lax.erf(upper * (0.5**0.5))
        act = (upper * phi).astype(BF16)
        y = y + dot_nn(act, wdown_ref[cols, :])
        slope = phi + upper * (jnp.exp(-0.5 * upper * upper) * 0.3989422804014327)
        dup = (dot_nt(g, wdown_ref[cols, :]) * slope).astype(BF16)
        da2 = da2 + dot_nt(dup, wup_ref[:, cols])
        grad_down = dot_nn(flip(act), g).astype(BF16)
        for o in range(width // rows_down):
            sources[0][c * (width // rows_down) + o] = grad_down[o * rows_down : (o + 1) * rows_down]
        grad_up = dot_nn(a2_t, dup).astype(BF16)
        for o in range(groups):
            sources[1][o, c * rows_up : (c + 1) * rows_up] = grad_up[o * rows_up : (o + 1) * rows_up]
    down.stage1()
    up.stage1()
    y = y.astype(BF16)
    for o in range(groups):
        slots[0, o] = y[o * length : (o + 1) * length]
    send_back(0, ret_out)
    small_ref[0, 2:3, :] = jnp.sum(da2 * normal, axis=0, keepdims=True)
    small_ref[0, 3:4, :] = jnp.sum(da2, axis=0, keepdims=True)
    dres = g.astype(F32) + norm_back(da2 * gain_two, normal, scale)
    dres_ref[...] = dres
    dbr = dres.astype(BF16)
    grad_out = dot_nn(flip(att_ref[...]), dbr).astype(BF16)
    rows_out = width // groups
    for o in range(groups):
        sources[2][o] = grad_out[o * rows_out : (o + 1) * rows_out]
    out_sum.stage1()
    do_ref[...] = dot_nt(dbr, wout_ref[...]).astype(BF16)
    q_t[...] = flip(q_ref[...])
    do_t[...] = flip(do_ref[...])

    lane = lax.broadcasted_iota(jnp.int32, (tokens, PAIR), 1)
    extra = lax.rem(lane, HD)
    low_half = lane < HD
    swap = (
        (lax.broadcasted_iota(jnp.int32, (PAIR, PAIR), 0) < HD)
        != (lax.broadcasted_iota(jnp.int32, (PAIR, PAIR), 1) < HD)
    ).astype(BF16)

    def prepare(pair, _):
        cols = pl.ds(pl.multiple_of(pair * PAIR, PAIR), PAIR)
        prod = do_ref[:, cols].astype(F32) * att_ref[:, cols].astype(F32)
        prod_hi = prod.astype(BF16)
        prod_lo = (prod - prod_hi.astype(F32)).astype(BF16)
        delta = -(dot_nn(prod_hi, swap) + dot_nn(prod_lo, swap))
        delta_hi = delta.astype(BF16).astype(F32)
        lse = -lse_ref[:, cols]
        lse_hi = lse.astype(BF16).astype(F32)
        lse_mid = (lse - lse_hi).astype(BF16).astype(F32)
        lse_lo = lse - lse_hi - lse_mid
        q_extra = jnp.where(
            extra == HD - 3,
            lse_hi,
            jnp.where(extra == HD - 2, lse_mid, jnp.where(extra == HD - 1, lse_lo, qx_ref[...].astype(F32))),
        ).astype(BF16)
        do_extra = jnp.where(extra == 0, delta_hi, jnp.where(extra == 1, delta - delta_hi, 0.0)).astype(BF16)
        qaug[2 * pair] = jnp.where(low_half, q_ref[:, cols], q_extra)
        qaug[2 * pair + 1] = jnp.where(low_half, q_extra, q_ref[:, cols])
        doaug[2 * pair] = jnp.where(low_half, do_ref[:, cols], do_extra)
        doaug[2 * pair + 1] = jnp.where(low_half, do_extra, do_ref[:, cols])
        return _

    lax.fori_loop(0, H // 2, prepare, 0)
    dd[...] = jnp.zeros_like(dd)
    dq_acc[...] = jnp.zeros_like(dq_acc)
    halo = []

    def attend(chunk, first, count, jobs):
        span = count * QB
        keys = pl.ds(chunk * tokens, tokens)
        fresh = set()

        def body(pair, _):
            cols = pl.ds(pl.multiple_of(pair * PAIR, PAIR), PAIR)
            k_pair, v_pair, kx = k_ref[keys, cols], v_ref[keys, cols], kx_ref[keys, :]
            for h in range(2):
                mine = low_half if h == 0 else jnp.logical_not(low_half)
                head = 2 * pair + h
                bias[:, :span] = toeplitz(base_ref[pair, h : h + 1, first * QB : (first + count + 1) * QB])
                k_aug = jnp.where(mine, k_pair, kx)
                v_aug = jnp.where(mine, v_pair, jnp.ones_like(v_pair))
                feat = pl.ds(pl.multiple_of(head * HD, HD), HD)
                spot = pl.ds(h * HD, HD)
                fresh.clear()
                dq = [None] * per_chunk
                for kt in range(per_chunk):
                    part = slice(kt * QB, (kt + 1) * QB)
                    dk_t = dv_t = None
                    for b in range(per_chunk):
                        if (kt, b, chunk * per_chunk + kt - b) not in jobs:
                            continue
                        j = chunk * per_chunk + kt - b - first
                        here = pl.ds(b * QB, QB)
                        over = pl.ds(j * QB, QB)
                        p = jnp.exp(dot_nt(qaug[head, here, :], k_aug[part]) + bias[:, over])
                        ds = p * dot_nt(doaug[head, here, :], v_aug[part])
                        ds_low = ds.astype(BF16)
                        more_v = dot_nn(do_t[feat, here], p.astype(BF16))
                        more_k = dot_nn(q_t[feat, here], ds_low)
                        more_q = dot_nn(ds_low, k_pair[part])
                        dv_t = more_v if dv_t is None else dv_t + more_v
                        dk_t = more_k if dk_t is None else dk_t + more_k
                        dq[b] = more_q if dq[b] is None else dq[b] + more_q
                        if j in fresh:
                            dsum[:, over] += ds
                        else:
                            fresh.add(j)
                            dsum[:, over] = ds
                    dkt[spot, part] = dk_t
                    dvt[spot, part] = dv_t
                for b in range(per_chunk):
                    if dq[b] is not None:
                        here = pl.ds(b * QB, QB)
                        dq_acc[here, cols] += jnp.where(mine[:QB], dq[b], 0.0)
                left = jnp.concatenate([jnp.zeros((QB, QB), F32), dsum[:, :span]], axis=1)
                half = QB // 2
                while half:
                    left = left[:half] + pltpu.roll(left[half:], span + QB - half, 1)
                    half //= 2
                dd[pair, h : h + 1, first * QB : (first + count + 1) * QB] += left
            dkv[:, cols] = dkt[...].T.astype(BF16)
            dkv[:, pl.ds(pl.multiple_of(width + pair * PAIR, PAIR), PAIR)] = dvt[...].T.astype(BF16)
            return _

        lax.fori_loop(0, H // 2, body, 0)

    def halo_copy(step):
        return pltpu.make_async_remote_copy(
            src_ref=halo_send.at[step - 1], dst_ref=halo_land.at[step - 1],
            send_sem=halo_sems.at[0, step - 1], recv_sem=halo_sems.at[1, step - 1],
            device_id={"seq": lax.rem(seq + splits - 1, splits)}, device_id_type=pl.DeviceIdType.MESH,
        )

    grad_normed = None
    for index, (chunk, first, count, jobs) in enumerate(phase_spans(back, per_chunk, tiles)):
        attend(chunk, first, count, jobs)
        step = back - chunk
        part = dot_nt(dkv[...], wqkv_ref[:, width:])
        rows_t = flip(rows_ref[chunk * tokens : (chunk + 1) * tokens, :])
        if index == 0:
            gkv[...] = dot_nn(rows_t, dkv[...])
        else:
            gkv[...] += dot_nn(rows_t, dkv[...])
        if step == 0:
            dq_low = (dq_acc[...] * (HD**-0.5)).astype(BF16)
            grad_normed = part + dot_nt(dq_low, wqkv_ref[:, :width])
            grad_q = dot_nn(rows_t, dq_low).astype(BF16)
            for o in range(groups):
                take = slice(o * rows_up, (o + 1) * rows_up)
                sources[3][o, :rows_up] = grad_q[take]
                sources[3][o, rows_up : 2 * rows_up] = gkv[take, :width].astype(BF16)
                sources[3][o, 2 * rows_up :] = gkv[take, width:].astype(BF16)
            qkv_sum.stage1()
        else:
            if step < back:

                @pl.when((seq + 1 < splits) & (seq >= step))
                def _(step=step):
                    halo_copy(step + 1).wait_recv()

                arrived = jnp.where((seq + 1 < splits) & (seq >= step), halo_land[step].astype(F32), 0.0)
                part = part + arrived
            halo_send[step - 1] = part.astype(BF16)

            @pl.when(seq >= step)
            def _(step=step):
                halo_copy(step).start()

        if index == 0:
            down.stage2()
            up.stage2()
            out_sum.stage2()
        if index == back - 1 and back > 0:
            down.stage3()
    up.stage3()
    out_sum.stage3()
    qkv_sum.stage2()

    @pl.when(seq + 1 < splits)
    def _():
        halo_copy(1).wait_recv()

    grad_normed = grad_normed + jnp.where(seq + 1 < splits, halo_land[0].astype(F32), 0.0)
    normal, scale = norm_stats(x_ref[...].astype(F32))
    small_ref[0, 0:1, :] = jnp.sum(grad_normed * normal, axis=0, keepdims=True)
    small_ref[0, 1:2, :] = jnp.sum(grad_normed, axis=0, keepdims=True)
    small_ref[0, 4:8, :] = jnp.zeros((4, width), F32)
    dd_all = dd[...].reshape(H, dd.shape[-1])
    dd_hi = dd_all.astype(BF16)
    dd_mid = (dd_all - dd_hi.astype(F32)).astype(BF16)
    small_ref[0, 8:16, :PAIR] = dot_nn(dd_hi, hot_hi_ref[...]) + dot_nn(dd_mid, hot_hi_ref[...])
    small_ref[0, 8:16, PAIR:] = jnp.zeros((8, width - PAIR), F32)
    small = SmallSummer(small_ref, small_land, small_sems)
    small.pair()
    dx = (dres_ref[...] + norm_back(grad_normed * gains_ref[0:1, :], normal, scale)).astype(BF16)
    for o in range(groups):
        slots[1, o] = dx[o * length : (o + 1) * length]
    send_back(1, ret_grad)
    small.take()
    small.plane()
    down.stage4()
    up.stage4()
    qkv_sum.stage3()
    small.take()
    small.along()
    out_sum.stage4()
    qkv_sum.stage4()
    small.take()
    small_out[...] = small_ref[3]
    for summer in summers:
        summer.finish()
    small.finish()
    for copy in returns:
        copy.wait()
    for step in range(1, back + 1):

        @pl.when(seq >= step)
        def _(step=step):
            halo_copy(step).wait_send()


def rest(back, x, g, gains, wqkv, wout, wup, wdown, rows, base, hot, q, qx, k, kx, v, att, lse):
    splits, groups = lax.axis_size("seq"), lax.axis_size("dp")
    tokens, width = x.shape
    length = tokens // groups
    per_chunk = tokens // QB
    span = max(count for _, _, count, _ in phase_spans(back, per_chunk, base.shape[-1] // QB - 1)) * QB
    grads = [(wdown.shape[0] // groups), (wup.shape[1] // groups), width // groups, 3 * width // groups]
    out_shapes, more, sources = [], [], []
    for height in grads:
        shape = (groups, height, width)
        out, scratch = summer_shapes(shape, BF16, splits)
        sources.append(pltpu.VMEM(shape, BF16))
        out_shapes.append(out)
        more += scratch
    out_shapes.append(jax.ShapeDtypeStruct((16, width), F32))
    out_shapes += [jax.ShapeDtypeStruct((groups, length, width), BF16)] * 2
    small_copies = 1 + (groups // 2 - 1) + (splits - 1)
    scratch = sources + more + [
        pltpu.VMEM((4, 16, width), F32),
        pltpu.VMEM((small_copies, 16, width), F32),
        pltpu.SemaphoreType.DMA((2, small_copies)),
        pltpu.VMEM((2, groups, length, width), BF16),
        pltpu.SemaphoreType.DMA((2, 2, groups - 1)),
        pltpu.VMEM((back, tokens, width), BF16),
        pltpu.VMEM((back, tokens, width), BF16),
        pltpu.SemaphoreType.DMA((2, back)),
        pltpu.VMEM((tokens, width), F32),
        pltpu.VMEM((tokens, width), BF16),
        pltpu.VMEM((H, tokens, PAIR), BF16),
        pltpu.VMEM((H, tokens, PAIR), BF16),
        pltpu.VMEM((width, tokens), BF16),
        pltpu.VMEM((width, tokens), BF16),
        pltpu.VMEM((QB, span), F32),
        pltpu.VMEM((QB, span), F32),
        pltpu.VMEM(base.shape, F32),
        pltpu.VMEM((tokens, width), F32),
        pltpu.VMEM((PAIR, tokens), F32),
        pltpu.VMEM((PAIR, tokens), F32),
        pltpu.VMEM((tokens, 2 * width), BF16),
        pltpu.VMEM((width, 2 * width), F32),
    ]
    vmem = pl.BlockSpec(memory_space=pltpu.VMEM)
    return pl.pallas_call(
        functools.partial(rest_kernel, back),
        in_specs=[vmem] * 17,
        out_specs=[vmem] * len(out_shapes),
        out_shape=out_shapes,
        scratch_shapes=scratch,
        compiler_params=pltpu.CompilerParams(collective_id=1, has_side_effects=True, vmem_limit_bytes=VMEM_LIMIT),
        name="rest",
    )(x, g, gains, wqkv, wout, wup, wdown, rows, base, hot, q, qx, k, kx, v, att, lse)


def finish_kernel(deal_ref, down, up, out, qkv, ret_out, ret_grad, *outs):
    o_out, o_grad, o_qkv, o_wout, o_up, o_down = outs
    length = ret_out.shape[1]
    for g in range(ret_out.shape[0]):
        piece = deal_ref[0, g]
        o_out[pl.ds(g * length, length), :] = ret_out[piece]
        o_grad[pl.ds(g * length, length), :] = ret_grad[piece]
    for source, target in ((down, o_down), (up, o_up), (out, o_wout), (qkv, o_qkv)):
        direct = source.shape[0] * source.shape[1] * source.shape[2] != target.shape[0] * target.shape[1]
        cols = source.shape[2]
        if direct:
            value = add_low(*[source[t] for t in range(source.shape[0])])
        else:
            value = source[...].reshape(-1, cols).astype(F32)
        height = target.shape[0]
        for c in range(target.shape[1] // cols):
            target[:, c * cols : (c + 1) * cols] = value[c * height : (c + 1) * height]


def finish(deal, sums, returned, shapes):
    return pl.pallas_call(
        finish_kernel,
        in_specs=[pl.BlockSpec(memory_space=pltpu.SMEM)] + [pl.BlockSpec(memory_space=pltpu.VMEM)] * 6,
        out_specs=[pl.BlockSpec(memory_space=pltpu.VMEM)] * len(shapes),
        out_shape=shapes,
        compiler_params=pltpu.CompilerParams(vmem_limit_bytes=VMEM_LIMIT),
        name="finish",
    )(deal, *sums, *returned)


def swap_slots(values):
    return lax.all_to_all(values, "dp", split_axis=0, concat_axis=0, tiled=True)


def shards(
    tokens,
    cotangent,
    deal,
    lengths,
    buckets,
    ln1_gain,
    ln1_bias,
    w_qkv,
    w_out,
    rel_bias,
    ln2_gain,
    ln2_bias,
    w_up,
    w_down,
):
    groups = lax.axis_size("dp")
    splits = lax.axis_size("seq")
    tok_dev, width = tokens.shape
    block_len = tok_dev // groups
    maxlen = buckets.shape[0]
    back = -(-maxlen // tok_dev)
    window = (back + 1) * tok_dev
    span = back * tok_dev + QB
    chunk = lax.axis_index("seq")
    deal_row = deal[0]
    shard_rows = ln1_gain.shape[0]

    small = jnp.concatenate([ln1_gain, ln1_bias, ln2_gain, ln2_bias, rel_bias.reshape(-1)])
    wqkv_full = lax.all_gather(w_qkv, "dp", axis=0, tiled=True)
    small_full = lax.all_gather(small, "dp", axis=0, tiled=False)
    wout_full = lax.all_gather(w_out, "dp", axis=0, tiled=True)
    wup_full = lax.all_gather(w_up, "dp", axis=0, tiled=True)
    wdown_full = lax.all_gather(w_down, "dp", axis=0, tiled=True)
    gains = small_full[:, : 4 * shard_rows].reshape(groups, 4, shard_rows).transpose(1, 0, 2).reshape(4, width)
    gain_one, bias_one = (gains[i].astype(F32) for i in range(2))
    rel_full = small_full[:, 4 * shard_rows :].reshape(NBK, H)

    pieces = (groups, block_len, width)
    slot_in, slot_grad = to_slots(deal_row, [tokens.reshape(pieces), cotangent.reshape(pieces)])
    dealt = swap_slots(jnp.stack([slot_in, slot_grad], axis=1))
    x_rows = dealt[:, 0].reshape(tok_dev, width).astype(F32)
    grad_out = dealt[:, 1].reshape(tok_dev, width)

    ends, so_far = [], 0
    for c in range(lengths.shape[1]):
        so_far = so_far + lengths[0, c]
        ends.append(so_far)
    lane = lax.rem(jnp.arange(PAIR, dtype=jnp.int32), HD)[None, :]
    key_pos = (chunk - back) * tok_dev + jnp.arange(window, dtype=jnp.int32)
    key_seg = sum((key_pos >= e).astype(jnp.int32) for e in ends)
    key_seg = jnp.where(key_pos < 0, len(ends), key_seg)[:, None]
    query_seg = key_seg[back * tok_dev :]
    kx = jnp.where((lane == key_seg) | (lane >= HD - 3), 1.0, 0.0).astype(BF16)
    qx = jnp.where((lane <= len(ends)) & (lane != query_seg), BIG, 0.0).astype(BF16)
    offset = jnp.arange(span + QB, dtype=jnp.int32) - QB
    distance = back * tok_dev - offset
    in_reach = (distance >= 0) & (distance < maxlen) & (offset >= 0)
    table_bucket = jnp.concatenate(
        [
            jnp.zeros((QB + back * tok_dev + 1 - maxlen,), jnp.int32),
            buckets[::-1],
            jnp.zeros((QB - 1,), jnp.int32),
        ]
    )
    hot = (table_bucket[:, None] == jnp.arange(PAIR, dtype=jnp.int32)[None, :]) & in_reach[:, None]
    hot = hot.astype(BF16)
    base = jnp.einsum("cb,bh->hc", hot[:, :NBK], rel_full, preferred_element_type=F32)
    base = jnp.where(in_reach[None], base, BIG).reshape(H // 2, 2, span + QB)

    normed_low = norm_rows(x_rows, gain_one, bias_one).astype(BF16)
    earlier = [
        lax.ppermute(normed_low, "seq", [(i, i + step) for i in range(splits - step)]) for step in range(back, 0, -1)
    ]
    scale = HD**-0.5
    own_qkv = jnp.dot(normed_low, wqkv_full, preferred_element_type=F32).astype(BF16)
    rows_before = jnp.concatenate(earlier, axis=0)
    kv_before = jnp.dot(rows_before, wqkv_full[:, width:], preferred_element_type=F32).astype(BF16)
    queries = own_qkv[:, :width] * jnp.asarray(scale, BF16)
    keys_all = jnp.concatenate([kv_before[:, :width], own_qkv[:, width : 2 * width]], axis=0)
    values_all = jnp.concatenate([kv_before[:, width:], own_qkv[:, 2 * width :]], axis=0)
    attended, lse = attention_fwd(base, queries, qx, keys_all, kx, values_all)
    gains_all = jnp.pad(gains.astype(F32), ((0, 4), (0, 0)))
    *sums, small_total, back_out, back_grad = rest(
        back, dealt[:, 0].reshape(tok_dev, width), grad_out, gains_all, wqkv_full, wout_full, wup_full, wdown_full,
        jnp.concatenate([rows_before, normed_low], axis=0), base, hot, queries, qx, keys_all, kx, values_all, attended, lse,
    )
    output, grad_tokens, total_qkv, total_out, total_up, total_down = finish(
        deal,
        sums,
        [back_out, back_grad],
        [
            jax.ShapeDtypeStruct((tok_dev, width), BF16),
            jax.ShapeDtypeStruct((tok_dev, width), BF16),
            jax.ShapeDtypeStruct(w_qkv.shape, F32),
            jax.ShapeDtypeStruct(w_out.shape, F32),
            jax.ShapeDtypeStruct(w_up.shape, F32),
            jax.ShapeDtypeStruct(w_down.shape, F32),
        ],
    )
    slice_of = lax.axis_index("dp")
    cut = [lax.dynamic_slice_in_dim(small_total[i], slice_of * shard_rows, shard_rows) for i in range(4)]
    rel_rows = rel_bias.shape[0]
    total_rel = lax.dynamic_slice_in_dim(small_total[8 : 8 + H, :NBK].T, slice_of * rel_rows, rel_rows)
    return (
        output,
        grad_tokens,
        cut[0],
        cut[1],
        total_qkv,
        total_out,
        total_rel,
        cut[2],
        cut[3],
        total_up,
        total_down,
    )


def solution(mesh):
    by_all, by_dp = P(("seq", "dp"), None), P("dp", None)
    return jax.shard_map(
        shards,
        mesh=mesh,
        in_specs=(
            by_all, by_all, by_all, by_dp, P(), P("dp"), P("dp"), by_dp, by_dp, by_dp, P("dp"), P("dp"), by_dp, by_dp,
        ),
        out_specs=(by_all, by_all, P("dp"), P("dp"), by_dp, by_dp, by_dp, P("dp"), P("dp"), by_dp, by_dp),
        check_vma=False,
    )
```

time: 322 us -> 242 us (0.75)
  matrix products: 48.2 us -> 3.88 us
  local copies, waits for them, and re-layouts: 34.1 us -> 10.6 us
  Pallas kernels: 140 us -> 130 us
  waiting for transfers between devices: 15 us -> 20.5 us
  other arithmetic: 15.1 us -> 11.1 us
  starting transfers between devices: 16.8 us -> 13.2 us
    dot_general x15 -> x1, matrix products: 43.1 us -> 0.25 us  [shards(): jnp.einsum('cb,bh->hc', hot[:, :NBK], rel_full, preferred_element_type=F32)]
    pallas_call x2 -> x1, Pallas kernels: 118 us -> 107 us  [rest(): pl.pallas_call(functools.partial(rest_kernel, back), in_specs=[vmem] * 17...]
    reshape x9 -> x1, local copies, waits for them, and re-layouts: 9.79 us -> 0.65 us  [shards(): base = jnp.where(in_reach[None], base, BIG).reshape(H // 2, 2, span + QB)]
    convert_element_type x5 -> x3, local copies, waits for them, and re-layouts: 5.89 us -> 0.24 us  [the longest x2 0.15 us: shards(): gain_one, bias_one = (gains[i].astype(F32) for i in range(2))]
    ppermute x2, waiting for transfers between devices: 12.9 us -> 18.4 us  [shards(): lax.ppermute(normed_low, 'seq', [(i, i + step) for i in range(splits - st...]
    transpose x1, local copies, waits for them, and re-layouts: 3.41 us -> 0.01 us  [shards(): small_full[:, :4 * shard_rows].reshape(groups, 4, shard_rows)]
  transfers between devices with their start and end apart: 8 -> 6, of which waited for: 2 -> 2; matrix products, arithmetic and copies ran while one was open for 17% -> 8% of each run, Pallas kernels for 6% -> 8%
where the time goes in v3:
time: 242 us; the launch traced here: 241 us
  Pallas kernels  130 us (54%)
  blocking collectives  35.3 us (15%)
  waiting for transfers between devices  20.5 us (8%)
  between operations  16.7 us (7%)
  starting transfers between devices  13.2 us (5%)
  other arithmetic  11.1 us (5%)
  local copies, waits for them, and re-layouts  10.6 us (4%)
  matrix products  3.88 us (2%)
    pallas_call x1, Pallas kernels, rest(): pl.pallas_call(functools.partial(rest_kernel, back), in_specs=[vmem] * 17...  107 us
    unnamed x1, blocking collectives  24 us
    ppermute x2, waiting for transfers between devices, shards(): lax.ppermute(normed_low, 'seq', [(i, i + step) for i in range(splits - st...  18.4 us
    pallas_call x1, Pallas kernels, attention_fwd(): pl.pallas_call(attention_fwd_kernel, grid=(H // 2,), in_specs=[pl.BlockSp...  14 us
    all_gather x1, blocking collectives, shards(): wout_full = lax.all_gather(w_out, 'dp', axis=0, tiled=True)  11.3 us
    ppermute x2, starting transfers between devices, shards(): lax.ppermute(normed_low, 'seq', [(i, i + step) for i in range(splits - st...  7.78 us
    pallas_call x1, Pallas kernels, to_slots(): pl.pallas_call(copy_kernel, grid_spec=pltpu.PrefetchScalarGridSpec(num_sc...  5.72 us
    all_to_all x1, starting transfers between devices, swap_slots(): return lax.all_to_all(values, 'dp', split_axis=0, concat_axis=0, tiled=True)  5.31 us
  transfers between devices with their start and end apart: 6, of which 2 were waited for; matrix products, arithmetic and copies ran while one was open for 8% of the time, Pallas kernels for 8%

profile of v3, /device:TPU:0, one launch (start us, length us, event | category | flops | bytes accessed | tf_op | source)
XLA Modules:
  0.0 241.1 jit_solution(18054400235653145866)
XLA Ops:
  7.2 0.7 all-gather.5.cloned.1.call-update
  8.0 0.7 all-gather.7.cloned.1.call-update
  8.7 5.7 %to_slots.1 = (bf16[8,64,512]{2,1,0:T(8,128)(2,1)}, bf16[8,64,512]{2,1,0:T(8,128)(2,1)}) custom-call(s32[8]{0:T(128)} %bitcast.34, bf16[8,64,512]{2,1,0:T(8,128)(2,1)} %bitcast.28, bf16[8,64,512]{2,1,0:T(8,128)(2,1)} %bitcast.29), custom_call_target="tpu_custom_call" | custom-call | tf_op jit(solution)/shard_map/to_slots/pallas_call | solution.py:124
  14.4 1.3 pad_maximum_fusion.3
  15.7 1.1 copy.28
  16.8 5.3 %all-to-all-start = ((bf16[8,2,64,512]{3,2,1,0:T(8,128)(2,1)}), bf16[8,2,64,512]{3,2,1,0:T(8,128)(2,1)S(1)}, u32[]{:S(2)}, u32[]{:S(2)}) async-start(bf16[8,2,64,512]{3,2,1,0:T(8,128)(2,1)} %copy.28), calls=%async_computation | async-start | bytes 2097152 | tf_op jit(solution)/shard_map/all_to_all | solution.py:678
  22.2 0.7 all-gather.9.cloned.1.call-update
  23.0 0.6 dynamic-slice.8
  24.3 0.1 concatenate.19
  24.4 0.2 dynamic-update-slice
  24.6 24.0 %all-reduce.1 = bf16[2304]{0:T(1024)(128)(2,1)S(1)} all-reduce(bf16[2304]{0:T(1024)(128)(2,1)S(1)} %dynamic-update-slice), channel_id=2, replica_groups=mesh['seq'=4,'dp'=8] {'dp'}, use_global_device_ids=true, to_apply=%add.1 | all-reduce | flops 2304 | bytes 9216
  48.6 0.1 reshape.160
  48.8 0.6 fusion.30
  51.4 0.7 add_select_fusion
  52.2 0.1 convert_element_type.72
  52.3 11.3 %all_gather.21.refs_4_ = bf16[512,512]{1,0:T(8,128)(2,1)} all-gather(bf16[64,512]{1,0:T(8,128)(2,1)S(1)} %copy-done.4), channel_id=1, replica_groups=mesh['seq'=4,'dp'=8] {'dp'}, dimensions={0}, use_global_device_ids=true | all-gather | bytes 589824 | tf_op jit(solution)/shard_map/all_gather | solution.py:712
  63.7 0.8 select_convert_fusion.1.qx_ref.refs_11_
  64.5 1.8 fusion.25
  66.3 0.2 convolution_select_fusion
  66.5 0.6 pad_convert_fusion.refs_2_
  67.3 0.6 reshape.157.base_ref.refs_8_
  68.0 0.1 convert_reduce_fusion
  68.2 0.3 fusion.1
  68.6 0.9 fusion.28
  69.5 0.3 add_convert_fusion
  69.8 4.3 %collective-permute-start = (bf16[512,512]{1,0:T(8,128)(2,1)S(1)}, bf16[512,512]{1,0:T(8,128)(2,1)S(1)}, u32[]{:S(2)}, u32[]{:S(2)}) collective-permute-start(bf16[512,512]{1,0:T(8,128)(2,1)S(1)} %add_convert_fusion), channel_id=1, source_target_pairs={{0,16},{8,24},{1,17},{9,25},{2,18},{10,26},{3,19},{11,27},{4,20},{... | collective-permute-start | bytes 1572872 | tf_op jit(solution)/shard_map/ppermute | solution.py:753
  74.1 3.4 %collective-permute-start.1 = (bf16[512,512]{1,0:T(8,128)(2,1)S(1)}, bf16[512,512]{1,0:T(8,128)(2,1)S(1)}, u32[]{:S(2)}, u32[]{:S(2)}) collective-permute-start(bf16[512,512]{1,0:T(8,128)(2,1)S(1)} %add_convert_fusion), channel_id=1, source_target_pairs={{0,8},{8,16},{16,24},{1,9},{9,17},{17,25},{2,10},{10,18},{18,26},{... | collective-permute-start | bytes 1572872 | tf_op jit(solution)/shard_map/ppermute | solution.py:753
  77.6 1.0 select_convert_fusion.kx_ref.refs_13_
  78.6 7.8 %collective-permute-done = bf16[512,512]{1,0:T(8,128)(2,1)S(1)} collective-permute-done((bf16[512,512]{1,0:T(8,128)(2,1)S(1)}, bf16[512,512]{1,0:T(8,128)(2,1)S(1)}, u32[]{:S(2)}, u32[]{:S(2)}) %collective-permute-start) | collective-permute-done | bytes 524320 | tf_op jit(solution)/shard_map/ppermute | solution.py:753
  86.4 10.7 %collective-permute-done.1 = bf16[512,512]{1,0:T(8,128)(2,1)S(1)} collective-permute-done((bf16[512,512]{1,0:T(8,128)(2,1)S(1)}, bf16[512,512]{1,0:T(8,128)(2,1)S(1)}, u32[]{:S(2)}, u32[]{:S(2)}) %collective-permute-start.1) | collective-permute-done | bytes 524320 | tf_op jit(solution)/shard_map/ppermute | solution.py:753
  97.0 1.3 pad_maximum_fusion.refs_7_
  98.4 2.4 convolution_convert_fusion
  100.8 0.9 fusion.27
  101.7 0.7 copy-done.1
  102.4 0.1 copy-done.3
  102.5 1.2 convolution_convert_fusion.1
  103.7 0.1 fusion.26
  103.9 2.0 pad_maximum_fusion.1
  105.8 14.0 %attention_fwd.1 = (bf16[512,512]{1,0:T(8,128)(2,1)}, f32[512,512]{1,0:T(8,128)}) custom-call(f32[4,2,1536]{2,1,0:T(2,128)} %reshape.157.base_ref.refs_8_, bf16[512,512]{1,0:T(8,128)(2,1)} %get-tuple-element.84.q_ref.refs_10_, bf16[512,128]{1,0:T(8,128)(2,1)} %select_convert_fusion.1.qx_ref.refs_11_, bf16[1536,512]{1,0:T(8,128)(2,1)} %get-tuple-element.96.k_ref.refs_12_, ...), custom_call_target="tpu_custom_call" | custom-call | tf_op jit(solution)/shard_map/attention_fwd/pallas_call | solution.py:90
  119.8 107.1 %rest.1 = (bf16[4,64,512]{2,1,0:T(8,128)(2,1)}, bf16[4,64,512]{2,1,0:T(8,128)(2,1)}, bf16[4,16,512]{2,1,0:T(8,128)(2,1)}, bf16[4,48,512]{2,1,0:T(8,128)(2,1)}, f...) custom-call(bf16[512,512]{1,0:T(8,128)(2,1)} %bitcast.26, bf16[512,512]{1,0:T(8,128)(2,1)} %bitcast.27, ...), custom_call_target="tpu_custom_call" | custom-call | tf_op jit(solution)/shard_map/rest/pallas_call | solution.py:636
  226.9 0.7 slice.89
  227.6 0.9 fusion.29
  228.5 0.7 copy.30
  229.2 0.6 fusion.20
  229.8 0.6 fusion.21
  230.3 0.6 fusion.22
  230.9 0.6 fusion.23
  231.5 3.0 %finish.1 = (bf16[512,512]{1,0:T(8,128)(2,1)}, bf16[512,512]{1,0:T(8,128)(2,1)}, f32[64,1536]{1,0:T(8,128)}, f32[64,512]{1,0:T(8,128)}, f32[64,2048]{1,0:T(8,128)}, /*index=5*/f32[256,512]{1,0:T(8,128)}) custom-call(s32[1,8]{1,0:T(1,128)} %deal_ref.1, bf16[4,64,512]{2,1,0:T(8,128)(2,1)} %get-tuple-element.32.down, bf16[4,64,512]{2,1,0:T(8,128)(2,1)} %get-tuple-element.33.up, ...), custom_call_target="tpu_custom_call" | custom-call | tf_op jit(solution)/shard_map/finish/pallas_call | solution.py:667
  (55 shorter events, 1.1 us)
Async XLA Ops:
  7.2 91.2 %all-gather.5.cloned.1.call-start = ((), (), s32[]{:S(2)}) async-start(), calls=%async_computation.1 | async-start | bytes 1769472 | tf_op jit(solution)/shard_map/all_gather | solution.py:710
  7.9 111.9 %all-gather.7.cloned.1.call-start = ((), (), s32[]{:S(2)}) async-start(), calls=%async_computation.2 | async-start | bytes 2359296 | tf_op jit(solution)/shard_map/all_gather | solution.py:713
  16.8 6.2 %copy-start.11 = (bf16[4,8]{1,0:T(4,128)(2,1)S(1)}, bf16[4,8]{1,0:T(4,128)(2,1)}, u32[]{:S(2)}) copy-start(bf16[4,8]{1,0:T(4,128)(2,1)} %param.23) | copy-start | bytes 196
  16.8 6.2 %copy-start.12 = (u32[32]{0:T(128)S(1)}, u32[32]{0:T(128)}, u32[]{:S(2)}) copy-start(u32[32]{0:T(128)} %constant.69) | copy-start | bytes 388
  16.8 7.5 %copy-start.7 = (bf16[64]{0:T(256)(128)(2,1)S(1)}, bf16[64]{0:T(256)(128)(2,1)}, u32[]{:S(2)}) copy-start(bf16[64]{0:T(256)(128)(2,1)} %param.19) | copy-start | bytes 388
  16.8 7.5 %copy-start.8 = (bf16[64]{0:T(256)(128)(2,1)S(1)}, bf16[64]{0:T(256)(128)(2,1)}, u32[]{:S(2)}) copy-start(bf16[64]{0:T(256)(128)(2,1)} %param.20) | copy-start | bytes 388
  16.8 7.5 %copy-start.9 = (bf16[64]{0:T(256)(128)(2,1)S(1)}, bf16[64]{0:T(256)(128)(2,1)}, u32[]{:S(2)}) copy-start(bf16[64]{0:T(256)(128)(2,1)} %param.24) | copy-start | bytes 388
  16.8 7.5 %copy-start.10 = (bf16[64]{0:T(256)(128)(2,1)S(1)}, bf16[64]{0:T(256)(128)(2,1)}, u32[]{:S(2)}) copy-start(bf16[64]{0:T(256)(128)(2,1)} %param.25) | copy-start | bytes 388
  16.8 32.0 %copy-start.5 = (s32[1,3]{1,0:T(1,128)S(1)}, s32[1,3]{1,0:T(1,128)}, u32[]{:S(2)}) copy-start(s32[1,3]{1,0:T(1,128)} %param.17) | copy-start | bytes 40
  16.8 35.3 %copy-start.6 = (s32[1024]{0:T(1024)S(1)}, s32[1024]{0:T(1024)}, u32[]{:S(2)}) copy-start(s32[1024]{0:T(1024)} %param.18) | copy-start | bytes 12292
  16.8 35.5 %copy-start.4 = (bf16[64,512]{1,0:T(8,128)(2,1)S(1)}, bf16[64,512]{1,0:T(8,128)(2,1)}, u32[]{:S(2)}) copy-start(bf16[64,512]{1,0:T(8,128)(2,1)} %param.22) | copy-start | bytes 196612
  16.8 51.1 %all-to-all-start = ((bf16[8,2,64,512]{3,2,1,0:T(8,128)(2,1)}), bf16[8,2,64,512]{3,2,1,0:T(8,128)(2,1)S(1)}, u32[]{:S(2)}, u32[]{:S(2)}) async-start(bf16[8,2,64,512]{3,2,1,0:T(8,128)(2,1)} %copy.28), calls=%async_computation | async-start | bytes 2097152 | tf_op jit(solution)/shard_map/all_to_all | solution.py:678
  22.1 97.7 %all-gather.9.cloned.1.call-start = ((), (), s32[]{:S(2)}) async-start(), calls=%async_computation.3 | async-start | bytes 2359296 | tf_op jit(solution)/shard_map/all_gather | solution.py:714
  69.5 28.9 %copy-start = (bf16[8,1,64,512]{3,2,1,0:T(8,128)(2,1)}, bf16[8,1,64,512]{3,2,1,0:T(8,128)(2,1)S(1)}, u32[]{:S(2)}) copy-start(bf16[8,1,64,512]{3,2,1,0:T(8,128)(2,1)S(1)} %get-tuple-element.86) | copy-start | bytes 1572868
  69.8 16.6 %collective-permute-start = (bf16[512,512]{1,0:T(8,128)(2,1)S(1)}, bf16[512,512]{1,0:T(8,128)(2,1)S(1)}, u32[]{:S(2)}, u32[]{:S(2)}) collective-permute-start(bf16[512,512]{1,0:T(8,128)(2,1)S(1)} %add_convert_fusion), channel_id=1, source_target_pairs={{0,16},{8,24},{1,17},{9,25},{2,18},{10,26},{3,19},{11,27},{4,20},{... | collective-permute-start | bytes 1572872 | tf_op jit(solution)/shard_map/ppermute | solution.py:753
  74.1 22.9 %collective-permute-start.1 = (bf16[512,512]{1,0:T(8,128)(2,1)S(1)}, bf16[512,512]{1,0:T(8,128)(2,1)S(1)}, u32[]{:S(2)}, u32[]{:S(2)}) collective-permute-start(bf16[512,512]{1,0:T(8,128)(2,1)S(1)} %add_convert_fusion), channel_id=1, source_target_pairs={{0,8},{8,16},{16,24},{1,9},{9,17},{17,25},{2,10},{10,18},{18,26},{... | collective-permute-start | bytes 1572872 | tf_op jit(solution)/shard_map/ppermute | solution.py:753
  97.0 1.3 copy-start.2
  100.8 1.6 copy-start.1
  100.8 1.7 copy-start.3
Sparse Core Ops, SparseCore 0:
  9.9 32.4 all-gather.4
  44.2 28.8 all-gather.6
  75.0 27.8 all-gather.8

commit v4 on v3

--- a/solution.py
+++ b/solution.py
@@ -29,106 +29,9 @@
     return lax.dot_general(a, b, NN, preferred_element_type=F32)
 
 
-def norm_rows(values, gain_vec, bias_vec):
-    average = jnp.mean(values, axis=-1, keepdims=True)
-    centred = values - average
-    variance = jnp.mean(centred * centred, axis=-1, keepdims=True)
-    return centred * lax.rsqrt(variance + 1e-05) * gain_vec + bias_vec
-
-
 def toeplitz(row):
     width = row.shape[1]
     return pltpu.roll(jnp.broadcast_to(row, (QB, width)), 0, 1, stride=1, stride_axis=0)[:, QB:]
-
-
-def attention_fwd_kernel(base_ref, q_ref, qx_ref, k_ref, kx_ref, v_ref, att_ref, lse_ref, bias, kaug, vaug, scores):
-    rows = q_ref.shape[0]
-    tiles = base_ref.shape[-1] // QB - 1
-    lane_q = lax.broadcasted_iota(jnp.int32, (QB, PAIR), 1) < HD
-    lane_k = lax.broadcasted_iota(jnp.int32, k_ref.shape, 1) < HD
-    for h in range(2):
-        mine_k = lane_k if h == 0 else jnp.logical_not(lane_k)
-        mine_q = lane_q if h == 0 else jnp.logical_not(lane_q)
-        bias[...] = toeplitz(base_ref[0, h : h + 1, :])
-        kaug[...] = jnp.where(mine_k, k_ref[...], kx_ref[...])
-        vaug[...] = jnp.where(mine_k, v_ref[...], jnp.ones_like(v_ref))
-        for b in range(rows // QB):
-            here = pl.ds(b * QB, QB)
-            q_aug = jnp.where(mine_q, q_ref[here, :], qx_ref[here, :])
-            top = None
-            for j in range(tiles):
-                cols = pl.ds(j * QB, QB)
-                s = dot_nt(q_aug, kaug[pl.ds((b + j) * QB, QB), :]) + bias[:, cols]
-                scores[:, cols] = s
-                most = jnp.maximum(s[:, :128], s[:, 128:])
-                top = most if top is None else jnp.maximum(top, most)
-            top = jnp.max(top, axis=1, keepdims=True)
-            acc = jnp.zeros((QB, PAIR), F32)
-            for j in range(tiles):
-                p = jnp.exp(scores[:, pl.ds(j * QB, QB)] - top).astype(BF16)
-                acc = acc + dot_nn(p, vaug[pl.ds((b + j) * QB, QB), :])
-            att = acc / pltpu.roll(acc, HD, 1)
-            lse = top + jnp.log(acc)
-            if h == 0:
-                att_ref[here, :] = att.astype(BF16)
-                lse_ref[here, :] = lse
-            else:
-                att_ref[here, :] = jnp.where(mine_q, att.astype(BF16), att_ref[here, :])
-                lse_ref[here, :] = jnp.where(mine_q, lse_ref[here, :], lse)
-
-
-def column_block(rows):
-    return pl.BlockSpec((rows, PAIR), lambda i: (0, i))
-
-
-def whole_block(rows):
-    return pl.BlockSpec((rows, PAIR), lambda i: (0, 0))
-
-
-def attention_fwd(base, q, qx, k, kx, v):
-    rows, width, window = q.shape[0], base.shape[-1], k.shape[0]
-    return pl.pallas_call(
-        attention_fwd_kernel,
-        grid=(H // 2,),
-        in_specs=[
-            pl.BlockSpec((1, 2, width), lambda i: (i, 0, 0)),
-            column_block(rows),
-            whole_block(rows),
-            column_block(window),
-            whole_block(window),
-            column_block(window),
-        ],
-        out_specs=[column_block(rows), column_block(rows)],
-        out_shape=[jax.ShapeDtypeStruct(q.shape, BF16), jax.ShapeDtypeStruct(q.shape, F32)],
-        scratch_shapes=[
-            pltpu.VMEM((QB, width - QB), F32),
-            pltpu.VMEM((window, PAIR), BF16),
-            pltpu.VMEM((window, PAIR), BF16),
-            pltpu.VMEM((QB, width - QB), F32),
-        ],
-        compiler_params=pltpu.CompilerParams(vmem_limit_bytes=VMEM_LIMIT),
-        name="attention_fwd",
-    )(base, q, qx, k, kx, v)
-
-
-def copy_kernel(deal_ref, *refs):
-    count = len(refs) // 2
-    for i in range(count):
-        refs[count + i][...] = refs[i][...]
-
-
-def to_slots(deal_row, arrays):
-    groups, length, width = arrays[0].shape
-    spec_in = pl.BlockSpec((1, length, width), lambda g, deal: (g, 0, 0))
-    spec_out = pl.BlockSpec((1, length, width), lambda g, deal: (deal[g], 0, 0))
-    return pl.pallas_call(
-        copy_kernel,
-        grid_spec=pltpu.PrefetchScalarGridSpec(
-            num_scalar_prefetch=1, grid=(groups,), in_specs=[spec_in] * len(arrays), out_specs=[spec_out] * len(arrays)
-        ),
-        out_shape=[jax.ShapeDtypeStruct(a.shape, a.dtype) for a in arrays],
-        name="to_slots",
-    )(deal_row, *arrays)
 
 
 def add_low(first, *others):
@@ -318,13 +221,59 @@
     return spans
 
 
-def rest_kernel(back, *refs):
+class Gather:
+    def __init__(self, shard, full, sems, own_sem):
+        self.shard, self.full, self.sems = shard, full, sems
+        self.rows = shard.shape[0]
+        self.dp = lax.axis_index("dp")
+        self.pairs = lax.axis_size("dp") // 2
+        self.core, self.chip = lax.rem(self.dp, 2), self.dp // 2
+        self.sibling = {"dp": self.dp + 1 - 2 * self.core}
+        self.own = pltpu.make_async_copy(shard, self.place(self.dp), own_sem)
+
+    def place(self, owner):
+        return self.full.at[pl.ds(pl.multiple_of(owner * self.rows, self.rows), self.rows)]
+
+    def copy(self, src, owner, slot, device):
+        return pltpu.make_async_remote_copy(
+            src_ref=src, dst_ref=self.place(owner), send_sem=self.sems.at[0, slot], recv_sem=self.sems.at[1, slot],
+            device_id=device, device_id_type=pl.DeviceIdType.MESH,
+        )
+
+    def start(self):
+        self.sent = [
+            self.copy(self.shard, self.dp, step, {"dp": 2 * lax.rem(self.chip + step, self.pairs) + self.core})
+            for step in range(1, self.pairs)
+        ]
+        self.near = self.copy(self.shard, self.dp, 0, self.sibling)
+        for copy in self.sent + [self.near]:
+            copy.start()
+        self.own.start()
+
+    def relay(self):
+        self.relayed = []
+        for step in range(1, self.pairs):
+            self.sent[step - 1].wait_recv()
+            owner = 2 * lax.rem(self.chip + self.pairs - step, self.pairs) + self.core
+            self.relayed.append(self.copy(self.place(owner), owner, self.pairs - 1 + step, self.sibling))
+            self.relayed[-1].start()
+
+    def arrive(self):
+        self.own.wait()
+        for copy in [self.near] + self.relayed:
+            copy.wait_recv()
+
+    def finish(self):
+        for copy in self.sent + [self.near] + self.relayed:
+            copy.wait_send()
+
+
+def layer_kernel(back, maxlen, *refs):
     (
-        x_ref, g_ref, gains_ref, wqkv_ref, wout_ref, wup_ref, wdown_ref, rows_ref,
-        base_ref, hot_hi_ref, q_ref, qx_ref, k_ref, kx_ref, v_ref, att_ref, lse_ref,
-    ) = refs[:17]
-    sum_down, sum_up, sum_out, sum_qkv, small_out, ret_out, ret_grad = refs[17:24]
-    it = iter(refs[24:])
+        tokens_ref, cotangent_ref, deal_ref, small_in, wqkv_s, wout_s, wup_s, wdown_s, hot_ref, qx_ref, kx_ref,
+    ) = refs[:11]
+    sum_down, sum_up, sum_out, sum_qkv, small_out, ret_out, ret_grad = refs[11:18]
+    it = iter(refs[18:])
     sources = [next(it) for _ in range(4)]
     summers = [
         Summer(source, *[next(it) for _ in range(4)], out, next(it))
@@ -335,13 +284,177 @@
     slots, ret_sems, halo_send, halo_land, halo_sems = (next(it) for _ in range(5))
     dres_ref, do_ref, qaug, doaug, q_t, do_t = (next(it) for _ in range(6))
     bias, dsum, dd, dq_acc, dkt, dvt, dkv, gkv = (next(it) for _ in range(8))
+    xwin, g_ref, wqkv_ref, wout_ref, wup_ref, wdown_ref = (next(it) for _ in range(6))
+    gather_sems, own_sems, deal_sems, row_sems, few_land, few_sems = (next(it) for _ in range(6))
+    gains_ref, base_ref, q_ref, k_ref, v_ref, att_ref, lse_ref = (next(it) for _ in range(7))
     dp, groups = lax.axis_index("dp"), lax.axis_size("dp")
     seq, splits = lax.axis_index("seq"), lax.axis_size("seq")
-    tokens, width = x_ref.shape
+    tokens, width = tokens_ref.shape
     length = tokens // groups
     per_chunk = tokens // QB
     tiles = base_ref.shape[-1] // QB - 1
+    spans = phase_spans(back, per_chunk, tiles)
+    mesh_ids = pl.DeviceIdType.MESH
     greet(others("dp") + others("seq"))
+
+    def deal_out(which, source, target, first_row):
+        for j in range(groups):
+            piece = source[:length, :]
+            for k in range(1, groups):
+                piece = jnp.where(deal_ref[0, k] == j, source[k * length : (k + 1) * length, :], piece)
+            slots[which, j] = piece
+        copies = []
+        rows_here = pl.ds(pl.multiple_of(first_row + dp * length, length), length)
+        for step in range(1, groups):
+            peer = lax.rem(dp + step, groups)
+            copy = pltpu.make_async_remote_copy(
+                src_ref=slots.at[which, peer], dst_ref=target.at[rows_here],
+                send_sem=deal_sems.at[0, which, step - 1], recv_sem=deal_sems.at[1, which, step - 1],
+                device_id={"dp": peer}, device_id_type=mesh_ids,
+            )
+            copy.start()
+            copies.append(copy)
+        target[rows_here, :] = slots[which, dp]
+        return copies
+
+    own_first = back * tokens
+    own_rows = pl.ds(own_first, tokens)
+    dealt = deal_out(0, tokens_ref, xwin, own_first)
+    few = []
+    for step in range(1, groups):
+        copy = pltpu.make_async_remote_copy(
+            src_ref=small_in, dst_ref=few_land.at[step - 1],
+            send_sem=few_sems.at[0, step - 1], recv_sem=few_sems.at[1, step - 1],
+            device_id={"dp": lax.rem(dp + step, groups)}, device_id_type=mesh_ids,
+        )
+        copy.start()
+        few.append(copy)
+    gathers = [
+        Gather(shard, full, gather_sems.at[i], own_sems.at[i])
+        for i, (shard, full) in enumerate(
+            ((wqkv_s, wqkv_ref), (wout_s, wout_ref), (wup_s, wup_ref), (wdown_s, wdown_ref))
+        )
+    ]
+    gathers[0].start()
+    for copy in dealt:
+        copy.wait_recv()
+
+    def row_copy(step):
+        return pltpu.make_async_remote_copy(
+            src_ref=xwin.at[pl.ds((back - step + 1) * tokens, tokens)],
+            dst_ref=xwin.at[pl.ds((back - step) * tokens, tokens)],
+            send_sem=row_sems.at[0, step - 1], recv_sem=row_sems.at[1, step - 1],
+            device_id={"seq": lax.rem(seq + 1, splits)}, device_id_type=mesh_ids,
+        )
+
+    def row_send(step):
+        @pl.when((seq + 1 < splits) & (seq + 1 >= step))
+        def _():
+            row_copy(step).start()
+
+    def row_wait(step):
+        @pl.when(seq >= step)
+        def _():
+            row_copy(step).wait_recv()
+
+    row_send(1)
+    dealt_grad = deal_out(1, cotangent_ref, g_ref, 0)
+    for gather in gathers[1:]:
+        gather.start()
+    little = small_in[...].astype(F32)
+    for step in range(1, groups):
+        few[step - 1].wait_recv()
+        little = little + few_land[step - 1].astype(F32)
+    gains_ref[...] = little[:8]
+    reach = lax.broadcasted_iota(jnp.int32, (H, base_ref.shape[-1]), 1) - QB
+    far = back * tokens - reach
+    table = dot_nt(little[8 : 8 + H, :PAIR].astype(BF16), hot_ref[...])
+    base_ref[...] = jnp.where((far >= 0) & (far < maxlen) & (reach >= 0), table, BIG).reshape(base_ref.shape)
+
+    def first_norm(chunk):
+        normal, _ = norm_stats(xwin[chunk * tokens : (chunk + 1) * tokens, :].astype(F32))
+        return (normal * gains_ref[0:1, :] + gains_ref[1:2, :]).astype(BF16)
+
+    own_normed = first_norm(back)
+    gathers[0].relay()
+    gathers[0].arrive()
+    q_ref[...] = (dot_nn(own_normed, wqkv_ref[:, :width])).astype(BF16) * jnp.asarray(HD**-0.5, BF16)
+    k_ref[own_rows, :] = dot_nn(own_normed, wqkv_ref[:, width : 2 * width]).astype(BF16)
+    v_ref[own_rows, :] = dot_nn(own_normed, wqkv_ref[:, 2 * width :]).astype(BF16)
+
+    low_tile = lax.broadcasted_iota(jnp.int32, (QB, PAIR), 1) < HD
+
+    def look(chunk, first, count, jobs):
+        span = count * QB
+        keys = pl.ds(chunk * tokens, tokens)
+        started, last = chunk < back, chunk == 0
+
+        def body(pair, _):
+            cols = pl.ds(pl.multiple_of(pair * PAIR, PAIR), PAIR)
+            k_pair, v_pair, kx = k_ref[keys, cols], v_ref[keys, cols], kx_ref[keys, :]
+            low_k = lax.broadcasted_iota(jnp.int32, (tokens, PAIR), 1) < HD
+            for h in range(2):
+                mine_k = low_k if h == 0 else jnp.logical_not(low_k)
+                mine = low_tile if h == 0 else jnp.logical_not(low_tile)
+                bias[:, :span] = toeplitz(base_ref[pair, h : h + 1, first * QB : (first + count + 1) * QB])
+                k_aug = jnp.where(mine_k, k_pair, kx)
+                v_aug = jnp.where(mine_k, v_pair, jnp.ones_like(v_pair))
+                held = pl.ds(pl.multiple_of((2 * pair + h) * PAIR, PAIR), PAIR)
+                for b in range(per_chunk):
+                    here = pl.ds(b * QB, QB)
+                    work = [(kt, j - first) for kt, block, j in jobs if block == b]
+                    q_aug = jnp.where(mine, q_ref[here, cols], qx_ref[here, :])
+                    top = None
+                    for kt, j in work:
+                        over = pl.ds(j * QB, QB)
+                        score = dot_nt(q_aug, k_aug[kt * QB : (kt + 1) * QB]) + bias[:, over]
+                        dsum[:, over] = score
+                        most = jnp.maximum(score[:, :128], score[:, 128:])
+                        top = most if top is None else jnp.maximum(top, most)
+                    top = jnp.max(top, axis=1, keepdims=True)
+                    acc = None
+                    if started:
+                        lane_at = HD if h == 0 else 0
+                        before = lse_ref[here, cols][:, lane_at : lane_at + 1]
+                        top = jnp.maximum(top, before)
+                        acc = gkv[here, held] * jnp.exp(before - top)
+                    for kt, j in work:
+                        p = jnp.exp(dsum[:, pl.ds(j * QB, QB)] - top).astype(BF16)
+                        more = dot_nn(p, v_aug[kt * QB : (kt + 1) * QB])
+                        acc = more if acc is None else acc + more
+                    if last:
+                        value = (acc / pltpu.roll(acc, HD, 1)).astype(BF16)
+                        att_ref[here, cols] = value if h == 0 else jnp.where(mine, value, att_ref[here, cols])
+                        stat = top + jnp.log(acc)
+                    else:
+                        gkv[here, held] = acc
+                        stat = jnp.broadcast_to(top, (QB, PAIR))
+                    lse_ref[here, cols] = jnp.where(mine, lse_ref[here, cols], stat)
+            return _
+
+        lax.fori_loop(0, H // 2, body, 0)
+
+    for chunk, first, count, jobs in reversed(spans):
+        step = back - chunk
+        if step > 0:
+            row_wait(step)
+            if step < back:
+                row_send(step + 1)
+            normed = jnp.where(seq >= step, first_norm(chunk).astype(F32), 0.0).astype(BF16)
+            here = pl.ds(chunk * tokens, tokens)
+            k_ref[here, :] = dot_nn(normed, wqkv_ref[:, width : 2 * width]).astype(BF16)
+            v_ref[here, :] = dot_nn(normed, wqkv_ref[:, 2 * width :]).astype(BF16)
+        look(chunk, first, count, jobs)
+        if step == 0:
+            gathers[1].relay()
+            gathers[2].relay()
+    gathers[3].relay()
+    for gather in gathers[1:]:
+        gather.arrive()
+    for copy in dealt_grad:
+        copy.wait_recv()
+    for copy in dealt + dealt_grad:
+        copy.wait_send()
 
     returns = []
 
@@ -352,12 +465,12 @@
             copy = pltpu.make_async_remote_copy(
                 src_ref=slots.at[which, peer], dst_ref=landed.at[dp],
                 send_sem=ret_sems.at[0, which, step - 1], recv_sem=ret_sems.at[1, which, step - 1],
-                device_id={"dp": peer}, device_id_type=pl.DeviceIdType.MESH,
+                device_id={"dp": peer}, device_id_type=mesh_ids,
             )
             copy.start()
             returns.append(copy)
 
-    resid = x_ref[...].astype(F32) + dot_nn(att_ref[...], wout_ref[...])
+    resid = xwin[own_rows, :].astype(F32) + dot_nn(att_ref[...], wout_ref[...])
     normal, scale = norm_stats(resid)
     gain_two = gains_ref[2:3, :]
     a2 = (normal * gain_two + gains_ref[3:4, :]).astype(BF16)
@@ -504,11 +617,14 @@
         )
 
     grad_normed = None
-    for index, (chunk, first, count, jobs) in enumerate(phase_spans(back, per_chunk, tiles)):
+    for index, (chunk, first, count, jobs) in enumerate(spans):
         attend(chunk, first, count, jobs)
         step = back - chunk
         part = dot_nt(dkv[...], wqkv_ref[:, width:])
-        rows_t = flip(rows_ref[chunk * tokens : (chunk + 1) * tokens, :])
+        rows_t = first_norm(chunk)
+        if step > 0:
+            rows_t = jnp.where(seq >= step, rows_t.astype(F32), 0.0)
+        rows_t = flip(rows_t)
         if index == 0:
             gkv[...] = dot_nn(rows_t, dkv[...])
         else:
@@ -553,14 +669,14 @@
         halo_copy(1).wait_recv()
 
     grad_normed = grad_normed + jnp.where(seq + 1 < splits, halo_land[0].astype(F32), 0.0)
-    normal, scale = norm_stats(x_ref[...].astype(F32))
+    normal, scale = norm_stats(xwin[own_rows, :].astype(F32))
     small_ref[0, 0:1, :] = jnp.sum(grad_normed * normal, axis=0, keepdims=True)
     small_ref[0, 1:2, :] = jnp.sum(grad_normed, axis=0, keepdims=True)
     small_ref[0, 4:8, :] = jnp.zeros((4, width), F32)
     dd_all = dd[...].reshape(H, dd.shape[-1])
     dd_hi = dd_all.astype(BF16)
     dd_mid = (dd_all - dd_hi.astype(F32)).astype(BF16)
-    small_ref[0, 8:16, :PAIR] = dot_nn(dd_hi, hot_hi_ref[...]) + dot_nn(dd_mid, hot_hi_ref[...])
+    small_ref[0, 8:16, :PAIR] = dot_nn(dd_hi, hot_ref[...]) + dot_nn(dd_mid, hot_ref[...])
     small_ref[0, 8:16, PAIR:] = jnp.zeros((8, width - PAIR), F32)
     small = SmallSummer(small_ref, small_land, small_sems)
     small.pair()
@@ -584,6 +700,15 @@
     small.finish()
     for copy in returns:
         copy.wait()
+    for gather in gathers:
+        gather.finish()
+    for copy in few:
+        copy.wait_send()
+    for step in range(1, back + 1):
+
+        @pl.when((seq + 1 < splits) & (seq + 1 >= step))
+        def _(step=step):
+            row_copy(step).wait_send()
     for step in range(1, back + 1):
 
         @pl.when(seq >= step)
@@ -591,13 +716,14 @@
             halo_copy(step).wait_send()
 
 
-def rest(back, x, g, gains, wqkv, wout, wup, wdown, rows, base, hot, q, qx, k, kx, v, att, lse):
+def layer(back, maxlen, tokens_in, cotangent, deal, small, wqkv, wout, wup, wdown, hot, qx, kx):
     splits, groups = lax.axis_size("seq"), lax.axis_size("dp")
-    tokens, width = x.shape
+    tokens, width = tokens_in.shape
     length = tokens // groups
     per_chunk = tokens // QB
-    span = max(count for _, _, count, _ in phase_spans(back, per_chunk, base.shape[-1] // QB - 1)) * QB
-    grads = [(wdown.shape[0] // groups), (wup.shape[1] // groups), width // groups, 3 * width // groups]
+    window, reach = kx.shape[0], hot.shape[0]
+    span = max(count for _, _, count, _ in phase_spans(back, per_chunk, reach // QB - 1)) * QB
+    grads = [wdown.shape[0], wup.shape[0] * wup.shape[1] // width, width // groups, 3 * width // groups]
     out_shapes, more, sources = [], [], []
     for height in grads:
         shape = (groups, height, width)
@@ -625,23 +751,42 @@
         pltpu.VMEM((width, tokens), BF16),
         pltpu.VMEM((QB, span), F32),
         pltpu.VMEM((QB, span), F32),
-        pltpu.VMEM(base.shape, F32),
+        pltpu.VMEM((H // 2, 2, reach), F32),
         pltpu.VMEM((tokens, width), F32),
         pltpu.VMEM((PAIR, tokens), F32),
         pltpu.VMEM((PAIR, tokens), F32),
         pltpu.VMEM((tokens, 2 * width), BF16),
         pltpu.VMEM((width, 2 * width), F32),
+        pltpu.VMEM((window, width), BF16),
+        pltpu.VMEM((tokens, width), BF16),
+        pltpu.VMEM((width, 3 * width), BF16),
+        pltpu.VMEM((width, width), BF16),
+        pltpu.VMEM((width, wup.shape[1]), BF16),
+        pltpu.VMEM((wup.shape[1], width), BF16),
+        pltpu.SemaphoreType.DMA((4, 2, groups - 1)),
+        pltpu.SemaphoreType.DMA((4,)),
+        pltpu.SemaphoreType.DMA((2, 2, groups - 1)),
+        pltpu.SemaphoreType.DMA((2, back)),
+        pltpu.VMEM((groups - 1, 16, width), BF16),
+        pltpu.SemaphoreType.DMA((2, groups - 1)),
+        pltpu.VMEM((8, width), F32),
+        pltpu.VMEM((H // 2, 2, reach), F32),
+        pltpu.VMEM((tokens, width), BF16),
+        pltpu.VMEM((window, width), BF16),
+        pltpu.VMEM((window, width), BF16),
+        pltpu.VMEM((tokens, width), BF16),
+        pltpu.VMEM((tokens, width), F32),
     ]
     vmem = pl.BlockSpec(memory_space=pltpu.VMEM)
     return pl.pallas_call(
-        functools.partial(rest_kernel, back),
-        in_specs=[vmem] * 17,
+        functools.partial(layer_kernel, back, maxlen),
+        in_specs=[vmem, vmem, pl.BlockSpec(memory_space=pltpu.SMEM), vmem] + [pl.BlockSpec(memory_space=pl.ANY)] * 4 + [vmem] * 3,
         out_specs=[vmem] * len(out_shapes),
         out_shape=out_shapes,
         scratch_shapes=scratch,
         compiler_params=pltpu.CompilerParams(collective_id=1, has_side_effects=True, vmem_limit_bytes=VMEM_LIMIT),
-        name="rest",
-    )(x, g, gains, wqkv, wout, wup, wdown, rows, base, hot, q, qx, k, kx, v, att, lse)
+        name="layer",
+    )(tokens_in, cotangent, deal, small, wqkv, wout, wup, wdown, hot, qx, kx)
 
 
 def finish_kernel(deal_ref, down, up, out, qkv, ret_out, ret_grad, *outs):
@@ -672,10 +817,6 @@
         compiler_params=pltpu.CompilerParams(vmem_limit_bytes=VMEM_LIMIT),
         name="finish",
     )(deal, *sums, *returned)
-
-
-def swap_slots(values):
-    return lax.all_to_all(values, "dp", split_axis=0, concat_axis=0, tiled=True)
 
 
 def shards(
@@ -697,30 +838,20 @@
     groups = lax.axis_size("dp")
     splits = lax.axis_size("seq")
     tok_dev, width = tokens.shape
-    block_len = tok_dev // groups
     maxlen = buckets.shape[0]
     back = -(-maxlen // tok_dev)
     window = (back + 1) * tok_dev
     span = back * tok_dev + QB
     chunk = lax.axis_index("seq")
-    deal_row = deal[0]
     shard_rows = ln1_gain.shape[0]
 
-    small = jnp.concatenate([ln1_gain, ln1_bias, ln2_gain, ln2_bias, rel_bias.reshape(-1)])
-    wqkv_full = lax.all_gather(w_qkv, "dp", axis=0, tiled=True)
-    small_full = lax.all_gather(small, "dp", axis=0, tiled=False)
-    wout_full = lax.all_gather(w_out, "dp", axis=0, tiled=True)
-    wup_full = lax.all_gather(w_up, "dp", axis=0, tiled=True)
-    wdown_full = lax.all_gather(w_down, "dp", axis=0, tiled=True)
-    gains = small_full[:, : 4 * shard_rows].reshape(groups, 4, shard_rows).transpose(1, 0, 2).reshape(4, width)
-    gain_one, bias_one = (gains[i].astype(F32) for i in range(2))
-    rel_full = small_full[:, 4 * shard_rows :].reshape(NBK, H)
-
-    pieces = (groups, block_len, width)
-    slot_in, slot_grad = to_slots(deal_row, [tokens.reshape(pieces), cotangent.reshape(pieces)])
-    dealt = swap_slots(jnp.stack([slot_in, slot_grad], axis=1))
-    x_rows = dealt[:, 0].reshape(tok_dev, width).astype(F32)
-    grad_out = dealt[:, 1].reshape(tok_dev, width)
+    slice_of = lax.axis_index("dp")
+    vectors = jnp.stack([jnp.tile(v, groups) for v in (ln1_gain, ln1_bias, ln2_gain, ln2_bias)])
+    vectors = jnp.where(jnp.arange(width)[None, :] // shard_rows == slice_of, vectors, 0)
+    rel_rows = rel_bias.shape[0]
+    scores = jnp.tile(rel_bias.T, (1, groups))
+    scores = jnp.where(jnp.arange(NBK)[None, :] // rel_rows == slice_of, scores, 0)
+    small = jnp.concatenate([jnp.pad(vectors, ((0, 4), (0, 0))), jnp.pad(scores, ((0, 0), (0, width - NBK)))], axis=0)
 
     ends, so_far = [], 0
     for c in range(lengths.shape[1]):
@@ -745,25 +876,8 @@
     )
     hot = (table_bucket[:, None] == jnp.arange(PAIR, dtype=jnp.int32)[None, :]) & in_reach[:, None]
     hot = hot.astype(BF16)
-    base = jnp.einsum("cb,bh->hc", hot[:, :NBK], rel_full, preferred_element_type=F32)
-    base = jnp.where(in_reach[None], base, BIG).reshape(H // 2, 2, span + QB)
-
-    normed_low = norm_rows(x_rows, gain_one, bias_one).astype(BF16)
-    earlier = [
-        lax.ppermute(normed_low, "seq", [(i, i + step) for i in range(splits - step)]) for step in range(back, 0, -1)
-    ]
-    scale = HD**-0.5
-    own_qkv = jnp.dot(normed_low, wqkv_full, preferred_element_type=F32).astype(BF16)
-    rows_before = jnp.concatenate(earlier, axis=0)
-    kv_before = jnp.dot(rows_before, wqkv_full[:, width:], preferred_element_type=F32).astype(BF16)
-    queries = own_qkv[:, :width] * jnp.asarray(scale, BF16)
-    keys_all = jnp.concatenate([kv_before[:, :width], own_qkv[:, width : 2 * width]], axis=0)
-    values_all = jnp.concatenate([kv_before[:, width:], own_qkv[:, 2 * width :]], axis=0)
-    attended, lse = attention_fwd(base, queries, qx, keys_all, kx, values_all)
-    gains_all = jnp.pad(gains.astype(F32), ((0, 4), (0, 0)))
-    *sums, small_total, back_out, back_grad = rest(
-        back, dealt[:, 0].reshape(tok_dev, width), grad_out, gains_all, wqkv_full, wout_full, wup_full, wdown_full,
-        jnp.concatenate([rows_before, normed_low], axis=0), base, hot, queries, qx, keys_all, kx, values_all, attended, lse,
+    *sums, small_total, back_out, back_grad = layer(
+        back, maxlen, tokens, cotangent, deal, small, w_qkv, w_out, w_up, w_down, hot, qx, kx
     )
     output, grad_tokens, total_qkv, total_out, total_up, total_down = finish(
         deal,
@@ -778,9 +892,7 @@
             jax.ShapeDtypeStruct(w_down.shape, F32),
         ],
     )
-    slice_of = lax.axis_index("dp")
     cut = [lax.dynamic_slice_in_dim(small_total[i], slice_of * shard_rows, shard_rows) for i in range(4)]
-    rel_rows = rel_bias.shape[0]
     total_rel = lax.dynamic_slice_in_dim(small_total[8 : 8 + H, :NBK].T, slice_of * rel_rows, rel_rows)
     return (
         output,

time: 242 us -> 175 us (0.72)
  the two profiles are of different devices: /device:TPU:0 before, /device:TPU:29 now
where the time goes in v4:
time: 175 us
  Pallas kernels  159 us (91%)
  local copies, waits for them, and re-layouts  8.3 us (5%)
  other arithmetic  4.86 us (3%)
  between operations  2.73 us (2%)
    pallas_call x1, Pallas kernels, layer(): pl.pallas_call(functools.partial(layer_kernel, back, maxlen), in_specs=[v...  156 us
    unnamed x15, local copies, waits for them, and re-layouts  4.32 us

profile of v4, /device:TPU:29, one launch (start us, length us, event | category | flops | bytes accessed | tf_op | source)
XLA Modules:
  0.0 174.8 jit_solution(9814032573874877731)
XLA Ops:
  0.7 0.0 copy-start
  0.7 0.6 copy-done
  1.4 0.6 fusion.25
  3.2 0.0 copy-start.3
  3.9 0.0 copy-done.3
  3.9 0.0 copy-start.4
  3.9 0.1 stack_tile.12
  4.0 0.6 copy-done.4
  4.6 0.0 copy-start.5
  4.6 0.1 stack_tile.13
  4.7 0.6 copy-done.5
  5.3 0.0 copy-start.6
  5.3 0.1 stack_tile.14
  5.3 0.6 copy-done.6
  5.9 0.1 stack_tile.15
  6.0 0.0 copy-start.1
  6.0 0.6 copy-done.1
  6.7 0.1 rev.3
  6.8 0.1 concatenate.7
  6.9 0.7 add_select_fusion
  7.5 0.0 copy-start.2
  7.5 0.7 copy-done.2
  8.2 0.1 copy.27
  8.3 0.6 fusion.4.refs_3_
  8.9 0.8 select_convert_fusion.1.refs_9_
  9.7 1.7 fusion.1.refs_8_
  11.4 1.0 select_convert_fusion.refs_10_
  12.4 155.9 %layer.1 = (bf16[4,64,512]{2,1,0:T(8,128)(2,1)}, bf16[4,64,512]{2,1,0:T(8,128)(2,1)}, bf16[4,16,512]{2,1,0:T(8,128)(2,1)}, bf16[4,48,512]{2,1,0:T(8,128)(2,1)}, ...) custom-call(bf16[512,512]{1,0:T(8,128)(2,1)} %refs_0_.1, bf16[512,512]{1,0:T(8,128)(2,1)} %refs_1_.1, ...), custom_call_target="tpu_custom_call" | custom-call | tf_op jit(solution)/shard_map/layer/pallas_call | solution.py:781
  168.3 0.7 slice.34
  169.0 0.9 fusion.24
  169.9 0.1 dynamic-slice_bitcast_fusion
  170.0 0.7 copy.28
  170.6 0.6 fusion.22
  171.2 0.6 fusion.20
  171.8 3.0 %finish.1 = (bf16[512,512]{1,0:T(8,128)(2,1)}, bf16[512,512]{1,0:T(8,128)(2,1)}, f32[64,1536]{1,0:T(8,128)}, f32[64,512]{1,0:T(8,128)}, f32[64,2048]{1,0:T(8,128)}, /*index=5*/f32[256,512]{1,0:T(8,128)}) custom-call(s32[1,8]{1,0:T(1,128)} %deal_ref.1, bf16[4,64,512]{2,1,0:T(8,128)(2,1)} %get-tuple-element.24.down, bf16[4,64,512]{2,1,0:T(8,128)(2,1)} %get-tuple-element.25.up, ...), custom_call_target="tpu_custom_call" | custom-call | tf_op jit(solution)/shard_map/finish/pallas_call | solution.py:812
  (16 shorter events, 0.1 us)
Async XLA Ops:
  0.7 0.7 copy-start
  3.2 0.7 copy-start.3
  3.9 0.7 copy-start.4
  4.6 0.7 copy-start.5
  5.3 0.7 copy-start.6
  6.0 0.7 copy-start.1
  7.5 0.7 copy-start.2

commit v5 on v4

--- a/solution.py
+++ b/solution.py
@@ -270,10 +270,11 @@
 
 def layer_kernel(back, maxlen, *refs):
     (
-        tokens_ref, cotangent_ref, deal_ref, small_in, wqkv_s, wout_s, wup_s, wdown_s, hot_ref, qx_ref, kx_ref,
-    ) = refs[:11]
-    sum_down, sum_up, sum_out, sum_qkv, small_out, ret_out, ret_grad = refs[11:18]
-    it = iter(refs[18:])
+        tokens_ref, cotangent_ref, deal_ref, lengths_ref, buckets_ref, *vector_refs, rel_ref,
+        wqkv_s, wout_s, wup_s, wdown_s,
+    ) = refs[:14]
+    sum_down, sum_up, sum_out, sum_qkv, small_out, ret_out, ret_grad = refs[14:21]
+    it = iter(refs[21:])
     sources = [next(it) for _ in range(4)]
     summers = [
         Summer(source, *[next(it) for _ in range(4)], out, next(it))
@@ -287,6 +288,7 @@
     xwin, g_ref, wqkv_ref, wout_ref, wup_ref, wdown_ref = (next(it) for _ in range(6))
     gather_sems, own_sems, deal_sems, row_sems, few_land, few_sems = (next(it) for _ in range(6))
     gains_ref, base_ref, q_ref, k_ref, v_ref, att_ref, lse_ref = (next(it) for _ in range(7))
+    few_mine, rel_all, hot_ref, qx_ref, kx_ref = (next(it) for _ in range(5))
     dp, groups = lax.axis_index("dp"), lax.axis_size("dp")
     seq, splits = lax.axis_index("seq"), lax.axis_size("seq")
     tokens, width = tokens_ref.shape
@@ -320,15 +322,21 @@
     own_first = back * tokens
     own_rows = pl.ds(own_first, tokens)
     dealt = deal_out(0, tokens_ref, xwin, own_first)
+    shard_rows, rel_rows = vector_refs[0].shape[0], rel_ref.shape[0]
+    few_mine[...] = jnp.zeros_like(few_mine)
+    for i, vector in enumerate(vector_refs):
+        few_mine[i : i + 1, :shard_rows] = vector[...].astype(F32).reshape(1, shard_rows)
+    few_mine[8 : 8 + rel_rows, :H] = rel_ref[...].astype(F32)
     few = []
     for step in range(1, groups):
         copy = pltpu.make_async_remote_copy(
-            src_ref=small_in, dst_ref=few_land.at[step - 1],
+            src_ref=few_mine, dst_ref=few_land.at[dp],
             send_sem=few_sems.at[0, step - 1], recv_sem=few_sems.at[1, step - 1],
             device_id={"dp": lax.rem(dp + step, groups)}, device_id_type=mesh_ids,
         )
         copy.start()
         few.append(copy)
+    few_land[dp] = few_mine[...]
     gathers = [
         Gather(shard, full, gather_sems.at[i], own_sems.at[i])
         for i, (shard, full) in enumerate(
@@ -336,6 +344,34 @@
         )
     ]
     gathers[0].start()
+
+    seqs = lengths_ref.shape[1]
+
+    def segments(rows, first_pos):
+        place = lax.broadcasted_iota(jnp.int32, (rows, PAIR), 0) + first_pos
+        found, end = jnp.zeros((rows, PAIR), jnp.int32), 0
+        for c in range(seqs):
+            end = end + lengths_ref[0, c]
+            found = found + (place >= end).astype(jnp.int32)
+        return jnp.where(place < 0, seqs, found)
+
+    window = kx_ref.shape[0]
+    lane_w = lax.rem(lax.broadcasted_iota(jnp.int32, (window, PAIR), 1), HD)
+    key_seg = segments(window, (seq - back) * tokens)
+    kx_ref[...] = jnp.where((lane_w == key_seg) | (lane_w >= HD - 3), 1.0, 0.0).astype(BF16)
+    lane_q = lane_w[:tokens]
+    qx_ref[...] = jnp.where((lane_q <= seqs) & (lane_q != segments(tokens, seq * tokens)), BIG, 0.0).astype(BF16)
+
+    level = lax.broadcasted_iota(jnp.int32, (NBK, PAIR), 0)
+    below, up_to = jnp.zeros((NBK, PAIR), F32), jnp.zeros((NBK, PAIR), F32)
+    for r in range(buckets_ref.shape[0]):
+        row = buckets_ref[r : r + 1, :]
+        below = below + (row < level).astype(F32)
+        up_to = up_to + (row <= level).astype(F32)
+    below = jnp.sum(below, axis=1, keepdims=True)
+    up_to = jnp.sum(up_to, axis=1, keepdims=True)
+    far = (back * tokens + QB - lax.broadcasted_iota(jnp.int32, hot_ref.shape, 1)).astype(F32)
+    hot_ref[...] = jnp.where((far >= below) & (far < up_to), 1.0, 0.0).astype(BF16)
     for copy in dealt:
         copy.wait_recv()
 
@@ -358,18 +394,19 @@
             row_copy(step).wait_recv()
 
     row_send(1)
-    dealt_grad = deal_out(1, cotangent_ref, g_ref, 0)
-    for gather in gathers[1:]:
-        gather.start()
-    little = small_in[...].astype(F32)
-    for step in range(1, groups):
-        few[step - 1].wait_recv()
-        little = little + few_land[step - 1].astype(F32)
-    gains_ref[...] = little[:8]
-    reach = lax.broadcasted_iota(jnp.int32, (H, base_ref.shape[-1]), 1) - QB
-    far = back * tokens - reach
-    table = dot_nt(little[8 : 8 + H, :PAIR].astype(BF16), hot_ref[...])
-    base_ref[...] = jnp.where((far >= 0) & (far < maxlen) & (reach >= 0), table, BIG).reshape(base_ref.shape)
+    for copy in few:
+        copy.wait_recv()
+    per_tile = PAIR // shard_rows
+    for i in range(width // PAIR):
+        tile = few_land[i * per_tile, :8, :]
+        for o in range(1, per_tile):
+            tile = tile + pltpu.roll(few_land[i * per_tile + o, :8, :], o * shard_rows, 1)
+        gains_ref[:, i * PAIR : (i + 1) * PAIR] = tile
+    for o in range(groups):
+        rel_all[o * rel_rows : (o + 1) * rel_rows, :] = few_land[o, 8 : 8 + rel_rows, :]
+    table = dot_nn(flip(rel_all[...])[:H], hot_ref[...])
+    far = back * tokens + QB - lax.broadcasted_iota(jnp.int32, table.shape, 1)
+    base_ref[...] = jnp.where((far >= 0) & (far < maxlen), table, BIG).reshape(base_ref.shape)
 
     def first_norm(chunk):
         normal, _ = norm_stats(xwin[chunk * tokens : (chunk + 1) * tokens, :].astype(F32))
@@ -377,6 +414,8 @@
 
     own_normed = first_norm(back)
     gathers[0].relay()
+    gathers[1].start()
+    gathers[2].start()
     gathers[0].arrive()
     q_ref[...] = (dot_nn(own_normed, wqkv_ref[:, :width])).astype(BF16) * jnp.asarray(HD**-0.5, BF16)
     k_ref[own_rows, :] = dot_nn(own_normed, wqkv_ref[:, width : 2 * width]).astype(BF16)
@@ -447,6 +486,9 @@
         look(chunk, first, count, jobs)
         if step == 0:
             gathers[1].relay()
+            dealt_grad = deal_out(1, cotangent_ref, g_ref, 0)
+            gathers[3].start()
+        if step == back - 1:
             gathers[2].relay()
     gathers[3].relay()
     for gather in gathers[1:]:
@@ -676,8 +718,8 @@
     dd_all = dd[...].reshape(H, dd.shape[-1])
     dd_hi = dd_all.astype(BF16)
     dd_mid = (dd_all - dd_hi.astype(F32)).astype(BF16)
-    small_ref[0, 8:16, :PAIR] = dot_nn(dd_hi, hot_ref[...]) + dot_nn(dd_mid, hot_ref[...])
-    small_ref[0, 8:16, PAIR:] = jnp.zeros((8, width - PAIR), F32)
+    small_ref[0, 8:16, :] = jnp.zeros((8, width), F32)
+    small_ref[0, 8:16, :NBK] = dot_nt(dd_hi, hot_ref[...]) + dot_nt(dd_mid, hot_ref[...])
     small = SmallSummer(small_ref, small_land, small_sems)
     small.pair()
     dx = (dres_ref[...] + norm_back(grad_normed * gains_ref[0:1, :], normal, scale)).astype(BF16)
@@ -716,12 +758,13 @@
             halo_copy(step).wait_send()
 
 
-def layer(back, maxlen, tokens_in, cotangent, deal, small, wqkv, wout, wup, wdown, hot, qx, kx):
+def layer(back, tokens_in, cotangent, deal, lengths, buckets, vectors, rel, wqkv, wout, wup, wdown):
     splits, groups = lax.axis_size("seq"), lax.axis_size("dp")
     tokens, width = tokens_in.shape
     length = tokens // groups
     per_chunk = tokens // QB
-    window, reach = kx.shape[0], hot.shape[0]
+    maxlen = buckets.shape[0]
+    window, reach = (back + 1) * tokens, back * tokens + 2 * QB
     span = max(count for _, _, count, _ in phase_spans(back, per_chunk, reach // QB - 1)) * QB
     grads = [wdown.shape[0], wup.shape[0] * wup.shape[1] // width, width // groups, 3 * width // groups]
     out_shapes, more, sources = [], [], []
@@ -767,7 +810,7 @@
         pltpu.SemaphoreType.DMA((4,)),
         pltpu.SemaphoreType.DMA((2, 2, groups - 1)),
         pltpu.SemaphoreType.DMA((2, back)),
-        pltpu.VMEM((groups - 1, 16, width), BF16),
+        pltpu.VMEM((groups, 16, PAIR), F32),
         pltpu.SemaphoreType.DMA((2, groups - 1)),
         pltpu.VMEM((8, width), F32),
         pltpu.VMEM((H // 2, 2, reach), F32),
@@ -776,21 +819,26 @@
         pltpu.VMEM((window, width), BF16),
         pltpu.VMEM((tokens, width), BF16),
         pltpu.VMEM((tokens, width), F32),
+        pltpu.VMEM((16, PAIR), F32),
+        pltpu.VMEM((NBK, PAIR), F32),
+        pltpu.VMEM((NBK, reach), BF16),
+        pltpu.VMEM((tokens, PAIR), BF16),
+        pltpu.VMEM((window, PAIR), BF16),
     ]
-    vmem = pl.BlockSpec(memory_space=pltpu.VMEM)
+    vmem, smem = pl.BlockSpec(memory_space=pltpu.VMEM), pl.BlockSpec(memory_space=pltpu.SMEM)
     return pl.pallas_call(
         functools.partial(layer_kernel, back, maxlen),
-        in_specs=[vmem, vmem, pl.BlockSpec(memory_space=pltpu.SMEM), vmem] + [pl.BlockSpec(memory_space=pl.ANY)] * 4 + [vmem] * 3,
+        in_specs=[vmem] * 2 + [smem] * 2 + [vmem] * (2 + len(vectors)) + [pl.BlockSpec(memory_space=pl.ANY)] * 4,
         out_specs=[vmem] * len(out_shapes),
         out_shape=out_shapes,
         scratch_shapes=scratch,
         compiler_params=pltpu.CompilerParams(collective_id=1, has_side_effects=True, vmem_limit_bytes=VMEM_LIMIT),
         name="layer",
-    )(tokens_in, cotangent, deal, small, wqkv, wout, wup, wdown, hot, qx, kx)
-
-
-def finish_kernel(deal_ref, down, up, out, qkv, ret_out, ret_grad, *outs):
-    o_out, o_grad, o_qkv, o_wout, o_up, o_down = outs
+    )(tokens_in, cotangent, deal, lengths, buckets.reshape(-1, PAIR), *vectors, rel, wqkv, wout, wup, wdown)
+
+
+def finish_kernel(deal_ref, down, up, out, qkv, small, ret_out, ret_grad, *outs):
+    o_out, o_grad, o_qkv, o_wout, o_up, o_down, *o_vectors, o_rel = outs
     length = ret_out.shape[1]
     for g in range(ret_out.shape[0]):
         piece = deal_ref[0, g]
@@ -806,12 +854,25 @@
         height = target.shape[0]
         for c in range(target.shape[1] // cols):
             target[:, c * cols : (c + 1) * cols] = value[c * height : (c + 1) * height]
+    dp, groups = lax.axis_index("dp"), lax.axis_size("dp")
+    for i, target in enumerate(o_vectors):
+        size = target.shape[0]
+        value = small[i : i + 1, :size]
+        for o in range(1, groups):
+            value = jnp.where(dp == o, small[i : i + 1, o * size : (o + 1) * size], value)
+        target[...] = value.reshape(size)
+    levels = small[8 : 8 + H, :PAIR].T
+    size = o_rel.shape[0]
+    value = levels[:size, :H]
+    for o in range(1, groups):
+        value = jnp.where(dp == o, levels[o * size : (o + 1) * size, :H], value)
+    o_rel[...] = value
 
 
 def finish(deal, sums, returned, shapes):
     return pl.pallas_call(
         finish_kernel,
-        in_specs=[pl.BlockSpec(memory_space=pltpu.SMEM)] + [pl.BlockSpec(memory_space=pltpu.VMEM)] * 6,
+        in_specs=[pl.BlockSpec(memory_space=pltpu.SMEM)] + [pl.BlockSpec(memory_space=pltpu.VMEM)] * 7,
         out_specs=[pl.BlockSpec(memory_space=pltpu.VMEM)] * len(shapes),
         out_shape=shapes,
         compiler_params=pltpu.CompilerParams(vmem_limit_bytes=VMEM_LIMIT),
@@ -835,77 +896,24 @@
     w_up,
     w_down,
 ):
-    groups = lax.axis_size("dp")
-    splits = lax.axis_size("seq")
-    tok_dev, width = tokens.shape
-    maxlen = buckets.shape[0]
-    back = -(-maxlen // tok_dev)
-    window = (back + 1) * tok_dev
-    span = back * tok_dev + QB
-    chunk = lax.axis_index("seq")
-    shard_rows = ln1_gain.shape[0]
-
-    slice_of = lax.axis_index("dp")
-    vectors = jnp.stack([jnp.tile(v, groups) for v in (ln1_gain, ln1_bias, ln2_gain, ln2_bias)])
-    vectors = jnp.where(jnp.arange(width)[None, :] // shard_rows == slice_of, vectors, 0)
-    rel_rows = rel_bias.shape[0]
-    scores = jnp.tile(rel_bias.T, (1, groups))
-    scores = jnp.where(jnp.arange(NBK)[None, :] // rel_rows == slice_of, scores, 0)
-    small = jnp.concatenate([jnp.pad(vectors, ((0, 4), (0, 0))), jnp.pad(scores, ((0, 0), (0, width - NBK)))], axis=0)
-
-    ends, so_far = [], 0
-    for c in range(lengths.shape[1]):
-        so_far = so_far + lengths[0, c]
-        ends.append(so_far)
-    lane = lax.rem(jnp.arange(PAIR, dtype=jnp.int32), HD)[None, :]
-    key_pos = (chunk - back) * tok_dev + jnp.arange(window, dtype=jnp.int32)
-    key_seg = sum((key_pos >= e).astype(jnp.int32) for e in ends)
-    key_seg = jnp.where(key_pos < 0, len(ends), key_seg)[:, None]
-    query_seg = key_seg[back * tok_dev :]
-    kx = jnp.where((lane == key_seg) | (lane >= HD - 3), 1.0, 0.0).astype(BF16)
-    qx = jnp.where((lane <= len(ends)) & (lane != query_seg), BIG, 0.0).astype(BF16)
-    offset = jnp.arange(span + QB, dtype=jnp.int32) - QB
-    distance = back * tok_dev - offset
-    in_reach = (distance >= 0) & (distance < maxlen) & (offset >= 0)
-    table_bucket = jnp.concatenate(
-        [
-            jnp.zeros((QB + back * tok_dev + 1 - maxlen,), jnp.int32),
-            buckets[::-1],
-            jnp.zeros((QB - 1,), jnp.int32),
-        ]
+    tok_dev = tokens.shape[0]
+    back = -(-buckets.shape[0] // tok_dev)
+    *sums, small_total, back_out, back_grad = layer(
+        back, tokens, cotangent, deal, lengths, buckets, (ln1_gain, ln1_bias, ln2_gain, ln2_bias), rel_bias,
+        w_qkv, w_out, w_up, w_down,
     )
-    hot = (table_bucket[:, None] == jnp.arange(PAIR, dtype=jnp.int32)[None, :]) & in_reach[:, None]
-    hot = hot.astype(BF16)
-    *sums, small_total, back_out, back_grad = layer(
-        back, maxlen, tokens, cotangent, deal, small, w_qkv, w_out, w_up, w_down, hot, qx, kx
-    )
-    output, grad_tokens, total_qkv, total_out, total_up, total_down = finish(
+    output, grad_tokens, total_qkv, total_out, total_up, total_down, g_one, b_one, g_two, b_two, total_rel = finish(
         deal,
-        sums,
+        [*sums, small_total],
         [back_out, back_grad],
-        [
-            jax.ShapeDtypeStruct((tok_dev, width), BF16),
-            jax.ShapeDtypeStruct((tok_dev, width), BF16),
-            jax.ShapeDtypeStruct(w_qkv.shape, F32),
-            jax.ShapeDtypeStruct(w_out.shape, F32),
-            jax.ShapeDtypeStruct(w_up.shape, F32),
-            jax.ShapeDtypeStruct(w_down.shape, F32),
+        [jax.ShapeDtypeStruct(tokens.shape, BF16)] * 2
+        + [
+            jax.ShapeDtypeStruct(a.shape, F32)
+            for a in (w_qkv, w_out, w_up, w_down, ln1_gain, ln1_bias, ln2_gain, ln2_bias, rel_bias)
         ],
     )
-    cut = [lax.dynamic_slice_in_dim(small_total[i], slice_of * shard_rows, shard_rows) for i in range(4)]
-    total_rel = lax.dynamic_slice_in_dim(small_total[8 : 8 + H, :NBK].T, slice_of * rel_rows, rel_rows)
     return (
-        output,
-        grad_tokens,
-        cut[0],
-        cut[1],
-        total_qkv,
-        total_out,
-        total_rel,
-        cut[2],
-        cut[3],
-        total_up,
-        total_down,
+        output, grad_tokens, g_one, b_one, total_qkv, total_out, total_rel, g_two, b_two, total_up, total_down,
     )
 
 

time: 175 us -> 152 us (0.87)
  the two profiles are of different devices: /device:TPU:29 before, /device:TPU:0 now
where the time goes in v5:
time: 152 us
  Pallas kernels  151 us (99%)
    pallas_call x1, Pallas kernels, layer(): pl.pallas_call(functools.partial(layer_kernel, back, maxlen), in_specs=[v...  148 us
    pallas_call x1, Pallas kernels, finish(): pl.pallas_call(finish_kernel, in_specs=[pl.BlockSpec(memory_space=pltpu.S...  3.54 us

profile of v5, /device:TPU:0, one launch (start us, length us, event | category | flops | bytes accessed | tf_op | source)
XLA Modules:
  0.0 152.2 jit_solution(17008776029564519273)
XLA Ops:
  0.6 147.9 %layer.1 = (bf16[4,64,512]{2,1,0:T(8,128)(2,1)}, bf16[4,64,512]{2,1,0:T(8,128)(2,1)}, bf16[4,16,512]{2,1,0:T(8,128)(2,1)}, bf16[4,48,512]{2,1,0:T(8,128)(2,1)}, ...) custom-call(bf16[512,512]{1,0:T(8,128)(2,1)} %refs_0_.1, bf16[512,512]{1,0:T(8,128)(2,1)} %refs_1_.1, ...), custom_call_target="tpu_custom_call" | custom-call | tf_op jit(solution)/shard_map/layer/pallas_call | solution.py:829
  148.5 3.5 %finish.1 = (bf16[512,512]{1,0:T(8,128)(2,1)}, bf16[512,512]{1,0:T(8,128)(2,1)}, f32[64,1536]{1,0:T(8,128)}, f32[64,512]{1,0:T(8,128)}, f32[64,2048]{1,0:T(8,128...) custom-call(s32[1,8]{1,0:T(1,128)} %deal_ref.1, ...), custom_call_target="tpu_custom_call" | custom-call | tf_op jit(solution)/shard_map/finish/pallas_call | solution.py:873

commit v6 on v5

--- a/solution.py
+++ b/solution.py
@@ -41,6 +41,10 @@
     return total
 
 
+def square(chip):
+    return chip + 1 - 2 * lax.rem(chip, 2), chip + 2 - 4 * (chip // 2), 3 - chip
+
+
 class Summer:
     def __init__(self, source, pair, recv2, mine, recv3, out, sems):
         self.source, self.pair, self.recv2 = source, pair, recv2
@@ -48,74 +52,130 @@
         self.dp, self.seq = lax.axis_index("dp"), lax.axis_index("seq")
         self.pairs, self.splits = source.shape[0] // 2, lax.axis_size("seq")
         self.core, self.chip = lax.rem(self.dp, 2), self.dp // 2
-        self.scatter = out.shape[1] < mine.shape[0]
-        self.sent = []
-        self.count = 0
-
-    def send(self, src, dst, device):
-        slot = self.count
-        self.count += 1
-        copy = pltpu.make_async_remote_copy(
+        self.rows = out.shape[1]
+        self.scatter = self.rows < mine.shape[0]
+        self.square = False
+        self.hops2 = 6 if self.square else self.pairs - 1
+
+    def copy(self, src, dst, slot, device):
+        return pltpu.make_async_remote_copy(
             src_ref=src, dst_ref=dst, send_sem=self.sems.at[0, slot], recv_sem=self.sems.at[1, slot],
             device_id=device, device_id_type=pl.DeviceIdType.MESH,
         )
-        copy.start()
-        self.sent.append(copy)
-        return copy
-
-    def stage1(self):
+
+    def copy1(self, k):
         other = 1 - self.core
-        self.first = [
-            self.send(self.source.at[2 * k + other], self.pair.at[k], {"dp": self.dp + 1 - 2 * self.core})
-            for k in range(self.pairs)
-        ]
+        return self.copy(self.source.at[2 * k + other], self.pair.at[k], k, {"dp": self.dp + 1 - 2 * self.core})
+
+    def copy2(self, step):
+        k = lax.rem(self.chip + 1 + step, self.pairs)
+        return self.copy(self.pair.at[k], self.recv2.at[step], self.pairs + step, {"dp": 2 * k + self.core})
+
+    def square2(self):
+        across, along, far = square(self.chip)
+        half = self.mine.shape[0] // 2
+        copies = []
+        for i, (one, two) in enumerate(((across, along), (along, across))):
+            part = pl.ds(i * half, half)
+            for j, owner in enumerate((one, far)):
+                copies.append(
+                    self.copy(
+                        self.pair.at[owner, part], self.recv2.at[j, part], self.pairs + 2 * i + j,
+                        {"dp": 2 * one + self.core},
+                    )
+                )
+        late = []
+        for i, two in enumerate((along, across)):
+            part = pl.ds(i * half, half)
+            late.append(
+                self.copy(
+                    self.pair.at[two, part], self.recv2.at[2, part], self.pairs + 4 + i, {"dp": 2 * two + self.core}
+                )
+            )
+        return copies, late
+
+    def copies2(self):
+        if self.square:
+            copies, late = self.square2()
+            return copies + late
+        return [self.copy2(step) for step in range(self.pairs - 1)]
+
+    def copy3(self, step):
+        t = lax.rem(self.seq + 1 + step, self.splits)
+        src = self.mine.at[pl.ds(pl.multiple_of(t * self.rows, self.rows), self.rows)] if self.scatter else self.mine
+        dst = self.recv3.at[step] if self.scatter else self.out.at[self.seq]
+        return self.copy(src, dst, self.pairs + self.hops2 + step, {"seq": t})
+
+    def copy4(self, step):
+        t = lax.rem(self.seq + 1 + step, self.splits)
+        slot = self.pairs + self.hops2 + self.splits - 1 + step
+        return self.copy(self.out.at[self.seq], self.out.at[self.seq], slot, {"seq": t})
+
+    def stage1(self, some=None):
+        for k in range(self.pairs) if some is None else some:
+            self.copy1(k).start()
 
     def stage2(self):
-        self.second = []
+        for k in range(self.pairs):
+            self.copy1(k).wait_recv()
         for step in range(self.pairs):
             k = lax.rem(self.chip + 1 + step, self.pairs)
-            if step == 0:
-                for copy in self.first:
-                    copy.wait_recv()
             self.pair[k] = add_low(self.source[2 * k + self.core], self.pair[k]).astype(self.pair.dtype)
-            if step < self.pairs - 1:
-                self.second.append(self.send(self.pair.at[k], self.recv2.at[step], {"dp": 2 * k + self.core}))
+            if step < self.pairs - 1 and not self.square:
+                self.copy2(step).start()
+        if self.square:
+            for copy in self.square2()[0]:
+                copy.start()
+
+    def stage2b(self):
+        if not self.square:
+            return
+        across, along, _ = square(self.chip)
+        copies, late = self.square2()
+        half = self.mine.shape[0] // 2
+        for copy in copies:
+            copy.wait_recv()
+        for i, two in enumerate((along, across)):
+            part = pl.ds(i * half, half)
+            self.pair[two, part] = add_low(self.pair[two, part], self.recv2[1, part]).astype(self.pair.dtype)
+            late[i].start()
 
     def stage3(self):
-        for copy in self.second:
-            copy.wait_recv()
-        total = add_low(self.pair[self.chip], *[self.recv2[step] for step in range(self.pairs - 1)])
+        if self.square:
+            for copy in self.square2()[1]:
+                copy.wait_recv()
+            total = add_low(self.pair[self.chip], self.recv2[0], self.recv2[2])
+        else:
+            for step in range(self.pairs - 1):
+                self.copy2(step).wait_recv()
+            total = add_low(self.pair[self.chip], *[self.recv2[step] for step in range(self.pairs - 1)])
         self.mine[...] = total.astype(self.mine.dtype)
-        self.third = []
-        rows = self.out.shape[1]
         for step in range(self.splits - 1):
-            t = lax.rem(self.seq + 1 + step, self.splits)
-            src = self.mine.at[pl.ds(pl.multiple_of(t * rows, rows), rows)] if self.scatter else self.mine
-            dst = self.recv3.at[step] if self.scatter else self.out.at[self.seq]
-            self.third.append(self.send(src, dst, {"seq": t}))
+            self.copy3(step).start()
         if not self.scatter:
             self.out[self.seq] = self.mine[...]
 
     def stage4(self):
-        for copy in self.third:
-            copy.wait_recv()
+        for step in range(self.splits - 1):
+            self.copy3(step).wait_recv()
         if not self.scatter:
             return
-        rows = self.out.shape[1]
-        own = self.mine[pl.ds(pl.multiple_of(self.seq * rows, rows), rows)]
+        own = self.mine[pl.ds(pl.multiple_of(self.seq * self.rows, self.rows), self.rows)]
         total = add_low(own, *[self.recv3[step] for step in range(self.splits - 1)])
         self.out[self.seq] = total.astype(self.out.dtype)
-        self.fourth = [
-            self.send(self.out.at[self.seq], self.out.at[self.seq], {"seq": lax.rem(self.seq + 1 + step, self.splits)})
-            for step in range(self.splits - 1)
-        ]
+        for step in range(self.splits - 1):
+            self.copy4(step).start()
 
     def finish(self):
+        for k in range(self.pairs):
+            self.copy1(k).wait_send()
+        for copy in self.copies2():
+            copy.wait_send()
+        for step in range(self.splits - 1):
+            self.copy3(step).wait_send()
         if self.scatter:
-            for copy in self.fourth:
-                copy.wait_recv()
-        for copy in self.sent:
-            copy.wait_send()
+            for step in range(self.splits - 1):
+                self.copy4(step).wait()
 
 
 def summer_shapes(shape, dtype, splits):
@@ -123,7 +183,7 @@
     pairs = groups // 2
     scatter = rows % (16 * splits) == 0
     out = jax.ShapeDtypeStruct((splits, rows // splits if scatter else rows, cols), dtype)
-    copies = pairs + (pairs - 1) + (splits - 1) * (2 if scatter else 1)
+    copies = pairs + (6 if pairs == 4 else pairs - 1) + (splits - 1) * (2 if scatter else 1)
     scratch = [
         pltpu.VMEM((pairs, rows, cols), dtype),
         pltpu.VMEM((pairs - 1, rows, cols), dtype),
@@ -227,44 +287,78 @@
         self.rows = shard.shape[0]
         self.dp = lax.axis_index("dp")
         self.pairs = lax.axis_size("dp") // 2
+        self.square = self.pairs == 4
         self.core, self.chip = lax.rem(self.dp, 2), self.dp // 2
         self.sibling = {"dp": self.dp + 1 - 2 * self.core}
         self.own = pltpu.make_async_copy(shard, self.place(self.dp), own_sem)
-
-    def place(self, owner):
-        return self.full.at[pl.ds(pl.multiple_of(owner * self.rows, self.rows), self.rows)]
-
-    def copy(self, src, owner, slot, device):
+        if self.square:
+            self.around = square(self.chip)
+        else:
+            self.around = [lax.rem(self.chip + step, self.pairs) for step in range(1, self.pairs)]
+            self.behind = [lax.rem(self.chip + self.pairs - step, self.pairs) for step in range(1, self.pairs)]
+
+    def place(self, owner, first=0, rows=None):
+        start = pl.multiple_of(owner * self.rows, self.rows)
+        return self.full.at[pl.ds(start + first, self.rows if rows is None else rows)]
+
+    def copy(self, src, dst, slot, device):
         return pltpu.make_async_remote_copy(
-            src_ref=src, dst_ref=self.place(owner), send_sem=self.sems.at[0, slot], recv_sem=self.sems.at[1, slot],
+            src_ref=src, dst_ref=dst, send_sem=self.sems.at[0, slot], recv_sem=self.sems.at[1, slot],
             device_id=device, device_id_type=pl.DeviceIdType.MESH,
         )
 
+    def mate(self, chip):
+        return {"dp": 2 * chip + self.core}
+
     def start(self):
-        self.sent = [
-            self.copy(self.shard, self.dp, step, {"dp": 2 * lax.rem(self.chip + step, self.pairs) + self.core})
-            for step in range(1, self.pairs)
-        ]
-        self.near = self.copy(self.shard, self.dp, 0, self.sibling)
+        reach = self.around[:2] if self.square else self.around
+        self.sent = [self.copy(self.shard, self.place(self.dp), 1 + i, self.mate(c)) for i, c in enumerate(reach)]
+        self.near = self.copy(self.shard, self.place(self.dp), 0, self.sibling)
         for copy in self.sent + [self.near]:
             copy.start()
         self.own.start()
+        self.waiting = [self.near]
+
+    def share(self, chip, slot):
+        there = self.place(2 * chip + self.core)
+        copy = self.copy(there, there, slot, self.sibling)
+        copy.start()
+        self.waiting.append(copy)
+        self.sent.append(copy)
 
     def relay(self):
-        self.relayed = []
-        for step in range(1, self.pairs):
-            self.sent[step - 1].wait_recv()
-            owner = 2 * lax.rem(self.chip + self.pairs - step, self.pairs) + self.core
-            self.relayed.append(self.copy(self.place(owner), owner, self.pairs - 1 + step, self.sibling))
-            self.relayed[-1].start()
+        for copy in self.sent:
+            copy.wait_recv()
+        if not self.square:
+            for i, chip in enumerate(self.behind):
+                self.share(chip, self.pairs + i)
+            return
+        across, along, _ = self.around
+        half = self.rows // 2
+        self.passed = []
+        for i, (origin, target) in enumerate(((across, along), (along, across))):
+            there = self.place(2 * origin + self.core, i * half, half)
+            copy = self.copy(there, there, 3 + i, self.mate(target))
+            copy.start()
+            self.passed.append(copy)
+        self.share(across, 5)
+        self.share(along, 6)
+
+    def relay_far(self):
+        if not self.square:
+            return
+        for copy in self.passed:
+            copy.wait_recv()
+        self.share(self.around[2], 7)
+        self.sent += self.passed
 
     def arrive(self):
         self.own.wait()
-        for copy in [self.near] + self.relayed:
+        for copy in self.waiting:
             copy.wait_recv()
 
     def finish(self):
-        for copy in self.sent + [self.near] + self.relayed:
+        for copy in self.sent + [self.near]:
             copy.wait_send()
 
 
@@ -284,7 +378,8 @@
     small_ref, small_land, small_sems = next(it), next(it), next(it)
     slots, ret_sems, halo_send, halo_land, halo_sems = (next(it) for _ in range(5))
     dres_ref, do_ref, qaug, doaug, q_t, do_t = (next(it) for _ in range(6))
-    bias, dsum, dd, dq_acc, dkt, dvt, dkv, gkv = (next(it) for _ in range(8))
+    bias, scores, kaug, vaug, dd, dq_acc, dkt, dvt, dkv, gkv = (next(it) for _ in range(10))
+    dsum = scores.at[0]
     xwin, g_ref, wqkv_ref, wout_ref, wup_ref, wdown_ref = (next(it) for _ in range(6))
     gather_sems, own_sems, deal_sems, row_sems, few_land, few_sems = (next(it) for _ in range(6))
     gains_ref, base_ref, q_ref, k_ref, v_ref, att_ref, lse_ref = (next(it) for _ in range(7))
@@ -344,6 +439,7 @@
         )
     ]
     gathers[0].start()
+    gathers[1].start()
 
     seqs = lengths_ref.shape[1]
 
@@ -414,8 +510,8 @@
 
     own_normed = first_norm(back)
     gathers[0].relay()
-    gathers[1].start()
     gathers[2].start()
+    gathers[0].relay_far()
     gathers[0].arrive()
     q_ref[...] = (dot_nn(own_normed, wqkv_ref[:, :width])).astype(BF16) * jnp.asarray(HD**-0.5, BF16)
     k_ref[own_rows, :] = dot_nn(own_normed, wqkv_ref[:, width : 2 * width]).astype(BF16)
@@ -423,31 +519,32 @@
 
     low_tile = lax.broadcasted_iota(jnp.int32, (QB, PAIR), 1) < HD
 
-    def look(chunk, first, count, jobs):
-        span = count * QB
-        keys = pl.ds(chunk * tokens, tokens)
-        started, last = chunk < back, chunk == 0
+    def look(low, high, started, last):
+        jobs = [(kt, b, kt - b) for kt in range(low, high) for b in range(per_chunk) if 0 <= kt - b < tiles]
+        first = min(j for _, _, j in jobs)
+        span = (max(j for _, _, j in jobs) + 1 - first) * QB
+        keys = pl.ds(low * QB, (high - low) * QB)
+        jobs = [(kt - low, b, j) for kt, b, j in jobs]
 
         def body(pair, _):
             cols = pl.ds(pl.multiple_of(pair * PAIR, PAIR), PAIR)
             k_pair, v_pair, kx = k_ref[keys, cols], v_ref[keys, cols], kx_ref[keys, :]
-            low_k = lax.broadcasted_iota(jnp.int32, (tokens, PAIR), 1) < HD
+            low_k = lax.broadcasted_iota(jnp.int32, k_pair.shape, 1) < HD
             for h in range(2):
                 mine_k = low_k if h == 0 else jnp.logical_not(low_k)
                 mine = low_tile if h == 0 else jnp.logical_not(low_tile)
-                bias[:, :span] = toeplitz(base_ref[pair, h : h + 1, first * QB : (first + count + 1) * QB])
-                k_aug = jnp.where(mine_k, k_pair, kx)
-                v_aug = jnp.where(mine_k, v_pair, jnp.ones_like(v_pair))
+                bias[:, :span] = toeplitz(base_ref[pair, h : h + 1, first * QB : first * QB + span + QB])
+                kaug[: (high - low) * QB] = jnp.where(mine_k, k_pair, kx)
+                vaug[: (high - low) * QB] = jnp.where(mine_k, v_pair, jnp.ones_like(v_pair))
                 held = pl.ds(pl.multiple_of((2 * pair + h) * PAIR, PAIR), PAIR)
                 for b in range(per_chunk):
                     here = pl.ds(b * QB, QB)
-                    work = [(kt, j - first) for kt, block, j in jobs if block == b]
                     q_aug = jnp.where(mine, q_ref[here, cols], qx_ref[here, :])
+                    work = [(pl.ds(kt * QB, QB), pl.ds((j - first) * QB, QB)) for kt, block, j in jobs if block == b]
                     top = None
-                    for kt, j in work:
-                        over = pl.ds(j * QB, QB)
-                        score = dot_nt(q_aug, k_aug[kt * QB : (kt + 1) * QB]) + bias[:, over]
-                        dsum[:, over] = score
+                    for part, over in work:
+                        score = dot_nt(q_aug, kaug[part, :]) + bias[:, over]
+                        scores[b % scores.shape[0], :, over] = score
                         most = jnp.maximum(score[:, :128], score[:, 128:])
                         top = most if top is None else jnp.maximum(top, most)
                     top = jnp.max(top, axis=1, keepdims=True)
@@ -457,9 +554,9 @@
                         before = lse_ref[here, cols][:, lane_at : lane_at + 1]
                         top = jnp.maximum(top, before)
                         acc = gkv[here, held] * jnp.exp(before - top)
-                    for kt, j in work:
-                        p = jnp.exp(dsum[:, pl.ds(j * QB, QB)] - top).astype(BF16)
-                        more = dot_nn(p, v_aug[kt * QB : (kt + 1) * QB])
+                    for part, over in work:
+                        p = jnp.exp(scores[b % scores.shape[0], :, over] - top).astype(BF16)
+                        more = dot_nn(p, vaug[part, :])
                         acc = more if acc is None else acc + more
                     if last:
                         value = (acc / pltpu.roll(acc, HD, 1)).astype(BF16)
@@ -473,24 +570,29 @@
 
         lax.fori_loop(0, H // 2, body, 0)
 
-    for chunk, first, count, jobs in reversed(spans):
-        step = back - chunk
-        if step > 0:
-            row_wait(step)
-            if step < back:
-                row_send(step + 1)
-            normed = jnp.where(seq >= step, first_norm(chunk).astype(F32), 0.0).astype(BF16)
-            here = pl.ds(chunk * tokens, tokens)
-            k_ref[here, :] = dot_nn(normed, wqkv_ref[:, width : 2 * width]).astype(BF16)
-            v_ref[here, :] = dot_nn(normed, wqkv_ref[:, 2 * width :]).astype(BF16)
-        look(chunk, first, count, jobs)
-        if step == 0:
-            gathers[1].relay()
+    def keys_of(chunk):
+        normed = jnp.where(seq >= back - chunk, first_norm(chunk).astype(F32), 0.0).astype(BF16)
+        here = pl.ds(chunk * tokens, tokens)
+        k_ref[here, :] = dot_nn(normed, wqkv_ref[:, width : 2 * width]).astype(BF16)
+        v_ref[here, :] = dot_nn(normed, wqkv_ref[:, 2 * width :]).astype(BF16)
+
+    for step in range(1, back):
+        row_wait(step)
+        row_send(step + 1)
+        if step == 1:
             dealt_grad = deal_out(1, cotangent_ref, g_ref, 0)
             gathers[3].start()
-        if step == back - 1:
-            gathers[2].relay()
-    gathers[3].relay()
+        keys_of(back - step)
+        if step % 2:
+            high = (back - step + 2) * per_chunk
+            look((back - step) * per_chunk, high, step > 1, False)
+    for gather in gathers[1:]:
+        gather.relay()
+    row_wait(back)
+    keys_of(0)
+    look(0, per_chunk, True, True)
+    for gather in gathers[1:]:
+        gather.relay_far()
     for gather in gathers[1:]:
         gather.arrive()
     for copy in dealt_grad:
@@ -498,19 +600,18 @@
     for copy in dealt + dealt_grad:
         copy.wait_send()
 
-    returns = []
-
-    def send_back(which, landed):
-        landed[dp] = slots[which, dp]
+    def ret_copy(which, step):
+        peer = lax.rem(dp + step, groups)
+        return pltpu.make_async_remote_copy(
+            src_ref=slots.at[which, peer], dst_ref=(ret_out, ret_grad)[which].at[dp],
+            send_sem=ret_sems.at[0, which, step - 1], recv_sem=ret_sems.at[1, which, step - 1],
+            device_id={"dp": peer}, device_id_type=mesh_ids,
+        )
+
+    def send_back(which):
         for step in range(1, groups):
-            peer = lax.rem(dp + step, groups)
-            copy = pltpu.make_async_remote_copy(
-                src_ref=slots.at[which, peer], dst_ref=landed.at[dp],
-                send_sem=ret_sems.at[0, which, step - 1], recv_sem=ret_sems.at[1, which, step - 1],
-                device_id={"dp": peer}, device_id_type=mesh_ids,
-            )
-            copy.start()
-            returns.append(copy)
+            ret_copy(which, step).start()
+        (ret_out, ret_grad)[which][dp] = slots[which, dp]
 
     resid = xwin[own_rows, :].astype(F32) + dot_nn(att_ref[...], wout_ref[...])
     normal, scale = norm_stats(resid)
@@ -533,15 +634,15 @@
         grad_down = dot_nn(flip(act), g).astype(BF16)
         for o in range(width // rows_down):
             sources[0][c * (width // rows_down) + o] = grad_down[o * rows_down : (o + 1) * rows_down]
+        per_step = width // rows_down // 2
+        down.stage1(range(c * per_step, (c + 1) * per_step))
         grad_up = dot_nn(a2_t, dup).astype(BF16)
         for o in range(groups):
             sources[1][o, c * rows_up : (c + 1) * rows_up] = grad_up[o * rows_up : (o + 1) * rows_up]
-    down.stage1()
     up.stage1()
     y = y.astype(BF16)
     for o in range(groups):
         slots[0, o] = y[o * length : (o + 1) * length]
-    send_back(0, ret_out)
     small_ref[0, 2:3, :] = jnp.sum(da2 * normal, axis=0, keepdims=True)
     small_ref[0, 3:4, :] = jnp.sum(da2, axis=0, keepdims=True)
     dres = g.astype(F32) + norm_back(da2 * gain_two, normal, scale)
@@ -588,16 +689,28 @@
         return _
 
     lax.fori_loop(0, H // 2, prepare, 0)
+    down.stage2()
+    up.stage2()
+    out_sum.stage2()
     dd[...] = jnp.zeros_like(dd)
     dq_acc[...] = jnp.zeros_like(dq_acc)
     halo = []
 
-    def attend(chunk, first, count, jobs):
+    rounds = len(spans) * (H // 2)
+    plan = {}
+    for part, action in (
+    ):
+        plan.setdefault(part * rounds // 12, []).append(action)
+
+    def attend(index, chunk, first, count, jobs):
         span = count * QB
         keys = pl.ds(chunk * tokens, tokens)
         fresh = set()
 
         def body(pair, _):
+            for spot in range(H // 2):
+                for action in plan.get(index * (H // 2) + spot, ()):
+                    pl.when(pair == spot)(action)
             cols = pl.ds(pl.multiple_of(pair * PAIR, PAIR), PAIR)
             k_pair, v_pair, kx = k_ref[keys, cols], v_ref[keys, cols], kx_ref[keys, :]
             for h in range(2):
@@ -653,14 +766,14 @@
 
     def halo_copy(step):
         return pltpu.make_async_remote_copy(
-            src_ref=halo_send.at[step - 1], dst_ref=halo_land.at[step - 1],
+            src_ref=halo_send.at[(step - 1) % 2], dst_ref=halo_land.at[step - 1],
             send_sem=halo_sems.at[0, step - 1], recv_sem=halo_sems.at[1, step - 1],
             device_id={"seq": lax.rem(seq + splits - 1, splits)}, device_id_type=pl.DeviceIdType.MESH,
         )
 
     grad_normed = None
     for index, (chunk, first, count, jobs) in enumerate(spans):
-        attend(chunk, first, count, jobs)
+        attend(index, chunk, first, count, jobs)
         step = back - chunk
         part = dot_nt(dkv[...], wqkv_ref[:, width:])
         rows_t = first_norm(chunk)
@@ -690,21 +803,24 @@
 
                 arrived = jnp.where((seq + 1 < splits) & (seq >= step), halo_land[step].astype(F32), 0.0)
                 part = part + arrived
-            halo_send[step - 1] = part.astype(BF16)
+            if step + 2 <= back:
+
+                @pl.when(seq >= step + 2)
+                def _(step=step):
+                    halo_copy(step + 2).wait_send()
+
+            halo_send[(step - 1) % 2] = part.astype(BF16)
 
             @pl.when(seq >= step)
             def _(step=step):
                 halo_copy(step).start()
 
-        if index == 0:
-            down.stage2()
-            up.stage2()
-            out_sum.stage2()
-        if index == back - 1 and back > 0:
-            down.stage3()
+    down.stage3()
     up.stage3()
     out_sum.stage3()
     qkv_sum.stage2()
+    send_back(0)
+    down.stage4()
 
     @pl.when(seq + 1 < splits)
     def _():
@@ -725,23 +841,24 @@
     dx = (dres_ref[...] + norm_back(grad_normed * gains_ref[0:1, :], normal, scale)).astype(BF16)
     for o in range(groups):
         slots[1, o] = dx[o * length : (o + 1) * length]
-    send_back(1, ret_grad)
+    send_back(1)
+    qkv_sum.stage2b()
     small.take()
     small.plane()
-    down.stage4()
     up.stage4()
+    out_sum.stage4()
     qkv_sum.stage3()
     small.take()
     small.along()
-    out_sum.stage4()
     qkv_sum.stage4()
     small.take()
     small_out[...] = small_ref[3]
     for summer in summers:
         summer.finish()
     small.finish()
-    for copy in returns:
-        copy.wait()
+    for which in range(2):
+        for step in range(1, groups):
+            ret_copy(which, step).wait()
     for gather in gathers:
         gather.finish()
     for copy in few:
@@ -751,7 +868,7 @@
         @pl.when((seq + 1 < splits) & (seq + 1 >= step))
         def _(step=step):
             row_copy(step).wait_send()
-    for step in range(1, back + 1):
+    for step in range(1, min(back, 2) + 1):
 
         @pl.when(seq >= step)
         def _(step=step):
@@ -765,7 +882,8 @@
     per_chunk = tokens // QB
     maxlen = buckets.shape[0]
     window, reach = (back + 1) * tokens, back * tokens + 2 * QB
-    span = max(count for _, _, count, _ in phase_spans(back, per_chunk, reach // QB - 1)) * QB
+    wide = min(2, back) * per_chunk
+    span = min(wide + per_chunk - 1, reach // QB - 1) * QB
     grads = [wdown.shape[0], wup.shape[0] * wup.shape[1] // width, width // groups, 3 * width // groups]
     out_shapes, more, sources = [], [], []
     for height in grads:
@@ -783,7 +901,7 @@
         pltpu.SemaphoreType.DMA((2, small_copies)),
         pltpu.VMEM((2, groups, length, width), BF16),
         pltpu.SemaphoreType.DMA((2, 2, groups - 1)),
-        pltpu.VMEM((back, tokens, width), BF16),
+        pltpu.VMEM((min(back, 2), tokens, width), BF16),
         pltpu.VMEM((back, tokens, width), BF16),
         pltpu.SemaphoreType.DMA((2, back)),
         pltpu.VMEM((tokens, width), F32),
@@ -793,7 +911,9 @@
         pltpu.VMEM((width, tokens), BF16),
         pltpu.VMEM((width, tokens), BF16),
         pltpu.VMEM((QB, span), F32),
-        pltpu.VMEM((QB, span), F32),
+        pltpu.VMEM((2 if span <= 1024 else 1, QB, span), F32),
+        pltpu.VMEM((wide * QB, PAIR), BF16),
+        pltpu.VMEM((wide * QB, PAIR), BF16),
         pltpu.VMEM((H // 2, 2, reach), F32),
         pltpu.VMEM((tokens, width), F32),
         pltpu.VMEM((PAIR, tokens), F32),
@@ -806,7 +926,7 @@
         pltpu.VMEM((width, width), BF16),
         pltpu.VMEM((width, wup.shape[1]), BF16),
         pltpu.VMEM((wup.shape[1], width), BF16),
-        pltpu.SemaphoreType.DMA((4, 2, groups - 1)),
+        pltpu.SemaphoreType.DMA((4, 2, max(8, groups - 1))),
         pltpu.SemaphoreType.DMA((4,)),
         pltpu.SemaphoreType.DMA((2, 2, groups - 1)),
         pltpu.SemaphoreType.DMA((2, back)),

time: 152 us -> 145 us (0.954)
  Pallas kernels: 151 us -> 144 us
    pallas_call x1, Pallas kernels: 148 us -> 141 us  [layer(): pl.pallas_call(functools.partial(layer_kernel, back, maxlen), in_specs=[v...]
where the time goes in v6:
time: 145 us
  Pallas kernels  144 us (99%)
    pallas_call x1, Pallas kernels, layer(): pl.pallas_call(functools.partial(layer_kernel, back, maxlen), in_specs=[v...  141 us
    pallas_call x1, Pallas kernels, finish(): pl.pallas_call(finish_kernel, in_specs=[pl.BlockSpec(memory_space=pltpu.S...  3.54 us

profile of v6, /device:TPU:0, one launch (start us, length us, event | category | flops | bytes accessed | tf_op | source)
XLA Modules:
  0.0 145.1 jit_solution(12516530857870952490)
XLA Ops:
  0.6 140.8 %layer.1 = (bf16[4,64,512]{2,1,0:T(8,128)(2,1)}, bf16[4,64,512]{2,1,0:T(8,128)(2,1)}, bf16[4,16,512]{2,1,0:T(8,128)(2,1)}, bf16[4,48,512]{2,1,0:T(8,128)(2,1)}, ...) custom-call(bf16[512,512]{1,0:T(8,128)(2,1)} %refs_0_.1, bf16[512,512]{1,0:T(8,128)(2,1)} %refs_1_.1, ...), custom_call_target="tpu_custom_call" | custom-call | tf_op jit(solution)/shard_map/layer/pallas_call | solution.py:949
  141.4 3.5 %finish.1 = (bf16[512,512]{1,0:T(8,128)(2,1)}, bf16[512,512]{1,0:T(8,128)(2,1)}, f32[64,1536]{1,0:T(8,128)}, f32[64,512]{1,0:T(8,128)}, f32[64,2048]{1,0:T(8,128...) custom-call(s32[1,8]{1,0:T(1,128)} %deal_ref.1, ...), custom_call_target="tpu_custom_call" | custom-call | tf_op jit(solution)/shard_map/finish/pallas_call | solution.py:993

commit v7 on v6

--- a/solution.py
+++ b/solution.py
@@ -46,7 +46,7 @@
 
 
 class Summer:
-    def __init__(self, source, pair, recv2, mine, recv3, out, sems):
+    def __init__(self, source, pair, recv2, mine, recv3, out, sems, halving):
         self.source, self.pair, self.recv2 = source, pair, recv2
         self.mine, self.recv3, self.out, self.sems = mine, recv3, out, sems
         self.dp, self.seq = lax.axis_index("dp"), lax.axis_index("seq")
@@ -54,8 +54,9 @@
         self.core, self.chip = lax.rem(self.dp, 2), self.dp // 2
         self.rows = out.shape[1]
         self.scatter = self.rows < mine.shape[0]
-        self.square = False
-        self.hops2 = 6 if self.square else self.pairs - 1
+        self.halving = halving and self.scatter
+        self.rounds = (self.splits - 1).bit_length() if self.halving else 1
+        self.hops2 = self.pairs - 1
 
     def copy(self, src, dst, slot, device):
         return pltpu.make_async_remote_copy(
@@ -71,35 +72,6 @@
         k = lax.rem(self.chip + 1 + step, self.pairs)
         return self.copy(self.pair.at[k], self.recv2.at[step], self.pairs + step, {"dp": 2 * k + self.core})
 
-    def square2(self):
-        across, along, far = square(self.chip)
-        half = self.mine.shape[0] // 2
-        copies = []
-        for i, (one, two) in enumerate(((across, along), (along, across))):
-            part = pl.ds(i * half, half)
-            for j, owner in enumerate((one, far)):
-                copies.append(
-                    self.copy(
-                        self.pair.at[owner, part], self.recv2.at[j, part], self.pairs + 2 * i + j,
-                        {"dp": 2 * one + self.core},
-                    )
-                )
-        late = []
-        for i, two in enumerate((along, across)):
-            part = pl.ds(i * half, half)
-            late.append(
-                self.copy(
-                    self.pair.at[two, part], self.recv2.at[2, part], self.pairs + 4 + i, {"dp": 2 * two + self.core}
-                )
-            )
-        return copies, late
-
-    def copies2(self):
-        if self.square:
-            copies, late = self.square2()
-            return copies + late
-        return [self.copy2(step) for step in range(self.pairs - 1)]
-
     def copy3(self, step):
         t = lax.rem(self.seq + 1 + step, self.splits)
         src = self.mine.at[pl.ds(pl.multiple_of(t * self.rows, self.rows), self.rows)] if self.scatter else self.mine
@@ -110,6 +82,48 @@
         t = lax.rem(self.seq + 1 + step, self.splits)
         slot = self.pairs + self.hops2 + self.splits - 1 + step
         return self.copy(self.out.at[self.seq], self.out.at[self.seq], slot, {"seq": t})
+
+    def exchange(self, back, turn):
+        low, stride = 2**turn, 2 ** (turn + 1)
+        bit = lax.rem(self.seq // low, 2)
+        partner = self.seq + low - 2 * low * bit
+        kept, given = lax.rem(self.seq, stride), lax.rem(partner, stride)
+        count = self.splits // stride
+        base = self.splits - self.splits // low
+        slot = self.pairs + self.hops2 + base + (self.splits - 1 if back else 0)
+        moves = []
+        for i in range(count):
+            mine, theirs = kept + i * stride, given + i * stride
+            src = self.out.at[mine] if back else self.mine.at[self.part(theirs)]
+            dst = self.out.at[mine] if back else self.recv3.at[base + i]
+            moves.append((self.copy(src, dst, slot + i, {"seq": partner}), mine, base + i))
+        return moves
+
+    def part(self, t):
+        return pl.ds(pl.multiple_of(t * self.rows, self.rows), self.rows)
+
+    def turn(self, turn):
+        if not self.halving:
+            return
+        for copy, kept, slot in self.exchange(False, turn - 1):
+            copy.wait_recv()
+            self.mine[self.part(kept)] = add_low(self.mine[self.part(kept)], self.recv3[slot]).astype(self.mine.dtype)
+        if turn < self.rounds:
+            for copy, _, _ in self.exchange(False, turn):
+                copy.start()
+        else:
+            self.out[self.seq] = self.mine[self.part(self.seq)]
+            for copy, _, _ in self.exchange(True, turn - 1):
+                copy.start()
+
+    def turn_back(self, turn):
+        if not self.halving:
+            return
+        for copy, _, _ in self.exchange(True, turn):
+            copy.wait_recv()
+        if turn > 0:
+            for copy, _, _ in self.exchange(True, turn - 1):
+                copy.start()
 
     def stage1(self, some=None):
         for k in range(self.pairs) if some is None else some:
@@ -121,41 +135,26 @@
         for step in range(self.pairs):
             k = lax.rem(self.chip + 1 + step, self.pairs)
             self.pair[k] = add_low(self.source[2 * k + self.core], self.pair[k]).astype(self.pair.dtype)
-            if step < self.pairs - 1 and not self.square:
+            if step < self.pairs - 1:
                 self.copy2(step).start()
-        if self.square:
-            for copy in self.square2()[0]:
+
+    def stage3(self):
+        for step in range(self.pairs - 1):
+            self.copy2(step).wait_recv()
+        total = add_low(self.pair[self.chip], *[self.recv2[step] for step in range(self.pairs - 1)])
+        self.mine[...] = total.astype(self.mine.dtype)
+        if self.halving:
+            for copy, _, _ in self.exchange(False, 0):
                 copy.start()
-
-    def stage2b(self):
-        if not self.square:
             return
-        across, along, _ = square(self.chip)
-        copies, late = self.square2()
-        half = self.mine.shape[0] // 2
-        for copy in copies:
-            copy.wait_recv()
-        for i, two in enumerate((along, across)):
-            part = pl.ds(i * half, half)
-            self.pair[two, part] = add_low(self.pair[two, part], self.recv2[1, part]).astype(self.pair.dtype)
-            late[i].start()
-
-    def stage3(self):
-        if self.square:
-            for copy in self.square2()[1]:
-                copy.wait_recv()
-            total = add_low(self.pair[self.chip], self.recv2[0], self.recv2[2])
-        else:
-            for step in range(self.pairs - 1):
-                self.copy2(step).wait_recv()
-            total = add_low(self.pair[self.chip], *[self.recv2[step] for step in range(self.pairs - 1)])
-        self.mine[...] = total.astype(self.mine.dtype)
         for step in range(self.splits - 1):
             self.copy3(step).start()
         if not self.scatter:
             self.out[self.seq] = self.mine[...]
 
     def stage4(self):
+        if self.halving:
+            return
         for step in range(self.splits - 1):
             self.copy3(step).wait_recv()
         if not self.scatter:
@@ -169,8 +168,14 @@
     def finish(self):
         for k in range(self.pairs):
             self.copy1(k).wait_send()
-        for copy in self.copies2():
-            copy.wait_send()
+        for step in range(self.pairs - 1):
+            self.copy2(step).wait_send()
+        if self.halving:
+            for turn in range(self.rounds):
+                for back in (False, True):
+                    for copy, _, _ in self.exchange(back, turn):
+                        copy.wait_send()
+            return
         for step in range(self.splits - 1):
             self.copy3(step).wait_send()
         if self.scatter:
@@ -183,7 +188,7 @@
     pairs = groups // 2
     scatter = rows % (16 * splits) == 0
     out = jax.ShapeDtypeStruct((splits, rows // splits if scatter else rows, cols), dtype)
-    copies = pairs + (6 if pairs == 4 else pairs - 1) + (splits - 1) * (2 if scatter else 1)
+    copies = pairs + (pairs - 1) + (splits - 1) * (2 if scatter else 1)
     scratch = [
         pltpu.VMEM((pairs, rows, cols), dtype),
         pltpu.VMEM((pairs - 1, rows, cols), dtype),
@@ -367,14 +372,14 @@
         tokens_ref, cotangent_ref, deal_ref, lengths_ref, buckets_ref, *vector_refs, rel_ref,
         wqkv_s, wout_s, wup_s, wdown_s,
     ) = refs[:14]
-    sum_down, sum_up, sum_out, sum_qkv, small_out, ret_out, ret_grad = refs[14:21]
-    it = iter(refs[21:])
-    sources = [next(it) for _ in range(4)]
+    *sums, small_out, ret_out, ret_grad = refs[14:23]
+    it = iter(refs[23:])
+    sources = [next(it) for _ in range(6)]
     summers = [
-        Summer(source, *[next(it) for _ in range(4)], out, next(it))
-        for source, out in zip(sources, (sum_down, sum_up, sum_out, sum_qkv))
+        Summer(source, *[next(it) for _ in range(4)], out, next(it), halving)
+        for source, out, halving in zip(sources, sums, (True, True, True, False, False, False))
     ]
-    down, up, out_sum, qkv_sum = summers
+    down, up, out_sum, *qkv_sums = summers
     small_ref, small_land, small_sems = next(it), next(it), next(it)
     slots, ret_sems, halo_send, halo_land, halo_sems = (next(it) for _ in range(5))
     dres_ref, do_ref, qaug, doaug, q_t, do_t = (next(it) for _ in range(6))
@@ -511,6 +516,7 @@
     own_normed = first_norm(back)
     gathers[0].relay()
     gathers[2].start()
+    gathers[3].start()
     gathers[0].relay_far()
     gathers[0].arrive()
     q_ref[...] = (dot_nn(own_normed, wqkv_ref[:, :width])).astype(BF16) * jnp.asarray(HD**-0.5, BF16)
@@ -580,19 +586,20 @@
         row_wait(step)
         row_send(step + 1)
         if step == 1:
+            gathers[1].relay()
+            gathers[2].relay()
             dealt_grad = deal_out(1, cotangent_ref, g_ref, 0)
-            gathers[3].start()
         keys_of(back - step)
         if step % 2:
             high = (back - step + 2) * per_chunk
             look((back - step) * per_chunk, high, step > 1, False)
-    for gather in gathers[1:]:
-        gather.relay()
+    gathers[3].relay()
+    gathers[1].relay_far()
+    gathers[2].relay_far()
     row_wait(back)
     keys_of(0)
     look(0, per_chunk, True, True)
-    for gather in gathers[1:]:
-        gather.relay_far()
+    gathers[3].relay_far()
     for gather in gathers[1:]:
         gather.arrive()
     for copy in dealt_grad:
@@ -698,8 +705,7 @@
 
     rounds = len(spans) * (H // 2)
     plan = {}
-    for part, action in (
-    ):
+    for part, action in ((8, lambda: send_back(0)),):
         plan.setdefault(part * rounds // 12, []).append(action)
 
     def attend(index, chunk, first, count, jobs):
@@ -787,13 +793,11 @@
         if step == 0:
             dq_low = (dq_acc[...] * (HD**-0.5)).astype(BF16)
             grad_normed = part + dot_nt(dq_low, wqkv_ref[:, :width])
-            grad_q = dot_nn(rows_t, dq_low).astype(BF16)
-            for o in range(groups):
-                take = slice(o * rows_up, (o + 1) * rows_up)
-                sources[3][o, :rows_up] = grad_q[take]
-                sources[3][o, rows_up : 2 * rows_up] = gkv[take, :width].astype(BF16)
-                sources[3][o, 2 * rows_up :] = gkv[take, width:].astype(BF16)
-            qkv_sum.stage1()
+            grads = (dot_nn(rows_t, dq_low).astype(BF16), gkv[:, :width].astype(BF16), gkv[:, width:].astype(BF16))
+            for i, grad in enumerate(grads):
+                for o in range(groups):
+                    sources[3 + i][o] = grad[o * rows_up : (o + 1) * rows_up]
+                qkv_sums[i].stage1()
         else:
             if step < back:
 
@@ -815,12 +819,15 @@
             def _(step=step):
                 halo_copy(step).start()
 
-    down.stage3()
+            if index == back - 1:
+                down.stage3()
     up.stage3()
     out_sum.stage3()
-    qkv_sum.stage2()
-    send_back(0)
-    down.stage4()
+    for summer in qkv_sums:
+        summer.stage2()
+    wide = (down, up, out_sum)
+    for summer in wide:
+        summer.turn(1)
 
     @pl.when(seq + 1 < splits)
     def _():
@@ -842,15 +849,22 @@
     for o in range(groups):
         slots[1, o] = dx[o * length : (o + 1) * length]
     send_back(1)
-    qkv_sum.stage2b()
     small.take()
     small.plane()
-    up.stage4()
-    out_sum.stage4()
-    qkv_sum.stage3()
+    for turn in range(2, down.rounds + 1):
+        for summer in wide:
+            summer.turn(turn)
+    for summer in qkv_sums:
+        summer.stage3()
     small.take()
     small.along()
-    qkv_sum.stage4()
+    for turn in reversed(range(1, down.rounds)):
+        for summer in wide:
+            summer.turn_back(turn)
+    for summer in summers:
+        summer.stage4()
+    for summer in wide:
+        summer.turn_back(0)
     small.take()
     small_out[...] = small_ref[3]
     for summer in summers:
@@ -884,7 +898,7 @@
     window, reach = (back + 1) * tokens, back * tokens + 2 * QB
     wide = min(2, back) * per_chunk
     span = min(wide + per_chunk - 1, reach // QB - 1) * QB
-    grads = [wdown.shape[0], wup.shape[0] * wup.shape[1] // width, width // groups, 3 * width // groups]
+    grads = [wdown.shape[0], wup.shape[0] * wup.shape[1] // width, *[width // groups] * 4]
     out_shapes, more, sources = [], [], []
     for height in grads:
         shape = (groups, height, width)
@@ -957,23 +971,27 @@
     )(tokens_in, cotangent, deal, lengths, buckets.reshape(-1, PAIR), *vectors, rel, wqkv, wout, wup, wdown)
 
 
-def finish_kernel(deal_ref, down, up, out, qkv, small, ret_out, ret_grad, *outs):
+def finish_kernel(deal_ref, down, up, out, q, k, v, small, ret_out, ret_grad, *outs):
     o_out, o_grad, o_qkv, o_wout, o_up, o_down, *o_vectors, o_rel = outs
     length = ret_out.shape[1]
     for g in range(ret_out.shape[0]):
         piece = deal_ref[0, g]
         o_out[pl.ds(g * length, length), :] = ret_out[piece]
         o_grad[pl.ds(g * length, length), :] = ret_grad[piece]
-    for source, target in ((down, o_down), (up, o_up), (out, o_wout), (qkv, o_qkv)):
-        direct = source.shape[0] * source.shape[1] * source.shape[2] != target.shape[0] * target.shape[1]
-        cols = source.shape[2]
-        if direct:
-            value = add_low(*[source[t] for t in range(source.shape[0])])
-        else:
-            value = source[...].reshape(-1, cols).astype(F32)
-        height = target.shape[0]
-        for c in range(target.shape[1] // cols):
-            target[:, c * cols : (c + 1) * cols] = value[c * height : (c + 1) * height]
+    def collect(source, rows):
+        parts, height, cols = source.shape
+        if height == rows:
+            return add_low(*[source[t] for t in range(parts)])
+        return source[...].reshape(-1, cols).astype(F32)
+
+    width = down.shape[2]
+    for source, target in ((down, o_down), (up, o_up), (out, o_wout)):
+        height, columns = target.shape[0], target.shape[1] // width
+        value = collect(source, height * columns)
+        for c in range(columns):
+            target[:, c * width : (c + 1) * width] = value[c * height : (c + 1) * height]
+    for c, source in enumerate((q, k, v)):
+        o_qkv[:, c * width : (c + 1) * width] = collect(source, o_qkv.shape[0])
     dp, groups = lax.axis_index("dp"), lax.axis_size("dp")
     for i, target in enumerate(o_vectors):
         size = target.shape[0]
@@ -992,7 +1010,7 @@
 def finish(deal, sums, returned, shapes):
     return pl.pallas_call(
         finish_kernel,
-        in_specs=[pl.BlockSpec(memory_space=pltpu.SMEM)] + [pl.BlockSpec(memory_space=pltpu.VMEM)] * 7,
+        in_specs=[pl.BlockSpec(memory_space=pltpu.SMEM)] + [pl.BlockSpec(memory_space=pltpu.VMEM)] * 9,
         out_specs=[pl.BlockSpec(memory_space=pltpu.VMEM)] * len(shapes),
         out_shape=shapes,
         compiler_params=pltpu.CompilerParams(vmem_limit_bytes=VMEM_LIMIT),

time: 145 us -> 141 us (0.972)
  Pallas kernels: 144 us -> 140 us
    pallas_call x1, Pallas kernels: 141 us -> 136 us  [layer(): pl.pallas_call(functools.partial(layer_kernel, back, maxlen), in_specs=[v...]
where the time goes in v7:
time: 141 us; the launch traced here: 140 us
  Pallas kernels  140 us (99%)
    pallas_call x1, Pallas kernels, layer(): pl.pallas_call(functools.partial(layer_kernel, back, maxlen), in_specs=[v...  136 us
    pallas_call x1, Pallas kernels, finish(): pl.pallas_call(finish_kernel, in_specs=[pl.BlockSpec(memory_space=pltpu.S...  3.51 us

profile of v7, /device:TPU:0, one launch (start us, length us, event | category | flops | bytes accessed | tf_op | source)
XLA Modules:
  0.0 140.5 jit_solution(2360846168231918505)
XLA Ops:
  0.6 136.1 %layer.1 = (bf16[4,64,512]{2,1,0:T(8,128)(2,1)}, bf16[4,64,512]{2,1,0:T(8,128)(2,1)}, bf16[4,16,512]{2,1,0:T(8,128)(2,1)}, bf16[4,16,512]{2,1,0:T(8,128)(2,1)}, ...) custom-call(bf16[512,512]{1,0:T(8,128)(2,1)} %refs_0_.1, ...), custom_call_target="tpu_custom_call" | custom-call | tf_op jit(solution)/shard_map/layer/pallas_call | solution.py:963
  136.8 3.5 %finish.1 = (bf16[512,512]{1,0:T(8,128)(2,1)}, bf16[512,512]{1,0:T(8,128)(2,1)}, f32[64,1536]{1,0:T(8,128)}, f32[64,512]{1,0:T(8,128)}, f32[64,2048]{1,0:T(8,128...) custom-call(s32[1,8]{1,0:T(1,128)} %deal_ref.1, ...), custom_call_target="tpu_custom_call" | custom-call | tf_op jit(solution)/shard_map/finish/pallas_call | solution.py:1011

commit v8 on v7

--- a/solution.py
+++ b/solution.py
@@ -239,12 +239,9 @@
             total = total + self.land[slot]
         self.ref[stage + 1] = total
 
-    def pair(self):
-        self.send([{"dp": self.dp + 1 - 2 * lax.rem(self.dp, 2)}])
-
     def plane(self):
-        core, chip = lax.rem(self.dp, 2), self.dp // 2
-        self.send([{"dp": 2 * lax.rem(chip + step, self.pairs) + core} for step in range(1, self.pairs)])
+        groups = 2 * self.pairs
+        self.send([{"dp": lax.rem(self.dp + step, groups)} for step in range(1, groups)])
 
     def along(self):
         self.send([{"seq": lax.rem(self.seq + step, self.splits)} for step in range(1, self.splits)])
@@ -269,7 +266,7 @@
 
 
 def flip(values):
-    return values.astype(F32).T.astype(BF16)
+    return values.astype(BF16).T
 
 
 def phase_spans(back, per_chunk, tiles):
@@ -764,8 +761,8 @@
                     left = left[:half] + pltpu.roll(left[half:], span + QB - half, 1)
                     half //= 2
                 dd[pair, h : h + 1, first * QB : (first + count + 1) * QB] += left
-            dkv[:, cols] = dkt[...].T.astype(BF16)
-            dkv[:, pl.ds(pl.multiple_of(width + pair * PAIR, PAIR), PAIR)] = dvt[...].T.astype(BF16)
+            dkv[:, cols] = dkt[...].astype(BF16).T
+            dkv[:, pl.ds(pl.multiple_of(width + pair * PAIR, PAIR), PAIR)] = dvt[...].astype(BF16).T
             return _
 
         lax.fori_loop(0, H // 2, body, 0)
@@ -844,13 +841,11 @@
     small_ref[0, 8:16, :] = jnp.zeros((8, width), F32)
     small_ref[0, 8:16, :NBK] = dot_nt(dd_hi, hot_ref[...]) + dot_nt(dd_mid, hot_ref[...])
     small = SmallSummer(small_ref, small_land, small_sems)
-    small.pair()
+    small.plane()
     dx = (dres_ref[...] + norm_back(grad_normed * gains_ref[0:1, :], normal, scale)).astype(BF16)
     for o in range(groups):
         slots[1, o] = dx[o * length : (o + 1) * length]
     send_back(1)
-    small.take()
-    small.plane()
     for turn in range(2, down.rounds + 1):
         for summer in wide:
             summer.turn(turn)
@@ -866,7 +861,7 @@
     for summer in wide:
         summer.turn_back(0)
     small.take()
-    small_out[...] = small_ref[3]
+    small_out[...] = small_ref[2]
     for summer in summers:
         summer.finish()
     small.finish()
@@ -908,7 +903,7 @@
         more += scratch
     out_shapes.append(jax.ShapeDtypeStruct((16, width), F32))
     out_shapes += [jax.ShapeDtypeStruct((groups, length, width), BF16)] * 2
-    small_copies = 1 + (groups // 2 - 1) + (splits - 1)
+    small_copies = (groups - 1) + (splits - 1)
     scratch = sources + more + [
         pltpu.VMEM((4, 16, width), F32),
         pltpu.VMEM((small_copies, 16, width), F32),

time: 141 us -> 139 us (0.986)
  Pallas kernels: 140 us -> 138 us
    pallas_call x1, Pallas kernels: 136 us -> 134 us  [layer(): pl.pallas_call(functools.partial(layer_kernel, back, maxlen), in_specs=[v...]
where the time goes in v8:
time: 139 us
  Pallas kernels  138 us (99%)
    pallas_call x1, Pallas kernels, layer(): pl.pallas_call(functools.partial(layer_kernel, back, maxlen), in_specs=[v...  134 us
    pallas_call x1, Pallas kernels, finish(): pl.pallas_call(finish_kernel, in_specs=[pl.BlockSpec(memory_space=pltpu.S...  3.51 us

profile of v8, /device:TPU:0, one launch (start us, length us, event | category | flops | bytes accessed | tf_op | source)
XLA Modules:
  0.0 138.7 jit_solution(2711130897850363573)
XLA Ops:
  0.6 134.3 %layer.1 = (bf16[4,64,512]{2,1,0:T(8,128)(2,1)}, bf16[4,64,512]{2,1,0:T(8,128)(2,1)}, bf16[4,16,512]{2,1,0:T(8,128)(2,1)}, bf16[4,16,512]{2,1,0:T(8,128)(2,1)}, ...) custom-call(bf16[512,512]{1,0:T(8,128)(2,1)} %refs_0_.1, ...), custom_call_target="tpu_custom_call" | custom-call | tf_op jit(solution)/shard_map/layer/pallas_call | solution.py:958
  135.0 3.5 %finish.1 = (bf16[512,512]{1,0:T(8,128)(2,1)}, bf16[512,512]{1,0:T(8,128)(2,1)}, f32[64,1536]{1,0:T(8,128)}, f32[64,512]{1,0:T(8,128)}, f32[64,2048]{1,0:T(8,128...) custom-call(s32[1,8]{1,0:T(1,128)} %deal_ref.1, ...), custom_call_target="tpu_custom_call" | custom-call | tf_op jit(solution)/shard_map/finish/pallas_call | solution.py:1006

commit v9 on v8

--- a/solution.py
+++ b/solution.py
@@ -378,12 +378,12 @@
     ]
     down, up, out_sum, *qkv_sums = summers
     small_ref, small_land, small_sems = next(it), next(it), next(it)
-    slots, ret_sems, halo_send, halo_land, halo_sems = (next(it) for _ in range(5))
+    slots, ret_sems, ret_own_sems, halo_send, halo_land, halo_sems = (next(it) for _ in range(6))
     dres_ref, do_ref, qaug, doaug, q_t, do_t = (next(it) for _ in range(6))
     bias, scores, kaug, vaug, dd, dq_acc, dkt, dvt, dkv, gkv = (next(it) for _ in range(10))
     dsum = scores.at[0]
     xwin, g_ref, wqkv_ref, wout_ref, wup_ref, wdown_ref = (next(it) for _ in range(6))
-    gather_sems, own_sems, deal_sems, row_sems, few_land, few_sems = (next(it) for _ in range(6))
+    gather_sems, own_sems, deal_sems, row_sems, piece_sems, few_land, few_sems = (next(it) for _ in range(7))
     gains_ref, base_ref, q_ref, k_ref, v_ref, att_ref, lse_ref = (next(it) for _ in range(7))
     few_mine, rel_all, hot_ref, qx_ref, kx_ref = (next(it) for _ in range(5))
     dp, groups = lax.axis_index("dp"), lax.axis_size("dp")
@@ -418,6 +418,13 @@
 
     own_first = back * tokens
     own_rows = pl.ds(own_first, tokens)
+    gathers = [
+        Gather(shard, full, gather_sems.at[i], own_sems.at[i])
+        for i, (shard, full) in enumerate(
+            ((wqkv_s, wqkv_ref), (wout_s, wout_ref), (wup_s, wup_ref), (wdown_s, wdown_ref))
+        )
+    ]
+    gathers[0].start()
     dealt = deal_out(0, tokens_ref, xwin, own_first)
     shard_rows, rel_rows = vector_refs[0].shape[0], rel_ref.shape[0]
     few_mine[...] = jnp.zeros_like(few_mine)
@@ -434,13 +441,6 @@
         copy.start()
         few.append(copy)
     few_land[dp] = few_mine[...]
-    gathers = [
-        Gather(shard, full, gather_sems.at[i], own_sems.at[i])
-        for i, (shard, full) in enumerate(
-            ((wqkv_s, wqkv_ref), (wout_s, wout_ref), (wup_s, wup_ref), (wdown_s, wdown_ref))
-        )
-    ]
-    gathers[0].start()
     gathers[1].start()
 
     seqs = lengths_ref.shape[1]
@@ -470,8 +470,6 @@
     up_to = jnp.sum(up_to, axis=1, keepdims=True)
     far = (back * tokens + QB - lax.broadcasted_iota(jnp.int32, hot_ref.shape, 1)).astype(F32)
     hot_ref[...] = jnp.where((far >= below) & (far < up_to), 1.0, 0.0).astype(BF16)
-    for copy in dealt:
-        copy.wait_recv()
 
     def row_copy(step):
         return pltpu.make_async_remote_copy(
@@ -481,6 +479,15 @@
             device_id={"seq": lax.rem(seq + 1, splits)}, device_id_type=mesh_ids,
         )
 
+    def piece_copy(step):
+        first = lax.rem(dp + groups - step, groups) * length
+        return pltpu.make_async_remote_copy(
+            src_ref=xwin.at[pl.ds(pl.multiple_of(own_first + first, length), length)],
+            dst_ref=xwin.at[pl.ds(pl.multiple_of(own_first - tokens + first, length), length)],
+            send_sem=piece_sems.at[0, step], recv_sem=piece_sems.at[1, step],
+            device_id={"seq": lax.rem(seq + 1, splits)}, device_id_type=mesh_ids,
+        )
+
     def row_send(step):
         @pl.when((seq + 1 < splits) & (seq + 1 >= step))
         def _():
@@ -489,9 +496,16 @@
     def row_wait(step):
         @pl.when(seq >= step)
         def _():
-            row_copy(step).wait_recv()
-
-    row_send(1)
+            if step > 1:
+                row_copy(step).wait_recv()
+                return
+            for piece in range(groups):
+                piece_copy(piece).wait_recv()
+
+    for step in range(groups):
+        if step > 0:
+            dealt[step - 1].wait_recv()
+        pl.when(seq + 1 < splits)(piece_copy(step).start)
     for copy in few:
         copy.wait_recv()
     per_tile = PAIR // shard_rows
@@ -514,6 +528,9 @@
     gathers[0].relay()
     gathers[2].start()
     gathers[3].start()
+    row_wait(1)
+    if back > 1:
+        row_send(2)
     gathers[0].relay_far()
     gathers[0].arrive()
     q_ref[...] = (dot_nn(own_normed, wqkv_ref[:, :width])).astype(BF16) * jnp.asarray(HD**-0.5, BF16)
@@ -580,9 +597,10 @@
         v_ref[here, :] = dot_nn(normed, wqkv_ref[:, 2 * width :]).astype(BF16)
 
     for step in range(1, back):
-        row_wait(step)
-        row_send(step + 1)
-        if step == 1:
+        if step > 1:
+            row_wait(step)
+            row_send(step + 1)
+        else:
             gathers[1].relay()
             gathers[2].relay()
             dealt_grad = deal_out(1, cotangent_ref, g_ref, 0)
@@ -593,7 +611,8 @@
     gathers[3].relay()
     gathers[1].relay_far()
     gathers[2].relay_far()
-    row_wait(back)
+    if back > 1:
+        row_wait(back)
     keys_of(0)
     look(0, per_chunk, True, True)
     gathers[3].relay_far()
@@ -612,10 +631,13 @@
             device_id={"dp": peer}, device_id_type=mesh_ids,
         )
 
+    def ret_own(which):
+        return pltpu.make_async_copy(slots.at[which, dp], (ret_out, ret_grad)[which].at[dp], ret_own_sems.at[which])
+
     def send_back(which):
         for step in range(1, groups):
             ret_copy(which, step).start()
-        (ret_out, ret_grad)[which][dp] = slots[which, dp]
+        ret_own(which).start()
 
     resid = xwin[own_rows, :].astype(F32) + dot_nn(att_ref[...], wout_ref[...])
     normal, scale = norm_stats(resid)
@@ -866,13 +888,16 @@
         summer.finish()
     small.finish()
     for which in range(2):
+        ret_own(which).wait()
         for step in range(1, groups):
             ret_copy(which, step).wait()
     for gather in gathers:
         gather.finish()
     for copy in few:
         copy.wait_send()
-    for step in range(1, back + 1):
+    for step in range(groups):
+        pl.when(seq + 1 < splits)(piece_copy(step).wait_send)
+    for step in range(2, back + 1):
 
         @pl.when((seq + 1 < splits) & (seq + 1 >= step))
         def _(step=step):
@@ -910,6 +935,7 @@
         pltpu.SemaphoreType.DMA((2, small_copies)),
         pltpu.VMEM((2, groups, length, width), BF16),
         pltpu.SemaphoreType.DMA((2, 2, groups - 1)),
+        pltpu.SemaphoreType.DMA((2,)),
         pltpu.VMEM((min(back, 2), tokens, width), BF16),
         pltpu.VMEM((back, tokens, width), BF16),
         pltpu.SemaphoreType.DMA((2, back)),
@@ -939,6 +965,7 @@
         pltpu.SemaphoreType.DMA((4,)),
         pltpu.SemaphoreType.DMA((2, 2, groups - 1)),
         pltpu.SemaphoreType.DMA((2, back)),
+        pltpu.SemaphoreType.DMA((2, groups)),
         pltpu.VMEM((groups, 16, PAIR), F32),
         pltpu.SemaphoreType.DMA((2, groups - 1)),
         pltpu.VMEM((8, width), F32),
@@ -958,7 +985,7 @@
     return pl.pallas_call(
         functools.partial(layer_kernel, back, maxlen),
         in_specs=[vmem] * 2 + [smem] * 2 + [vmem] * (2 + len(vectors)) + [pl.BlockSpec(memory_space=pl.ANY)] * 4,
-        out_specs=[vmem] * len(out_shapes),
+        out_specs=[vmem] * (len(out_shapes) - 2) + [pl.BlockSpec(memory_space=pl.ANY)] * 2,
         out_shape=out_shapes,
         scratch_shapes=scratch,
         compiler_params=pltpu.CompilerParams(collective_id=1, has_side_effects=True, vmem_limit_bytes=VMEM_LIMIT),

time: 139 us -> 138 us (level)
  no operation moved by 1% of the time
where the time goes in v9:
time: 138 us
  Pallas kernels  137 us (99%)
    pallas_call x1, Pallas kernels, layer(): pl.pallas_call(functools.partial(layer_kernel, back, maxlen), in_specs=[v...  133 us
    pallas_call x1, Pallas kernels, finish(): pl.pallas_call(finish_kernel, in_specs=[pl.BlockSpec(memory_space=pltpu.S...  3.51 us

profile of v9, /device:TPU:0, one launch (start us, length us, event | category | flops | bytes accessed | tf_op | source)
XLA Modules:
  0.0 137.5 jit_solution(2053519968573684946)
XLA Ops:
  0.6 133.2 %layer.1 = (bf16[4,64,512]{2,1,0:T(8,128)(2,1)}, bf16[4,64,512]{2,1,0:T(8,128)(2,1)}, bf16[4,16,512]{2,1,0:T(8,128)(2,1)}, bf16[4,16,512]{2,1,0:T(8,128)(2,1)}, ...) custom-call(bf16[512,512]{1,0:T(8,128)(2,1)} %refs_0_.1, ...), custom_call_target="tpu_custom_call" | custom-call | tf_op jit(solution)/shard_map/layer/pallas_call | solution.py:985
  133.8 3.5 %finish.1 = (bf16[512,512]{1,0:T(8,128)(2,1)}, bf16[512,512]{1,0:T(8,128)(2,1)}, f32[64,1536]{1,0:T(8,128)}, f32[64,512]{1,0:T(8,128)}, f32[64,2048]{1,0:T(8,128...) custom-call(s32[1,8]{1,0:T(1,128)} %deal_ref.1, ...), custom_call_target="tpu_custom_call" | custom-call | tf_op jit(solution)/shard_map/finish/pallas_call | solution.py:1033
